TPU v7x, 512 devices: a whole 4x4x16 slice. The times are simulated.
512 devices in a mesh: row: 16 (over z_hi, x, core), col: 32 (over z_lo, y).
Axes of the slice: x: 4, y: 4, z: 16 (z_hi: 2, z_lo: 8; z = z_hi * 8 + z_lo), core: 2. Of those that a mesh axis runs over, the one named last changes fastest.
Arguments:
- student: bfloat16 [65536, 768], P(('row', 'col')), may hold values from -0.21875 to 0.21875
- teacher: bfloat16 [65536, 768], P(('row', 'col')), may hold values from -32 to 32
Outputs:
- student_grad: float32 [65536, 768], P(('row', 'col'))
All inputs are finite; a program needn't handle non-finite values.
Results may differ from a plain program's by a relative error of at most 0.0045.
Values may be sent and summed in bfloat16 or wider, within the bound.
No kernel may reach another device: no remote copies, remote signals or barrier semaphores. Data moves between devices by JAX's collectives and lax.ppermute only.
A program may use at most 64 MiB of HBM per device.

v0:
```python
import jax
import jax.numpy as jnp
from jax import lax
from jax.sharding import PartitionSpec as P


def unit_rows(values):
    wide = values.astype(jnp.float32)
    length = jnp.sqrt(jnp.sum(wide * wide, axis=-1, keepdims=True) + 1e-06)
    return (wide / length, length)


def pair_products(left, right):
    return lax.dot_general(
        left, right, (((1,), (1,)), ((), ())), preferred_element_type=jnp.float32
    )


def on_device(student, teacher):
    unit_f, norm_s = unit_rows(student)
    unit_s = unit_f.astype(jnp.bfloat16)
    unit_t = unit_rows(teacher)[0].astype(jnp.bfloat16)
    batch_texts = student.shape[0] * lax.axis_size("col")
    total_texts = batch_texts * lax.axis_size("row")
    piece_s = lax.all_gather(unit_s, "col", axis=0, tiled=True)
    piece_t = lax.all_gather(unit_t, "col", axis=0, tiled=True)
    student_gram = pair_products(unit_s, piece_s)
    teacher_gram = pair_products(unit_t, piece_t)
    mismatch = student_gram - teacher_gram
    pull_sum = jnp.dot(mismatch, piece_s.astype(jnp.float32), precision=lax.Precision.HIGHEST)
    energy_sum = jnp.sum(teacher_gram * teacher_gram)
    energy = lax.psum(energy_sum, ("row", "col"))
    factor = batch_texts**0.5 * total_texts / energy
    pull = factor * pull_sum
    along = jnp.sum(pull * unit_f, axis=-1, keepdims=True)
    return (pull - along * unit_f) / norm_s


def solution(mesh):
    return jax.shard_map(
        on_device,
        mesh=mesh,
        in_specs=(P(("row", "col"), None), P(("row", "col"), None)),
        out_specs=P(("row", "col"), None),
        check_vma=False,
    )
```

profile of v0, /device:TPU:10, one launch (start us, length us, event | category | flops | bytes accessed | tf_op | source)
XLA Modules:
  0.0 498.2 jit_solution(11406697266622145857)
XLA Ops:
  6.5 0.0 all-gather.3.cloned.1.call-start
  6.5 1.0 fusion
  7.6 1.7 fusion.1
  9.3 0.0 all-gather.3.cloned.1.call-update
  9.3 0.0 all-gather.5.cloned.1.call-start
  9.4 1.0 fusion.2
  10.4 1.7 fusion.3
  12.2 0.0 copy-start.2
  12.2 0.0 all-gather.5.cloned.1.call-update
  12.2 235.0 %all-gather.3.cloned.1.call-done = bf16[4096,768]{1,0:T(8,128)(2,1)} async-done(((bf16[128,768]{1,0:T(8,128)(2,1)}), bf16[4096,768]{1,0:T(8,128)(2,1)}) %all-gather.3.cloned.1.call-update) | async-done | bytes 6291472 | tf_op jit(solution)/shard_map/all_gather | solution.py:26
  247.2 5.7 %multiply_reduce_fusion = (f32[]{:T(128)}, f32[128,4096]{1,0:T(8,128)S(1)}) fusion(bf16[128,768]{1,0:T(8,128)(2,1)} %fusion.1, bf16[4096,768]{1,0:T(8,128)(2,1)} %all-gather.3.cloned.1.call-done), kind=kOutput, calls=%fused_computation.1 | convolution fusion | flops 806354944 | bytes 8585220 | tf_op jit(solution)/shard_map/dot_general | solution.py:14
  252.9 0.0 copy-start.1
  252.9 103.0 %psum.7 = f32[]{:T(128)} all-reduce(f32[]{:T(128)} %get-tuple-element.5), channel_id=1, replica_groups=mesh['row'=16,'col'=32] {'row','col'}, use_global_device_ids=true, to_apply=%region_2.0 | all-reduce | flops 1 | bytes 8 | tf_op jit(solution)/shard_map/psum | solution.py:32
  356.6 125.3 %all-gather.5.cloned.1.call-done = bf16[4096,768]{1,0:T(8,128)(2,1)} async-done(((bf16[128,768]{1,0:T(8,128)(2,1)}), bf16[4096,768]{1,0:T(8,128)(2,1)}) %all-gather.5.cloned.1.call-update) | async-done | bytes 6291472 | tf_op jit(solution)/shard_map/all_gather | solution.py:25
  481.9 0.0 copy-start
  481.9 0.0 copy-done.2
  481.9 5.1 %convolution_subtract_fusion = f32[128,4096]{1,0:T(8,128)S(1)} fusion(f32[128,4096]{1,0:T(8,128)S(1)} %get-tuple-element.6, bf16[128,768]{1,0:T(8,128)(2,1)S(1)} %copy-done.2, bf16[4096,768]{1,0:T(8,128)(2,1)} %all-gather.5.cloned.1.call-done), kind=kOutput, calls=%fused_computation | convolution fusion | flops 805830656 | bytes 10682368 | tf_op jit(solution)/shard_map/dot_general | solution.py:14
  487.0 0.0 copy-done.1
  487.0 0.0 copy-done
  487.0 3.4 multiply_reduce_fusion.1
  490.4 0.9 subtract_divide_fusion
  (2 shorter events, 0.0 us)
Async XLA Ops:
  6.5 240.7 %all-gather.3.cloned.1.call-start = ((), (), s32[]{:S(2)}) async-start(), calls=%async_computation | async-start | bytes 6488064 | tf_op jit(solution)/shard_map/all_gather | solution.py:26
  9.3 472.5 %all-gather.5.cloned.1.call-start = ((), (), s32[]{:S(2)}) async-start(), calls=%async_computation.1 | async-start | bytes 6488064 | tf_op jit(solution)/shard_map/all_gather | solution.py:25
  12.2 469.7 %copy-start.2 = (bf16[128,768]{1,0:T(8,128)(2,1)S(1)}, bf16[128,768]{1,0:T(8,128)(2,1)}, u32[]{:S(2)}) copy-start(bf16[128,768]{1,0:T(8,128)(2,1)} %fusion.3) | copy-start | bytes 589828
  252.9 234.0 %copy-start.1 = (bf16[128,768]{1,0:T(8,128)(2,1)S(1)}, bf16[128,768]{1,0:T(8,128)(2,1)}, u32[]{:S(2)}) copy-start(bf16[128,768]{1,0:T(8,128)(2,1)} %param.2) | copy-start | bytes 589828
  481.9 5.1 %copy-start = (bf16[4096,768]{1,0:T(8,128)(2,1)S(1)}, bf16[4096,768]{1,0:T(8,128)(2,1)}, u32[]{:S(2)}) copy-start(bf16[4096,768]{1,0:T(8,128)(2,1)} %all-gather.5.cloned.1.call-done) | copy-start | bytes 18874372
Sparse Core Ops, SparseCore 0:
  9.5 237.7 all-gather.2
  249.3 232.5 all-gather.4
where the time goes:
time: 498 us
  waiting for transfers between devices  360 us (72%)
  blocking collectives  103 us (21%)
  matrix products  14.2 us (3%)
  between operations  14.1 us (3%)
  other arithmetic  6.46 us (1%)
    all_gather x1, waiting for transfers between devices, on_device(): piece_t = lax.all_gather(unit_t, 'col', axis=0, tiled=True)  235 us
    all_gather x1, waiting for transfers between devices, on_device(): piece_s = lax.all_gather(unit_s, 'col', axis=0, tiled=True)  125 us
    psum x1, blocking collectives, on_device(): energy = lax.psum(energy_sum, ('row', 'col'))  103 us
    dot_general x2, matrix products, pair_products(): lax.dot_general(left, right, (((1,), (1,)), ((), ())), preferred_element_...  10.8 us
  transfers between devices with their start and end apart: 2, of which 2 were waited for; matrix products, arithmetic and copies ran while one was open for 2% of the time, Pallas kernels for 0%

commit v1 on v0

v1 whole, which is shorter than its diff:
```python
import functools

import jax
import jax.numpy as jnp
from jax import lax
from jax.experimental import pallas as pl
from jax.experimental.pallas import tpu as pltpu
from jax.sharding import Mesh, PartitionSpec as P

NY = 4
NZ = 8
LANES = 128
TILE = 16
F32 = jnp.float32
BF16 = jnp.bfloat16
COL = ("zf", "z2", "z1", "y")
ALL = ("zh", "xc") + COL
VMEM_LIMIT = 12 * 1024 * 1024


def call(body, out_shape, operands, flops, scratch=(), after=()):
    size = sum(a.size * a.dtype.itemsize for a in operands)
    size += sum(s.size * s.dtype.itemsize for s in out_shape)
    count, extra = len(operands), len(after)

    def run(*refs):
        body(*refs[:count], *refs[count + extra :])

    whole = pl.BlockSpec(memory_space=pltpu.VMEM)
    return pl.pallas_call(
        run,
        out_shape=out_shape,
        in_specs=[whole] * count + [pl.BlockSpec(memory_space=pl.ANY)] * extra,
        out_specs=[whole] * len(out_shape),
        scratch_shapes=scratch,
        compiler_params=pltpu.CompilerParams(vmem_limit_bytes=VMEM_LIMIT),
        cost_estimate=pl.CostEstimate(flops=flops, bytes_accessed=size, transcendentals=0),
    )(*operands, *after)


def struct(shape, dtype):
    return jax.ShapeDtypeStruct(shape, dtype)


def unit_rows(values):
    wide = values.astype(F32)
    length = jnp.sqrt(jnp.sum(wide * wide, axis=-1, keepdims=True) + 1e-06)
    return (wide / length, length)


def split3(e):
    high = e.astype(BF16).astype(F32)
    mid = (e - high).astype(BF16).astype(F32)
    low = e - high - mid
    row = lax.broadcasted_iota(jnp.int32, (TILE, LANES), 0)
    parts = jnp.where(row == 0, high, jnp.where(row == 1, mid, jnp.where(row == 2, low, 0.0)))
    return parts.astype(BF16)


def join3(parts):
    return jnp.sum(parts.astype(F32), axis=0, keepdims=True)


def units_kernel(x_ref, copies_ref):
    unit = unit_rows(x_ref[...])[0].astype(BF16)
    for i in range(copies_ref.shape[0]):
        copies_ref[i] = unit


def nt(left, right):
    return lax.dot_general(left, right, (((1,), (1,)), ((), ())), preferred_element_type=F32)


def turned(ring_ref, flip):
    part = ring_ref.shape[1] // NY
    begin = lax.axis_index("y") * part // LANES * LANES
    rest = pl.multiple_of(lax.axis_index("y") * part - begin, TILE)
    flip[...] = ring_ref[:, pl.ds(pl.multiple_of(begin, LANES), 2 * LANES)].T
    return flip[pl.ds(rest, part)]


def split_rows(sums, axis, keep_ref, give_ref):
    rows = keep_ref.shape[0]
    here = lax.axis_index(axis)
    keep_ref[...] = sums[pl.ds(pl.multiple_of(here * rows, TILE), rows)]
    give_ref[...] = sums[pl.ds(pl.multiple_of((1 - here) * rows, TILE), rows)].astype(BF16)


def teacher_kernel(ring_ref, keep_ref, give_ref, flip, sums):
    sums[...] = jnp.dot(turned(ring_ref, flip), ring_ref[...], preferred_element_type=F32)
    split_rows(sums, "z1", keep_ref, give_ref)


def student_kernel(ring_s, ring_t, keep_ref, give_ref, flip, sums):
    width = ring_s.shape[1]
    part = sums.shape[0]
    left = turned(ring_s, flip)
    row = lax.broadcasted_iota(jnp.int32, (part, width), 0) + lax.axis_index("y") * part
    on = row == lax.broadcasted_iota(jnp.int32, (part, width), 1)
    sums[:, :width] = jnp.dot(left, ring_s[...], preferred_element_type=F32) - jnp.where(
        on, ring_s.shape[0] / width, 0.0
    )
    sums[:, width:] = -jnp.dot(left, ring_t[...], preferred_element_type=F32)
    split_rows(sums, "z1", keep_ref, give_ref)


def halve_kernel(mine_ref, got_ref, keep_ref, give_ref, sums):
    sums[...] = mine_ref[...] + got_ref[...].astype(F32)
    split_rows(sums, "z2", keep_ref, give_ref)


def energy_kernel(mine_ref, got_ref, e_ref):
    tt = mine_ref[...] + got_ref[...].astype(F32)
    e = jnp.sum(tt * tt, axis=0, keepdims=True)
    e = sum(e[:, i : i + LANES] for i in range(0, e.shape[1], LANES))
    e_ref[...] = jnp.broadcast_to(e, e_ref.shape)


def energies_kernel(e_ref, out_ref):
    out_ref[...] = jnp.sum(e_ref[...], axis=0)


def add_kernel(mine_ref, got_ref, total_ref, send_ref):
    total = mine_ref[...] + got_ref[...].astype(F32)
    total_ref[...] = total
    send_ref[...] = total.astype(BF16)


def exchange_kernel(mine_ref, got_ref, e_ref, f_ref, out_ref):
    main = mine_ref.shape[1]
    out_ref[:, :main] = (mine_ref[...] + got_ref[...].astype(F32)).astype(BF16)
    out_ref[:, main:] = jnp.zeros((out_ref.shape[0], LANES), BF16)
    out_ref[0:TILE, main:] = split3(e_ref[0:1] + f_ref[0:1])


def double_kernel(mine_ref, got_ref, out_ref):
    z2 = lax.axis_index("z2")
    rows, wide = mine_ref.shape
    main = wide - LANES
    out_ref[pl.ds(pl.multiple_of(z2 * rows, TILE), rows)] = mine_ref[...]
    out_ref[pl.ds(pl.multiple_of((1 - z2) * rows, TILE), rows)] = got_ref[...]
    e = join3(mine_ref[0:TILE, main:]) + join3(got_ref[0:TILE, main:])
    out_ref[0:TILE, main:] = split3(e)


def pull_kernel(mine_ref, got_ref, ring_s, ring_t, out_ref, whole):
    z1 = lax.axis_index("z1")
    rows, wide = mine_ref.shape
    main = wide - LANES
    whole[pl.ds(pl.multiple_of(z1 * rows, TILE), rows)] = mine_ref[:, :main]
    whole[pl.ds(pl.multiple_of((1 - z1) * rows, TILE), rows)] = got_ref[:, :main]
    width, part = main // 2, 2 * rows
    pull = nt(whole[:, :width], ring_s[...]) + nt(whole[:, width:], ring_t[...])
    e = join3(mine_ref[0:TILE, main:]) + join3(got_ref[0:TILE, main:])
    parts = split3(e)
    n = out_ref.shape[2]
    for i in range(NY):
        out_ref[i, 0:part] = pull[:, i * n : (i + 1) * n].astype(BF16)
        out_ref[i, part:] = parts


def finish_kernel(scale, diag, blocks_ref, student_ref, out_ref):
    n, width = student_ref.shape
    part = width // NY
    parts = sum(join3(blocks_ref[i, part:]) for i in range(NY))
    energy = jnp.sum(parts, axis=1, keepdims=True)
    factor = scale / energy
    unit_f, norm_s = unit_rows(student_ref[...])
    pull_t = jnp.concatenate([blocks_ref[i, 0:part].astype(F32) for i in range(NY)], axis=0)
    pull = (pull_t.T + diag * unit_f.astype(BF16).astype(F32)) * factor
    along = jnp.sum(pull * unit_f, axis=-1, keepdims=True)
    out_ref[...] = (pull - along * unit_f) / norm_s


def swap(x, axis):
    return lax.ppermute(x, axis, [(0, 1), (1, 0)])


def gather_y(x):
    n, width = x.shape
    (copies,) = call(units_kernel, [struct((NY, n, width), BF16)], [x], 5 * n * width)
    return lax.all_to_all(copies, "y", 0, 0).reshape(NY * n, width)


def on_device(student, teacher):
    n, width = student.shape
    batch_texts = n * lax.axis_size(COL)
    total_texts = n * lax.axis_size(ALL)
    part = width // NY
    half, rows = part // 2, part // 4
    texts = n * NY
    mac = texts * part * width

    def pair(rows, wide):
        return [struct((rows, wide), F32), struct((rows, wide), BF16)]

    def scratch(wide):
        return [pltpu.VMEM((2 * LANES, texts), BF16), pltpu.VMEM((part, wide), F32)]

    ring_t = gather_y(teacher)
    ring_s = gather_y(student)

    tt, tt_give = call(teacher_kernel, pair(half, width), [ring_t], 2 * mac, scratch(width))
    tt_got = swap(tt_give, "z1")
    tt, tt_give = call(
        halve_kernel, pair(rows, width), [tt, tt_got], part * width, [pltpu.VMEM((half, width), F32)]
    )
    tt_got = swap(tt_give, "z2")
    keep, give = call(
        student_kernel,
        pair(half, 2 * width),
        [ring_s, ring_t],
        4 * mac,
        scratch(2 * width),
        after=[tt_give],
    )
    got = swap(give, "z1")
    tt, tt_give = call(add_kernel, pair(rows, width), [tt, tt_got], rows * width)
    tt_got = swap(tt_give, "zf")
    keep, give = call(
        halve_kernel,
        pair(rows, 2 * width),
        [keep, got],
        2 * part * width,
        [pltpu.VMEM((half, 2 * width), F32)],
        after=[tt_give],
    )
    got = swap(give, "z2")
    near = lax.axis_size("xc")
    (e,) = call(
        energy_kernel,
        [struct((near, 8, LANES), F32)],
        [tt, tt_got],
        3 * rows * width,
        after=[give],
    )
    e = lax.all_to_all(e, "xc", 0, 0)
    keep, give = call(
        add_kernel, pair(rows, 2 * width), [keep, got], 2 * rows * width, after=[e]
    )
    got = swap(give, "zf")
    (e,) = call(energies_kernel, [struct((8, LANES), F32)], [e], e.size, after=[give])
    e_far = swap(e, "zh")
    (mine,) = call(
        exchange_kernel,
        [struct((rows, 2 * width + LANES), BF16)],
        [keep, got, e, e_far],
        2 * rows * width,
    )
    got = swap(mine, "z2")
    (mine,) = call(
        double_kernel, [struct((half, 2 * width + LANES), BF16)], [mine, got], 2 * rows * width
    )
    got = swap(mine, "z1")
    (blocks,) = call(
        pull_kernel,
        [struct((NY, part + TILE, n), BF16)],
        [mine, got, ring_s, ring_t],
        4 * mac,
        [pltpu.VMEM((part, 2 * width), BF16)],
    )
    blocks = lax.all_to_all(blocks, "y", 0, 0)
    (out,) = call(
        functools.partial(finish_kernel, batch_texts**0.5 * total_texts, batch_texts / width),
        [struct((n, width), F32)],
        [blocks, student],
        12 * n * width,
    )
    return out


def solution(mesh):
    rows, cols = mesh.devices.shape
    fine = Mesh(mesh.devices.reshape(2, rows // 2, 2, 2, 2, cols // NZ), ALL)
    return jax.shard_map(
        on_device,
        mesh=fine,
        in_specs=(P(ALL, None), P(ALL, None)),
        out_specs=P(ALL, None),
        check_vma=False,
    )
```

time: 498 us -> 127 us (0.26)
  the two profiles are of different devices: /device:TPU:10 before, /device:TPU:2 now
where the time goes in v1:
time: 127 us; the launch traced here: 126 us
  starting transfers between devices  58.4 us (46%)
  waiting for transfers between devices  44.2 us (35%)
  blocking collectives  17.4 us (14%)
  Pallas kernels  5.36 us (4%)
    ppermute x9, starting transfers between devices, swap(): return lax.ppermute(x, axis, [(0, 1), (1, 0)])  50.3 us
    ppermute x9, waiting for transfers between devices, swap(): return lax.ppermute(x, axis, [(0, 1), (1, 0)])  29.2 us
    all_to_all x2, waiting for transfers between devices, gather_y(): return lax.all_to_all(copies, 'y', 0, 0).reshape(NY * n, width)  15 us
    all_to_all x1, blocking collectives, on_device(): blocks = lax.all_to_all(blocks, 'y', 0, 0)  8.79 us
    all_to_all x1, blocking collectives, on_device(): e = lax.all_to_all(e, 'xc', 0, 0)  8.61 us
    all_to_all x2, starting transfers between devices, gather_y(): return lax.all_to_all(copies, 'y', 0, 0).reshape(NY * n, width)  8.09 us
    pallas_call x14, Pallas kernels, call(): pl.pallas_call(run, out_shape=out_shape, in_specs=[whole] * count + [pl.B...  5.36 us
  transfers between devices with their start and end apart: 11, of which 9 were waited for; matrix products, arithmetic and copies ran while one was open for 0% of the time, Pallas kernels for 1%

profile of v1, /device:TPU:2, one launch (start us, length us, event | category | flops | bytes accessed | tf_op | source)
XLA Modules:
  0.0 126.5 jit_solution(6980793484288906197)
XLA Ops:
  0.0 0.0 copy-start.1
  0.0 0.9 copy-done.1
  0.9 1.1 shard_map.29
  2.0 0.0 copy-start
  2.0 4.6 %all-to-all-start.1 = ((bf16[4,128,768]{2,1,0:T(8,128)(2,1)}), bf16[4,128,768]{2,1,0:T(8,128)(2,1)S(1)}, u32[]{:S(2)}, u32[]{:S(2)}) async-start(bf16[4,128,768]{2,1,0:T(8,128)(2,1)} %shard_map.29), calls=%async_computation.1 | async-start | bytes 1572864 | tf_op jit(solution)/shard_map/all_to_all | solution.py:182
  6.6 0.0 copy-done
  6.6 1.0 shard_map.28
  7.6 11.2 %all-to-all-done.1 = bf16[4,128,768]{2,1,0:T(8,128)(2,1)S(1)} async-done(((bf16[4,128,768]{2,1,0:T(8,128)(2,1)}), bf16[4,128,768]{2,1,0:T(8,128)(2,1)S(1)}, u32[]{:S(2)}, u32[]{:S(2)}) %all-to-all-start.1) | async-done | bytes 786464 | tf_op jit(solution)/shard_map/all_to_all | solution.py:182
  18.9 3.5 %all-to-all-start = ((bf16[4,128,768]{2,1,0:T(8,128)(2,1)}), bf16[4,128,768]{2,1,0:T(8,128)(2,1)S(1)}, u32[]{:S(2)}, u32[]{:S(2)}) async-start(bf16[4,128,768]{2,1,0:T(8,128)(2,1)} %shard_map.28), calls=%async_computation | async-start | bytes 1572864 | tf_op jit(solution)/shard_map/all_to_all | solution.py:182
  22.4 0.5 shard_map.30
  22.9 3.8 %collective-permute-start = (bf16[96,768]{1,0:T(8,128)(2,1)S(1)}, bf16[96,768]{1,0:T(8,128)(2,1)S(1)}, u32[]{:S(2)}, u32[]{:S(2)}) collective-permute-start(bf16[96,768]{1,0:T(8,128)(2,1)S(1)} %get-tuple-element.18), channel_id=1, source_target_pairs={{0,4},{4,0},{1,5},{5,1},{2,6},{6,2},{3,7},{7,3},{8,12},{12,8},{9,1... | collective-permute-start | bytes 442376 | tf_op jit(solution)/shard_map/ppermute | solution.py:176
  26.7 3.2 %collective-permute-done.refs_1_ = bf16[96,768]{1,0:T(8,128)(2,1)S(1)} collective-permute-done((bf16[96,768]{1,0:T(8,128)(2,1)S(1)}, bf16[96,768]{1,0:T(8,128)(2,1)S(1)}, u32[]{:S(2)}, u32[]{:S(2)}) %collective-permute-start) | collective-permute-done | bytes 147488 | tf_op jit(solution)/shard_map/ppermute | solution.py:176
  29.9 0.1 shard_map.31
  29.9 3.8 %all-to-all-done = bf16[4,128,768]{2,1,0:T(8,128)(2,1)S(1)} async-done(((bf16[4,128,768]{2,1,0:T(8,128)(2,1)}), bf16[4,128,768]{2,1,0:T(8,128)(2,1)S(1)}, u32[]{:S(2)}, u32[]{:S(2)}) %all-to-all-start) | async-done | bytes 786464 | tf_op jit(solution)/shard_map/all_to_all | solution.py:182
  33.7 0.7 shard_map.32
  34.4 3.8 %collective-permute-start.1 = (bf16[96,1536]{1,0:T(8,128)(2,1)S(1)}, bf16[96,1536]{1,0:T(8,128)(2,1)S(1)}, u32[]{:S(2)}, u32[]{:S(2)}) collective-permute-start(bf16[96,1536]{1,0:T(8,128)(2,1)S(1)} %get-tuple-element.21), channel_id=1, source_target_pairs={{0,4},{4,0},{1,5},{5,1},{2,6},{6,2},{3,7},{7,3},{8,12},{12,8},{9,1... | collective-permute-start | bytes 884744 | tf_op jit(solution)/shard_map/ppermute | solution.py:176
  38.3 5.2 %collective-permute-start.2 = (bf16[48,768]{1,0:T(8,128)(2,1)S(1)}, bf16[48,768]{1,0:T(8,128)(2,1)S(1)}, u32[]{:S(2)}, u32[]{:S(2)}) collective-permute-start(bf16[48,768]{1,0:T(8,128)(2,1)S(1)} %get-tuple-element.19.refs_2_), channel_id=1, source_target_pairs={{0,8},{8,0},{1,9},{9,1},{2,10},{10,2},{3,11},{11,3},{4,12},{12,4},... | collective-permute-start | bytes 221192 | tf_op jit(solution)/shard_map/ppermute | solution.py:176
  43.4 2.3 %collective-permute-done.2.refs_1_ = bf16[48,768]{1,0:T(8,128)(2,1)S(1)} collective-permute-done((bf16[48,768]{1,0:T(8,128)(2,1)S(1)}, bf16[48,768]{1,0:T(8,128)(2,1)S(1)}, u32[]{:S(2)}, u32[]{:S(2)}) %collective-permute-start.2) | collective-permute-done | bytes 73760 | tf_op jit(solution)/shard_map/ppermute | solution.py:176
  45.8 0.0 collective-permute-done.1.refs_1_
  45.8 0.1 shard_map.34
  45.9 4.8 %collective-permute-start.3 = (bf16[48,1536]{1,0:T(8,128)(2,1)S(1)}, bf16[48,1536]{1,0:T(8,128)(2,1)S(1)}, u32[]{:S(2)}, u32[]{:S(2)}) collective-permute-start(bf16[48,1536]{1,0:T(8,128)(2,1)S(1)} %get-tuple-element.25.refs_2_), channel_id=1, source_target_pairs={{0,8},{8,0},{1,9},{9,1},{2,10},{10,2},{3,11},{11,3},{4,12},{12,4},... | collective-permute-start | bytes 442376 | tf_op jit(solution)/shard_map/ppermute | solution.py:176
  50.7 9.1 %collective-permute-start.4 = (bf16[48,768]{1,0:T(8,128)(2,1)S(1)}, bf16[48,768]{1,0:T(8,128)(2,1)S(1)}, u32[]{:S(2)}, u32[]{:S(2)}) collective-permute-start(bf16[48,768]{1,0:T(8,128)(2,1)S(1)} %get-tuple-element.23.refs_2_), channel_id=1, source_target_pairs={{0,16},{16,0},{1,17},{17,1},{2,18},{18,2},{3,19},{19,3},{4,20},{20... | collective-permute-start | bytes 221192 | tf_op jit(solution)/shard_map/ppermute | solution.py:176
  59.9 3.8 %collective-permute-done.4.refs_1_ = bf16[48,768]{1,0:T(8,128)(2,1)S(1)} collective-permute-done((bf16[48,768]{1,0:T(8,128)(2,1)S(1)}, bf16[48,768]{1,0:T(8,128)(2,1)S(1)}, u32[]{:S(2)}, u32[]{:S(2)}) %collective-permute-start.4) | collective-permute-done | bytes 73760 | tf_op jit(solution)/shard_map/ppermute | solution.py:176
  63.7 8.6 %all_to_all.20.refs_2_.refs_0_ = f32[8,8,128]{2,1,0:T(8,128)S(1)} all-to-all(f32[8,8,128]{2,1,0:T(8,128)S(1)} %shard_map.35), channel_id=1, replica_groups=mesh['zh'=2,'xc'=8,'zf'=2,'z2'=2,'z1'=2,'y'=4] {'xc'}, dimensions={0} | all-to-all | bytes 65536 | tf_op jit(solution)/shard_map/all_to_all | solution.py:237
  72.3 0.0 collective-permute-done.3.refs_1_
  72.3 0.1 shard_map.36
  72.4 6.4 %collective-permute-start.5 = (bf16[48,1536]{1,0:T(8,128)(2,1)S(1)}, bf16[48,1536]{1,0:T(8,128)(2,1)S(1)}, u32[]{:S(2)}, u32[]{:S(2)}) collective-permute-start(bf16[48,1536]{1,0:T(8,128)(2,1)S(1)} %get-tuple-element.28.refs_1_), channel_id=1, source_target_pairs={{0,16},{16,0},{1,17},{17,1},{2,18},{18,2},{3,19},{19,3},{4,20},{20... | collective-permute-start | bytes 442376 | tf_op jit(solution)/shard_map/ppermute | solution.py:176
  78.8 8.6 %collective-permute-start.6 = (f32[8,128]{1,0:T(8,128)S(1)}, f32[8,128]{1,0:T(8,128)S(1)}, u32[]{:S(2)}, u32[]{:S(2)}) collective-permute-start(f32[8,128]{1,0:T(8,128)S(1)} %shard_map.37.refs_2_), channel_id=1, source_target_pairs={{0,256},{256,0},{1,257},{257,1},{2,258},{258,2},{3,259},{259,3},{4... | collective-permute-start | bytes 12296 | tf_op jit(solution)/shard_map/ppermute | solution.py:176
  87.4 5.7 %collective-permute-done.6.refs_3_ = f32[8,128]{1,0:T(8,128)S(1)} collective-permute-done((f32[8,128]{1,0:T(8,128)S(1)}, f32[8,128]{1,0:T(8,128)S(1)}, u32[]{:S(2)}, u32[]{:S(2)}) %collective-permute-start.6) | collective-permute-done | bytes 4128 | tf_op jit(solution)/shard_map/ppermute | solution.py:176
  93.2 0.2 collective-permute-done.5.refs_1_
  93.4 6.6 %collective-permute-start.7 = (bf16[48,1664]{1,0:T(8,128)(2,1)S(1)}, bf16[48,1664]{1,0:T(8,128)(2,1)S(1)}, u32[]{:S(2)}, u32[]{:S(2)}) collective-permute-start(bf16[48,1664]{1,0:T(8,128)(2,1)S(1)} %shard_map.38.refs_0_), channel_id=1, source_target_pairs={{0,8},{8,0},{1,9},{9,1},{2,10},{10,2},{3,11},{11,3},{4,12},{12,4},... | collective-permute-start | bytes 479240 | tf_op jit(solution)/shard_map/ppermute | solution.py:176
  100.0 4.7 %collective-permute-done.7.refs_1_ = bf16[48,1664]{1,0:T(8,128)(2,1)S(1)} collective-permute-done((bf16[48,1664]{1,0:T(8,128)(2,1)S(1)}, bf16[48,1664]{1,0:T(8,128)(2,1)S(1)}, u32[]{:S(2)}, u32[]{:S(2)}) %collective-permute-start.7) | collective-permute-done | bytes 159776 | tf_op jit(solution)/shard_map/ppermute | solution.py:176
  104.7 1.9 %collective-permute-start.8 = (bf16[96,1664]{1,0:T(8,128)(2,1)S(1)}, bf16[96,1664]{1,0:T(8,128)(2,1)S(1)}, u32[]{:S(2)}, u32[]{:S(2)}) collective-permute-start(bf16[96,1664]{1,0:T(8,128)(2,1)S(1)} %shard_map.39.refs_0_), channel_id=1, source_target_pairs={{0,4},{4,0},{1,5},{5,1},{2,6},{6,2},{3,7},{7,3},{8,12},{12,8},{9,1... | collective-permute-start | bytes 958472 | tf_op jit(solution)/shard_map/ppermute | solution.py:176
  106.7 9.3 %collective-permute-done.8.refs_1_ = bf16[96,1664]{1,0:T(8,128)(2,1)S(1)} collective-permute-done((bf16[96,1664]{1,0:T(8,128)(2,1)S(1)}, bf16[96,1664]{1,0:T(8,128)(2,1)S(1)}, u32[]{:S(2)}, u32[]{:S(2)}) %collective-permute-start.8) | collective-permute-done | bytes 319520 | tf_op jit(solution)/shard_map/ppermute | solution.py:176
  116.0 0.7 shard_map.40
  116.6 8.8 %all_to_all.21.refs_0_ = bf16[4,208,128]{2,1,0:T(8,128)(2,1)S(1)} all-to-all(bf16[4,208,128]{2,1,0:T(8,128)(2,1)S(1)} %shard_map.40), channel_id=1, replica_groups=mesh['zh'=2,'xc'=8,'zf'=2,'z2'=2,'z1'=2,'y'=4] {'y'}, dimensions={0} | all-to-all | bytes 425984 | tf_op jit(solution)/shard_map/all_to_all | solution.py:262
  125.4 1.1 shard_map.41
  (5 shorter events, 0.1 us)
Async XLA Ops:
  0.0 0.9 copy-start.1
  2.0 4.6 %copy-start = (bf16[128,768]{1,0:T(8,128)(2,1)S(1)}, bf16[128,768]{1,0:T(8,128)(2,1)}, u32[]{:S(2)}) copy-start(bf16[128,768]{1,0:T(8,128)(2,1)} %refs_1_.1) | copy-start | bytes 589828
  2.0 16.9 %all-to-all-start.1 = ((bf16[4,128,768]{2,1,0:T(8,128)(2,1)}), bf16[4,128,768]{2,1,0:T(8,128)(2,1)S(1)}, u32[]{:S(2)}, u32[]{:S(2)}) async-start(bf16[4,128,768]{2,1,0:T(8,128)(2,1)} %shard_map.29), calls=%async_computation.1 | async-start | bytes 1572864 | tf_op jit(solution)/shard_map/all_to_all | solution.py:182
  18.9 14.8 %all-to-all-start = ((bf16[4,128,768]{2,1,0:T(8,128)(2,1)}), bf16[4,128,768]{2,1,0:T(8,128)(2,1)S(1)}, u32[]{:S(2)}, u32[]{:S(2)}) async-start(bf16[4,128,768]{2,1,0:T(8,128)(2,1)} %shard_map.28), calls=%async_computation | async-start | bytes 1572864 | tf_op jit(solution)/shard_map/all_to_all | solution.py:182
  22.9 7.0 %collective-permute-start = (bf16[96,768]{1,0:T(8,128)(2,1)S(1)}, bf16[96,768]{1,0:T(8,128)(2,1)S(1)}, u32[]{:S(2)}, u32[]{:S(2)}) collective-permute-start(bf16[96,768]{1,0:T(8,128)(2,1)S(1)} %get-tuple-element.18), channel_id=1, source_target_pairs={{0,4},{4,0},{1,5},{5,1},{2,6},{6,2},{3,7},{7,3},{8,12},{12,8},{9,1... | collective-permute-start | bytes 442376 | tf_op jit(solution)/shard_map/ppermute | solution.py:176
  34.4 11.4 %collective-permute-start.1 = (bf16[96,1536]{1,0:T(8,128)(2,1)S(1)}, bf16[96,1536]{1,0:T(8,128)(2,1)S(1)}, u32[]{:S(2)}, u32[]{:S(2)}) collective-permute-start(bf16[96,1536]{1,0:T(8,128)(2,1)S(1)} %get-tuple-element.21), channel_id=1, source_target_pairs={{0,4},{4,0},{1,5},{5,1},{2,6},{6,2},{3,7},{7,3},{8,12},{12,8},{9,1... | collective-permute-start | bytes 884744 | tf_op jit(solution)/shard_map/ppermute | solution.py:176
  38.3 7.5 %collective-permute-start.2 = (bf16[48,768]{1,0:T(8,128)(2,1)S(1)}, bf16[48,768]{1,0:T(8,128)(2,1)S(1)}, u32[]{:S(2)}, u32[]{:S(2)}) collective-permute-start(bf16[48,768]{1,0:T(8,128)(2,1)S(1)} %get-tuple-element.19.refs_2_), channel_id=1, source_target_pairs={{0,8},{8,0},{1,9},{9,1},{2,10},{10,2},{3,11},{11,3},{4,12},{12,4},... | collective-permute-start | bytes 221192 | tf_op jit(solution)/shard_map/ppermute | solution.py:176
  45.9 26.4 %collective-permute-start.3 = (bf16[48,1536]{1,0:T(8,128)(2,1)S(1)}, bf16[48,1536]{1,0:T(8,128)(2,1)S(1)}, u32[]{:S(2)}, u32[]{:S(2)}) collective-permute-start(bf16[48,1536]{1,0:T(8,128)(2,1)S(1)} %get-tuple-element.25.refs_2_), channel_id=1, source_target_pairs={{0,8},{8,0},{1,9},{9,1},{2,10},{10,2},{3,11},{11,3},{4,12},{12,4},... | collective-permute-start | bytes 442376 | tf_op jit(solution)/shard_map/ppermute | solution.py:176
  50.7 12.9 %collective-permute-start.4 = (bf16[48,768]{1,0:T(8,128)(2,1)S(1)}, bf16[48,768]{1,0:T(8,128)(2,1)S(1)}, u32[]{:S(2)}, u32[]{:S(2)}) collective-permute-start(bf16[48,768]{1,0:T(8,128)(2,1)S(1)} %get-tuple-element.23.refs_2_), channel_id=1, source_target_pairs={{0,16},{16,0},{1,17},{17,1},{2,18},{18,2},{3,19},{19,3},{4,20},{20... | collective-permute-start | bytes 221192 | tf_op jit(solution)/shard_map/ppermute | solution.py:176
  72.4 21.0 %collective-permute-start.5 = (bf16[48,1536]{1,0:T(8,128)(2,1)S(1)}, bf16[48,1536]{1,0:T(8,128)(2,1)S(1)}, u32[]{:S(2)}, u32[]{:S(2)}) collective-permute-start(bf16[48,1536]{1,0:T(8,128)(2,1)S(1)} %get-tuple-element.28.refs_1_), channel_id=1, source_target_pairs={{0,16},{16,0},{1,17},{17,1},{2,18},{18,2},{3,19},{19,3},{4,20},{20... | collective-permute-start | bytes 442376 | tf_op jit(solution)/shard_map/ppermute | solution.py:176
  78.8 14.4 %collective-permute-start.6 = (f32[8,128]{1,0:T(8,128)S(1)}, f32[8,128]{1,0:T(8,128)S(1)}, u32[]{:S(2)}, u32[]{:S(2)}) collective-permute-start(f32[8,128]{1,0:T(8,128)S(1)} %shard_map.37.refs_2_), channel_id=1, source_target_pairs={{0,256},{256,0},{1,257},{257,1},{2,258},{258,2},{3,259},{259,3},{4... | collective-permute-start | bytes 12296 | tf_op jit(solution)/shard_map/ppermute | solution.py:176
  93.4 11.3 %collective-permute-start.7 = (bf16[48,1664]{1,0:T(8,128)(2,1)S(1)}, bf16[48,1664]{1,0:T(8,128)(2,1)S(1)}, u32[]{:S(2)}, u32[]{:S(2)}) collective-permute-start(bf16[48,1664]{1,0:T(8,128)(2,1)S(1)} %shard_map.38.refs_0_), channel_id=1, source_target_pairs={{0,8},{8,0},{1,9},{9,1},{2,10},{10,2},{3,11},{11,3},{4,12},{12,4},... | collective-permute-start | bytes 479240 | tf_op jit(solution)/shard_map/ppermute | solution.py:176
  104.7 11.2 %collective-permute-start.8 = (bf16[96,1664]{1,0:T(8,128)(2,1)S(1)}, bf16[96,1664]{1,0:T(8,128)(2,1)S(1)}, u32[]{:S(2)}, u32[]{:S(2)}) collective-permute-start(bf16[96,1664]{1,0:T(8,128)(2,1)S(1)} %shard_map.39.refs_0_), channel_id=1, source_target_pairs={{0,4},{4,0},{1,5},{5,1},{2,6},{6,2},{3,7},{7,3},{8,12},{12,8},{9,1... | collective-permute-start | bytes 958472 | tf_op jit(solution)/shard_map/ppermute | solution.py:176

commit v2 on v1

--- a/solution.py
+++ b/solution.py
@@ -91,17 +91,25 @@
     split_rows(sums, "z1", keep_ref, give_ref)
 
 
-def student_kernel(ring_s, ring_t, keep_ref, give_ref, flip, sums):
+def student_kernel(ring_s, ring_t, give_ref, flip):
     width = ring_s.shape[1]
-    part = sums.shape[0]
+    quad, rows = give_ref.shape[:2]
+    part = quad * rows
     left = turned(ring_s, flip)
     row = lax.broadcasted_iota(jnp.int32, (part, width), 0) + lax.axis_index("y") * part
     on = row == lax.broadcasted_iota(jnp.int32, (part, width), 1)
-    sums[:, :width] = jnp.dot(left, ring_s[...], preferred_element_type=F32) - jnp.where(
-        on, ring_s.shape[0] / width, 0.0
-    )
-    sums[:, width:] = -jnp.dot(left, ring_t[...], preferred_element_type=F32)
-    split_rows(sums, "z1", keep_ref, give_ref)
+    ss = jnp.dot(left, ring_s[...], preferred_element_type=F32)
+    ss = (ss - jnp.where(on, ring_s.shape[0] / width, 0.0)).astype(BF16)
+    st = -jnp.dot(left, ring_t[...], preferred_element_type=F32).astype(BF16)
+    for i in range(quad):
+        give_ref[i, :, :width] = ss[i * rows : (i + 1) * rows]
+        give_ref[i, :, width:] = st[i * rows : (i + 1) * rows]
+
+
+def quad_kernel(got_ref, total_ref, send_ref):
+    total = jnp.sum(got_ref[...].astype(F32), axis=0)
+    total_ref[...] = total
+    send_ref[...] = total.astype(BF16)
 
 
 def halve_kernel(mine_ref, got_ref, keep_ref, give_ref, sums):
@@ -117,7 +125,7 @@
 
 
 def energies_kernel(e_ref, out_ref):
-    out_ref[...] = jnp.sum(e_ref[...], axis=0)
+    out_ref[...] = jnp.broadcast_to(jnp.sum(e_ref[...], axis=0), out_ref.shape)
 
 
 def add_kernel(mine_ref, got_ref, total_ref, send_ref):
@@ -126,33 +134,16 @@
     send_ref[...] = total.astype(BF16)
 
 
-def exchange_kernel(mine_ref, got_ref, e_ref, f_ref, out_ref):
-    main = mine_ref.shape[1]
-    out_ref[:, :main] = (mine_ref[...] + got_ref[...].astype(F32)).astype(BF16)
-    out_ref[:, main:] = jnp.zeros((out_ref.shape[0], LANES), BF16)
-    out_ref[0:TILE, main:] = split3(e_ref[0:1] + f_ref[0:1])
-
-
-def double_kernel(mine_ref, got_ref, out_ref):
-    z2 = lax.axis_index("z2")
-    rows, wide = mine_ref.shape
-    main = wide - LANES
-    out_ref[pl.ds(pl.multiple_of(z2 * rows, TILE), rows)] = mine_ref[...]
-    out_ref[pl.ds(pl.multiple_of((1 - z2) * rows, TILE), rows)] = got_ref[...]
-    e = join3(mine_ref[0:TILE, main:]) + join3(got_ref[0:TILE, main:])
-    out_ref[0:TILE, main:] = split3(e)
-
-
-def pull_kernel(mine_ref, got_ref, ring_s, ring_t, out_ref, whole):
-    z1 = lax.axis_index("z1")
-    rows, wide = mine_ref.shape
-    main = wide - LANES
-    whole[pl.ds(pl.multiple_of(z1 * rows, TILE), rows)] = mine_ref[:, :main]
-    whole[pl.ds(pl.multiple_of((1 - z1) * rows, TILE), rows)] = got_ref[:, :main]
-    width, part = main // 2, 2 * rows
+def exchange_kernel(mine_ref, got_ref, out_ref):
+    out_ref[...] = jnp.broadcast_to(
+        (mine_ref[...] + got_ref[...].astype(F32)).astype(BF16), out_ref.shape
+    )
+
+
+def pull_kernel(whole, ring_s, ring_t, e_ref, f_ref, out_ref):
+    part, width = whole.shape[0], whole.shape[1] // 2
     pull = nt(whole[:, :width], ring_s[...]) + nt(whole[:, width:], ring_t[...])
-    e = join3(mine_ref[0:TILE, main:]) + join3(got_ref[0:TILE, main:])
-    parts = split3(e)
+    parts = split3(e_ref[0:1] + f_ref[0:1])
     n = out_ref.shape[2]
     for i in range(NY):
         out_ref[i, 0:part] = pull[:, i * n : (i + 1) * n].astype(BF16)
@@ -200,64 +191,52 @@
     ring_t = gather_y(teacher)
     ring_s = gather_y(student)
 
+    quad = ("z2", "z1")
     tt, tt_give = call(teacher_kernel, pair(half, width), [ring_t], 2 * mac, scratch(width))
     tt_got = swap(tt_give, "z1")
     tt, tt_give = call(
         halve_kernel, pair(rows, width), [tt, tt_got], part * width, [pltpu.VMEM((half, width), F32)]
     )
     tt_got = swap(tt_give, "z2")
-    keep, give = call(
+    tt, tt_give = call(add_kernel, pair(rows, width), [tt, tt_got], rows * width)
+    tt_got = swap(tt_give, "zf")
+    (give,) = call(
         student_kernel,
-        pair(half, 2 * width),
+        [struct((4, rows, 2 * width), BF16)],
         [ring_s, ring_t],
         4 * mac,
-        scratch(2 * width),
+        [pltpu.VMEM((2 * LANES, texts), BF16)],
         after=[tt_give],
     )
-    got = swap(give, "z1")
-    tt, tt_give = call(add_kernel, pair(rows, width), [tt, tt_got], rows * width)
-    tt_got = swap(tt_give, "zf")
+    got = lax.all_to_all(give, quad, 0, 0)
     keep, give = call(
-        halve_kernel,
-        pair(rows, 2 * width),
-        [keep, got],
-        2 * part * width,
-        [pltpu.VMEM((half, 2 * width), F32)],
-        after=[tt_give],
-    )
-    got = swap(give, "z2")
-    near = lax.axis_size("xc")
+        quad_kernel, pair(rows, 2 * width), [got], 4 * rows * width, after=[tt_got]
+    )
+    got = swap(give, "zf")
+    some = ("xc", "z2", "z1")
     (e,) = call(
         energy_kernel,
-        [struct((near, 8, LANES), F32)],
+        [struct((lax.axis_size(some), 1, LANES), F32)],
         [tt, tt_got],
         3 * rows * width,
         after=[give],
     )
-    e = lax.all_to_all(e, "xc", 0, 0)
-    keep, give = call(
-        add_kernel, pair(rows, 2 * width), [keep, got], 2 * rows * width, after=[e]
-    )
-    got = swap(give, "zf")
-    (e,) = call(energies_kernel, [struct((8, LANES), F32)], [e], e.size, after=[give])
-    e_far = swap(e, "zh")
+    e = lax.all_to_all(e, some, 0, 0)
     (mine,) = call(
         exchange_kernel,
-        [struct((rows, 2 * width + LANES), BF16)],
-        [keep, got, e, e_far],
+        [struct((4, rows, 2 * width), BF16)],
+        [keep, got],
         2 * rows * width,
-    )
-    got = swap(mine, "z2")
-    (mine,) = call(
-        double_kernel, [struct((half, 2 * width + LANES), BF16)], [mine, got], 2 * rows * width
-    )
-    got = swap(mine, "z1")
+        after=[e],
+    )
+    whole = lax.all_to_all(mine, quad, 0, 0).reshape(part, 2 * width)
+    (e,) = call(energies_kernel, [struct((8, LANES), F32)], [e], e.size, after=[mine])
+    e_far = swap(e, "zh")
     (blocks,) = call(
         pull_kernel,
         [struct((NY, part + TILE, n), BF16)],
-        [mine, got, ring_s, ring_t],
+        [whole, ring_s, ring_t, e, e_far],
         4 * mac,
-        [pltpu.VMEM((part, 2 * width), BF16)],
     )
     blocks = lax.all_to_all(blocks, "y", 0, 0)
     (out,) = call(

time: 127 us -> 119 us (0.937)
  waiting for transfers between devices: 44.2 us -> 32 us
  blocking collectives: 17.4 us -> 23.7 us
  starting transfers between devices: 58.4 us -> 55.1 us
  Pallas kernels: 5.36 us -> 6.83 us
    ppermute x9 -> x5, starting transfers between devices: 50.3 us -> 37.7 us  [swap(): return lax.ppermute(x, axis, [(0, 1), (1, 0)])]
    ppermute x9 -> x5, waiting for transfers between devices: 29.2 us -> 16.8 us  [swap(): return lax.ppermute(x, axis, [(0, 1), (1, 0)])]
    all_to_all x0 -> x2, starting transfers between devices: none -> 9.34 us  [the longest x1 5.86 us: on_device(): got = lax.all_to_all(give, quad, 0, 0)]
    all_to_all x1, blocking collectives: 8.61 us -> 13 us  [on_device(): e = lax.all_to_all(e, some, 0, 0)]
    all_to_all x0 -> x2, waiting for transfers between devices: none -> 3.91 us  [the longest x1 3.91 us: on_device(): got = lax.all_to_all(give, quad, 0, 0)]
    all_to_all x2, waiting for transfers between devices: 15 us -> 11.2 us  [gather_y(): return lax.all_to_all(copies, 'y', 0, 0).reshape(NY * n, width)]
    all_to_all x1, blocking collectives: 8.79 us -> 10.7 us  [on_device(): blocks = lax.all_to_all(blocks, 'y', 0, 0)]
    pallas_call x14 -> x12, Pallas kernels: 5.36 us -> 6.83 us  [call(): pl.pallas_call(run, out_shape=out_shape, in_specs=[whole] * count + [pl.B...]
  transfers between devices with their start and end apart: 11 -> 9, of which waited for: 9 -> 6; matrix products, arithmetic and copies ran while one was open for 0% -> 0% of each run, Pallas kernels for 1% -> 1%
where the time goes in v2:
time: 119 us
  starting transfers between devices  55.1 us (46%)
  waiting for transfers between devices  32 us (27%)
  blocking collectives  23.7 us (20%)
  Pallas kernels  6.83 us (6%)
    ppermute x5, starting transfers between devices, swap(): return lax.ppermute(x, axis, [(0, 1), (1, 0)])  37.7 us
    ppermute x5, waiting for transfers between devices, swap(): return lax.ppermute(x, axis, [(0, 1), (1, 0)])  16.8 us
    all_to_all x1, blocking collectives, on_device(): e = lax.all_to_all(e, some, 0, 0)  13 us
    all_to_all x2, waiting for transfers between devices, gather_y(): return lax.all_to_all(copies, 'y', 0, 0).reshape(NY * n, width)  11.2 us
    all_to_all x1, blocking collectives, on_device(): blocks = lax.all_to_all(blocks, 'y', 0, 0)  10.7 us
    all_to_all x2, starting transfers between devices, gather_y(): return lax.all_to_all(copies, 'y', 0, 0).reshape(NY * n, width)  8.09 us
    pallas_call x12, Pallas kernels, call(): pl.pallas_call(run, out_shape=out_shape, in_specs=[whole] * count + [pl.B...  6.83 us
    all_to_all x1, starting transfers between devices, on_device(): got = lax.all_to_all(give, quad, 0, 0)  5.86 us
  transfers between devices with their start and end apart: 9, of which 6 were waited for; matrix products, arithmetic and copies ran while one was open for 0% of the time, Pallas kernels for 1%

profile of v2, /device:TPU:2, one launch (start us, length us, event | category | flops | bytes accessed | tf_op | source)
XLA Modules:
  0.0 118.6 jit_solution(16665947054444297804)
XLA Ops:
  0.0 0.0 copy-start.1
  0.0 0.9 copy-done.1
  0.9 1.1 shard_map.29
  2.0 0.0 copy-start
  2.0 4.6 %all-to-all-start.1 = ((bf16[4,128,768]{2,1,0:T(8,128)(2,1)}), bf16[4,128,768]{2,1,0:T(8,128)(2,1)S(1)}, u32[]{:S(2)}, u32[]{:S(2)}) async-start(bf16[4,128,768]{2,1,0:T(8,128)(2,1)} %shard_map.29), calls=%async_computation.1 | async-start | bytes 1572864 | tf_op jit(solution)/shard_map/all_to_all | solution.py:173
  6.6 0.0 copy-done
  6.6 1.0 shard_map.28
  7.6 11.2 %all-to-all-done.1 = bf16[4,128,768]{2,1,0:T(8,128)(2,1)S(1)} async-done(((bf16[4,128,768]{2,1,0:T(8,128)(2,1)}), bf16[4,128,768]{2,1,0:T(8,128)(2,1)S(1)}, u32[]{:S(2)}, u32[]{:S(2)}) %all-to-all-start.1) | async-done | bytes 786464 | tf_op jit(solution)/shard_map/all_to_all | solution.py:173
  18.9 3.5 %all-to-all-start = ((bf16[4,128,768]{2,1,0:T(8,128)(2,1)}), bf16[4,128,768]{2,1,0:T(8,128)(2,1)S(1)}, u32[]{:S(2)}, u32[]{:S(2)}) async-start(bf16[4,128,768]{2,1,0:T(8,128)(2,1)} %shard_map.28), calls=%async_computation | async-start | bytes 1572864 | tf_op jit(solution)/shard_map/all_to_all | solution.py:173
  22.4 0.5 shard_map.30
  22.8 3.8 %collective-permute-start = (bf16[96,768]{1,0:T(8,128)(2,1)S(1)}, bf16[96,768]{1,0:T(8,128)(2,1)S(1)}, u32[]{:S(2)}, u32[]{:S(2)}) collective-permute-start(bf16[96,768]{1,0:T(8,128)(2,1)S(1)} %get-tuple-element.14), channel_id=1, source_target_pairs={{0,4},{4,0},{1,5},{5,1},{2,6},{6,2},{3,7},{7,3},{8,12},{12,8},{9,1... | collective-permute-start | bytes 442376 | tf_op jit(solution)/shard_map/ppermute | solution.py:167
  26.7 3.2 %collective-permute-done.refs_1_ = bf16[96,768]{1,0:T(8,128)(2,1)S(1)} collective-permute-done((bf16[96,768]{1,0:T(8,128)(2,1)S(1)}, bf16[96,768]{1,0:T(8,128)(2,1)S(1)}, u32[]{:S(2)}, u32[]{:S(2)}) %collective-permute-start) | collective-permute-done | bytes 147488 | tf_op jit(solution)/shard_map/ppermute | solution.py:167
  29.9 5.2 %collective-permute-start.1 = (bf16[48,768]{1,0:T(8,128)(2,1)S(1)}, bf16[48,768]{1,0:T(8,128)(2,1)S(1)}, u32[]{:S(2)}, u32[]{:S(2)}) collective-permute-start(bf16[48,768]{1,0:T(8,128)(2,1)S(1)} %get-tuple-element.16), channel_id=1, source_target_pairs={{0,8},{8,0},{1,9},{9,1},{2,10},{10,2},{3,11},{11,3},{4,12},{12,4},... | collective-permute-start | bytes 221192 | tf_op jit(solution)/shard_map/ppermute | solution.py:167
  35.1 2.3 %collective-permute-done.1.refs_1_ = bf16[48,768]{1,0:T(8,128)(2,1)S(1)} collective-permute-done((bf16[48,768]{1,0:T(8,128)(2,1)S(1)}, bf16[48,768]{1,0:T(8,128)(2,1)S(1)}, u32[]{:S(2)}, u32[]{:S(2)}) %collective-permute-start.1) | collective-permute-done | bytes 73760 | tf_op jit(solution)/shard_map/ppermute | solution.py:167
  37.5 0.0 all-to-all-done
  37.5 1.4 %shard_map.33 = bf16[4,48,1536]{2,1,0:T(8,128)(2,1)} custom-call(bf16[512,768]{1,0:T(8,128)(2,1)S(1)} %bitcast.6, bf16[512,768]{1,0:T(8,128)(2,1)S(1)} %bitcast.4, bf16[48,768]{1,0:T(8,128)(2,1)S(1)} %get-tuple-element.17.refs_2_), custom_call_target="tpu_custom_call" | custom-call | flops 301989888 | bytes 2162688 | tf_op jit(solution)/shard_map/pallas_call | solution.py:30
  38.9 5.9 %all-to-all-start.2 = ((bf16[4,48,1536]{2,1,0:T(8,128)(2,1)}), bf16[4,48,1536]{2,1,0:T(8,128)(2,1)S(1)}, u32[]{:S(2)}, u32[]{:S(2)}) async-start(bf16[4,48,1536]{2,1,0:T(8,128)(2,1)} %shard_map.33), calls=%async_computation.2 | async-start | bytes 1179648 | tf_op jit(solution)/shard_map/all_to_all | solution.py:211
  44.8 9.1 %collective-permute-start.2 = (bf16[48,768]{1,0:T(8,128)(2,1)S(1)}, bf16[48,768]{1,0:T(8,128)(2,1)S(1)}, u32[]{:S(2)}, u32[]{:S(2)}) collective-permute-start(bf16[48,768]{1,0:T(8,128)(2,1)S(1)} %get-tuple-element.17.refs_2_), channel_id=1, source_target_pairs={{0,16},{16,0},{1,17},{17,1},{2,18},{18,2},{3,19},{19,3},{4,20},{20... | collective-permute-start | bytes 221192 | tf_op jit(solution)/shard_map/ppermute | solution.py:167
  53.9 2.5 %collective-permute-done.2.refs_1_ = bf16[48,768]{1,0:T(8,128)(2,1)S(1)} collective-permute-done((bf16[48,768]{1,0:T(8,128)(2,1)S(1)}, bf16[48,768]{1,0:T(8,128)(2,1)S(1)}, u32[]{:S(2)}, u32[]{:S(2)}) %collective-permute-start.2) | collective-permute-done | bytes 73760 | tf_op jit(solution)/shard_map/ppermute | solution.py:167
  56.3 3.9 %all-to-all-done.2.refs_0_ = bf16[4,48,1536]{2,1,0:T(8,128)(2,1)S(1)} async-done(((bf16[4,48,1536]{2,1,0:T(8,128)(2,1)}), bf16[4,48,1536]{2,1,0:T(8,128)(2,1)S(1)}, u32[]{:S(2)}, u32[]{:S(2)}) %all-to-all-start.2) | async-done | bytes 589856 | tf_op jit(solution)/shard_map/all_to_all | solution.py:211
  60.2 0.1 shard_map.34
  60.3 8.9 %collective-permute-start.3 = (bf16[48,1536]{1,0:T(8,128)(2,1)S(1)}, bf16[48,1536]{1,0:T(8,128)(2,1)S(1)}, u32[]{:S(2)}, u32[]{:S(2)}) collective-permute-start(bf16[48,1536]{1,0:T(8,128)(2,1)S(1)} %get-tuple-element.19.refs_2_), channel_id=1, source_target_pairs={{0,16},{16,0},{1,17},{17,1},{2,18},{18,2},{3,19},{19,3},{4,20},{20... | collective-permute-start | bytes 442376 | tf_op jit(solution)/shard_map/ppermute | solution.py:167
  69.3 13.0 %all_to_all.30.refs_2_.refs_0_ = f32[32,1,128]{2,1,0:T(1,128)S(1)} all-to-all(f32[32,1,128]{2,1,0:T(1,128)S(1)} %shard_map.35), channel_id=1, replica_groups=mesh['zh'=2,'xc'=8,'zf'=2,'z2'=2,'z1'=2,'y'=4] {'xc','z2','z1'}, dimensions={0} | all-to-all | bytes 32768 | tf_op jit(solution)/shard_map/all_to_all | solution.py:224
  82.3 0.0 collective-permute-done.3.refs_1_
  82.3 0.9 shard_map.36.refs_1_
  83.2 3.5 %all-to-all-start.4 = ((bf16[4,48,1536]{2,1,0:T(8,128)(2,1)}), bf16[4,48,1536]{2,1,0:T(8,128)(2,1)S(1)}, u32[]{:S(2)}, u32[]{:S(2)}) async-start(bf16[4,48,1536]{2,1,0:T(8,128)(2,1)} %shard_map.36.refs_1_), calls=%async_computation.4 | async-start | bytes 1179648 | tf_op jit(solution)/shard_map/all_to_all | solution.py:232
  86.7 10.7 %collective-permute-start.4 = (f32[8,128]{1,0:T(8,128)S(1)}, f32[8,128]{1,0:T(8,128)S(1)}, u32[]{:S(2)}, u32[]{:S(2)}) collective-permute-start(f32[8,128]{1,0:T(8,128)S(1)} %shard_map.37.refs_3_), channel_id=1, source_target_pairs={{0,256},{256,0},{1,257},{257,1},{2,258},{258,2},{3,259},{259,3},{4... | collective-permute-start | bytes 12296 | tf_op jit(solution)/shard_map/ppermute | solution.py:167
  97.4 8.8 %collective-permute-done.4.refs_4_ = f32[8,128]{1,0:T(8,128)S(1)} collective-permute-done((f32[8,128]{1,0:T(8,128)S(1)}, f32[8,128]{1,0:T(8,128)S(1)}, u32[]{:S(2)}, u32[]{:S(2)}) %collective-permute-start.4) | collective-permute-done | bytes 4128 | tf_op jit(solution)/shard_map/ppermute | solution.py:167
  106.2 0.0 all-to-all-done.4
  106.2 0.7 shard_map.38
  106.9 10.7 %all_to_all.31.refs_0_ = bf16[4,208,128]{2,1,0:T(8,128)(2,1)S(1)} all-to-all(bf16[4,208,128]{2,1,0:T(8,128)(2,1)S(1)} %shard_map.38), channel_id=1, replica_groups=mesh['zh'=2,'xc'=8,'zf'=2,'z2'=2,'z1'=2,'y'=4] {'y'}, dimensions={0} | all-to-all | bytes 425984 | tf_op jit(solution)/shard_map/all_to_all | solution.py:241
  117.6 1.1 shard_map.39
  (4 shorter events, 0.1 us)
Async XLA Ops:
  0.0 0.9 copy-start.1
  2.0 4.6 %copy-start = (bf16[128,768]{1,0:T(8,128)(2,1)S(1)}, bf16[128,768]{1,0:T(8,128)(2,1)}, u32[]{:S(2)}) copy-start(bf16[128,768]{1,0:T(8,128)(2,1)} %refs_1_.1) | copy-start | bytes 589828
  2.0 16.9 %all-to-all-start.1 = ((bf16[4,128,768]{2,1,0:T(8,128)(2,1)}), bf16[4,128,768]{2,1,0:T(8,128)(2,1)S(1)}, u32[]{:S(2)}, u32[]{:S(2)}) async-start(bf16[4,128,768]{2,1,0:T(8,128)(2,1)} %shard_map.29), calls=%async_computation.1 | async-start | bytes 1572864 | tf_op jit(solution)/shard_map/all_to_all | solution.py:173
  18.9 18.6 %all-to-all-start = ((bf16[4,128,768]{2,1,0:T(8,128)(2,1)}), bf16[4,128,768]{2,1,0:T(8,128)(2,1)S(1)}, u32[]{:S(2)}, u32[]{:S(2)}) async-start(bf16[4,128,768]{2,1,0:T(8,128)(2,1)} %shard_map.28), calls=%async_computation | async-start | bytes 1572864 | tf_op jit(solution)/shard_map/all_to_all | solution.py:173
  22.8 7.0 %collective-permute-start = (bf16[96,768]{1,0:T(8,128)(2,1)S(1)}, bf16[96,768]{1,0:T(8,128)(2,1)S(1)}, u32[]{:S(2)}, u32[]{:S(2)}) collective-permute-start(bf16[96,768]{1,0:T(8,128)(2,1)S(1)} %get-tuple-element.14), channel_id=1, source_target_pairs={{0,4},{4,0},{1,5},{5,1},{2,6},{6,2},{3,7},{7,3},{8,12},{12,8},{9,1... | collective-permute-start | bytes 442376 | tf_op jit(solution)/shard_map/ppermute | solution.py:167
  29.9 7.5 %collective-permute-start.1 = (bf16[48,768]{1,0:T(8,128)(2,1)S(1)}, bf16[48,768]{1,0:T(8,128)(2,1)S(1)}, u32[]{:S(2)}, u32[]{:S(2)}) collective-permute-start(bf16[48,768]{1,0:T(8,128)(2,1)S(1)} %get-tuple-element.16), channel_id=1, source_target_pairs={{0,8},{8,0},{1,9},{9,1},{2,10},{10,2},{3,11},{11,3},{4,12},{12,4},... | collective-permute-start | bytes 221192 | tf_op jit(solution)/shard_map/ppermute | solution.py:167
  38.9 21.3 %all-to-all-start.2 = ((bf16[4,48,1536]{2,1,0:T(8,128)(2,1)}), bf16[4,48,1536]{2,1,0:T(8,128)(2,1)S(1)}, u32[]{:S(2)}, u32[]{:S(2)}) async-start(bf16[4,48,1536]{2,1,0:T(8,128)(2,1)} %shard_map.33), calls=%async_computation.2 | async-start | bytes 1179648 | tf_op jit(solution)/shard_map/all_to_all | solution.py:211
  44.8 11.6 %collective-permute-start.2 = (bf16[48,768]{1,0:T(8,128)(2,1)S(1)}, bf16[48,768]{1,0:T(8,128)(2,1)S(1)}, u32[]{:S(2)}, u32[]{:S(2)}) collective-permute-start(bf16[48,768]{1,0:T(8,128)(2,1)S(1)} %get-tuple-element.17.refs_2_), channel_id=1, source_target_pairs={{0,16},{16,0},{1,17},{17,1},{2,18},{18,2},{3,19},{19,3},{4,20},{20... | collective-permute-start | bytes 221192 | tf_op jit(solution)/shard_map/ppermute | solution.py:167
  60.3 22.0 %collective-permute-start.3 = (bf16[48,1536]{1,0:T(8,128)(2,1)S(1)}, bf16[48,1536]{1,0:T(8,128)(2,1)S(1)}, u32[]{:S(2)}, u32[]{:S(2)}) collective-permute-start(bf16[48,1536]{1,0:T(8,128)(2,1)S(1)} %get-tuple-element.19.refs_2_), channel_id=1, source_target_pairs={{0,16},{16,0},{1,17},{17,1},{2,18},{18,2},{3,19},{19,3},{4,20},{20... | collective-permute-start | bytes 442376 | tf_op jit(solution)/shard_map/ppermute | solution.py:167
  83.2 23.0 %all-to-all-start.4 = ((bf16[4,48,1536]{2,1,0:T(8,128)(2,1)}), bf16[4,48,1536]{2,1,0:T(8,128)(2,1)S(1)}, u32[]{:S(2)}, u32[]{:S(2)}) async-start(bf16[4,48,1536]{2,1,0:T(8,128)(2,1)} %shard_map.36.refs_1_), calls=%async_computation.4 | async-start | bytes 1179648 | tf_op jit(solution)/shard_map/all_to_all | solution.py:232
  86.7 19.5 %collective-permute-start.4 = (f32[8,128]{1,0:T(8,128)S(1)}, f32[8,128]{1,0:T(8,128)S(1)}, u32[]{:S(2)}, u32[]{:S(2)}) collective-permute-start(f32[8,128]{1,0:T(8,128)S(1)} %shard_map.37.refs_3_), channel_id=1, source_target_pairs={{0,256},{256,0},{1,257},{257,1},{2,258},{258,2},{3,259},{259,3},{4... | collective-permute-start | bytes 12296 | tf_op jit(solution)/shard_map/ppermute | solution.py:167

commit v3 on v2

v3 whole, which is shorter than its diff:
```python
import functools

import jax
import jax.numpy as jnp
from jax import lax
from jax.experimental import pallas as pl
from jax.experimental.pallas import tpu as pltpu
from jax.sharding import Mesh, PartitionSpec as P

NY = 4
NZ = 8
LANES = 128
TILE = 16
F32 = jnp.float32
BF16 = jnp.bfloat16
COL = ("zf", "z2", "z1", "y")
ALL = ("zh", "xc") + COL
VMEM_LIMIT = 12 * 1024 * 1024


def call(body, out_shape, operands, flops, scratch=(), after=()):
    size = sum(a.size * a.dtype.itemsize for a in operands)
    size += sum(s.size * s.dtype.itemsize for s in out_shape)
    count, extra = len(operands), len(after)

    def run(*refs):
        body(*refs[:count], *refs[count + extra :])

    whole = pl.BlockSpec(memory_space=pltpu.VMEM)
    return pl.pallas_call(
        run,
        out_shape=out_shape,
        in_specs=[whole] * count + [pl.BlockSpec(memory_space=pl.ANY)] * extra,
        out_specs=[whole] * len(out_shape),
        scratch_shapes=scratch,
        compiler_params=pltpu.CompilerParams(vmem_limit_bytes=VMEM_LIMIT),
        cost_estimate=pl.CostEstimate(flops=flops, bytes_accessed=size, transcendentals=0),
    )(*operands, *after)


def struct(shape, dtype):
    return jax.ShapeDtypeStruct(shape, dtype)


def unit_rows(values):
    wide = values.astype(F32)
    length = jnp.sqrt(jnp.sum(wide * wide, axis=-1, keepdims=True) + 1e-06)
    return (wide / length, length)


def split3(e):
    high = e.astype(BF16).astype(F32)
    mid = (e - high).astype(BF16).astype(F32)
    low = e - high - mid
    row = lax.broadcasted_iota(jnp.int32, (TILE, LANES), 0)
    parts = jnp.where(row == 0, high, jnp.where(row == 1, mid, jnp.where(row == 2, low, 0.0)))
    return parts.astype(BF16)


def join3(parts):
    return jnp.sum(parts.astype(F32), axis=0, keepdims=True)


def units_kernel(s_ref, t_ref, own_ref):
    width = s_ref.shape[1]
    own_ref[:, :width] = unit_rows(s_ref[...])[0].astype(BF16)
    own_ref[:, width:] = unit_rows(t_ref[...])[0].astype(BF16)


def nt(left, right):
    return lax.dot_general(left, right, (((1,), (1,)), ((), ())), preferred_element_type=F32)


def turned(ring_ref, at, part, flip):
    begin = lax.axis_index("y") * part // LANES * LANES
    rest = pl.multiple_of(lax.axis_index("y") * part - begin, TILE)
    flip[...] = ring_ref[:, pl.ds(pl.multiple_of(at + begin, LANES), 2 * LANES)].T
    return flip[pl.ds(rest, part)]


def products_kernel(own, prev, following, top, bottom, ring_ref, give_ref, flip):
    n, width = own.shape[0], own.shape[1] // 2
    y = lax.axis_index("y")
    for d, at, ref in ((0, 0, own), (3, 0, prev), (1, 0, following), (2, 0, top), (2, n // 2, bottom)):
        begin = pl.multiple_of(lax.rem(y + d, NY) * n + at, n // 2)
        ring_ref[pl.ds(begin, ref.shape[0])] = ref[...]
    quad, rows = give_ref.shape[:2]
    part = quad * rows
    left = turned(ring_ref, 0, part, flip)
    ss = jnp.dot(left, ring_ref[:, :width], preferred_element_type=F32)
    row = lax.broadcasted_iota(jnp.int32, (part, width), 0) + y * part
    on = row == lax.broadcasted_iota(jnp.int32, (part, width), 1)
    ss = ss - jnp.where(on, NY * n / width, 0.0)
    st = -jnp.dot(left, ring_ref[:, width:], preferred_element_type=F32)
    left = turned(ring_ref, width, part, flip)
    tt = jnp.dot(left, ring_ref[:, width:], preferred_element_type=F32)
    for at, sums in ((0, ss), (width, st), (2 * width, tt)):
        for i in range(quad):
            give_ref[i, :, at : at + width] = sums[i * rows : (i + 1) * rows].astype(BF16)


def quad_kernel(got_ref, *refs):
    total = jnp.sum(got_ref[...].astype(F32), axis=0)
    at = 0
    for total_ref, send_ref in (refs[:2], refs[2:]):
        piece = total[:, at : at + total_ref.shape[1]]
        total_ref[...] = piece
        send_ref[...] = piece.astype(BF16)
        at += total_ref.shape[1]


def energy_kernel(mine_ref, got_ref, e_ref):
    tt = mine_ref[...] + got_ref[...].astype(F32)
    e = jnp.sum(tt * tt, axis=0, keepdims=True)
    e = sum(e[:, i : i + LANES] for i in range(0, e.shape[1], LANES))
    e_ref[...] = jnp.broadcast_to(e, e_ref.shape)


def energies_kernel(e_ref, out_ref):
    out_ref[...] = jnp.broadcast_to(jnp.sum(e_ref[...], axis=0), out_ref.shape)


def exchange_kernel(mine_ref, got_ref, out_ref):
    total = (mine_ref[...] + got_ref[...].astype(F32)).astype(BF16)
    for i in range(out_ref.shape[0]):
        out_ref[i] = total


def pull_kernel(whole, ring_ref, e_ref, f_ref, out_ref):
    part, n = whole.shape[0], out_ref.shape[2]
    pull = nt(whole[...], ring_ref[...])
    parts = split3(e_ref[0:1] + f_ref[0:1])
    for i in range(NY):
        out_ref[i, 0:part] = pull[:, i * n : (i + 1) * n].astype(BF16)
        out_ref[i, part:] = parts


def finish_kernel(scale, diag, blocks_ref, student_ref, out_ref):
    n, width = student_ref.shape
    part = width // NY
    parts = sum(join3(blocks_ref[i, part:]) for i in range(NY))
    energy = jnp.sum(parts, axis=1, keepdims=True)
    factor = scale / energy
    unit_f, norm_s = unit_rows(student_ref[...])
    pull_t = jnp.concatenate([blocks_ref[i, 0:part].astype(F32) for i in range(NY)], axis=0)
    pull = (pull_t.T + diag * unit_f.astype(BF16).astype(F32)) * factor
    along = jnp.sum(pull * unit_f, axis=-1, keepdims=True)
    out_ref[...] = (pull - along * unit_f) / norm_s


def swap(x, axis):
    return lax.ppermute(x, axis, [(0, 1), (1, 0)])


def shift_y(x, d):
    return lax.ppermute(x, "y", [(i, (i + d) % NY) for i in range(NY)])


def on_device(student, teacher):
    n, width = student.shape
    batch_texts = n * lax.axis_size(COL)
    total_texts = n * lax.axis_size(ALL)
    part = width // NY
    rows = part // 4
    texts = n * NY
    mac = texts * part * width
    quad = ("z2", "z1")

    def pair(wide):
        return [struct((rows, wide), F32), struct((rows, wide), BF16)]

    (own,) = call(units_kernel, [struct((n, 2 * width), BF16)], [student, teacher], 10 * n * width)
    prev = shift_y(own, 1)
    following = shift_y(own, -1)
    top = shift_y(prev[: n // 2], 1)
    bottom = shift_y(following[n // 2 :], -1)

    ring, give = call(
        products_kernel,
        [struct((texts, 2 * width), BF16), struct((4, rows, 3 * width), BF16)],
        [own, prev, following, top, bottom],
        6 * mac,
        [pltpu.VMEM((2 * LANES, texts), BF16)],
    )
    got = lax.all_to_all(give, quad, 0, 0)
    keep, give, tt, tt_give = call(
        quad_kernel, pair(2 * width) + pair(width), [got], 3 * part * width
    )
    tt_got = swap(tt_give, "zf")
    got = swap(give, "zf")
    some = ("xc", "z2", "z1")
    (e,) = call(
        energy_kernel,
        [struct((lax.axis_size(some), 1, LANES), F32)],
        [tt, tt_got],
        3 * rows * width,
    )
    e = lax.all_to_all(e, some, 0, 0)
    (mine,) = call(
        exchange_kernel,
        [struct((4, rows, 2 * width), BF16)],
        [keep, got],
        2 * rows * width,
        after=[e],
    )
    whole = lax.all_to_all(mine, quad, 0, 0).reshape(part, 2 * width)
    (e,) = call(energies_kernel, [struct((8, LANES), F32)], [e], e.size, after=[mine])
    e_far = swap(e, "zh")
    (blocks,) = call(
        pull_kernel,
        [struct((NY, part + TILE, n), BF16)],
        [whole, ring, e, e_far],
        4 * mac,
    )
    blocks = lax.all_to_all(blocks, "y", 0, 0)
    (out,) = call(
        functools.partial(finish_kernel, batch_texts**0.5 * total_texts, batch_texts / width),
        [struct((n, width), F32)],
        [blocks, student],
        12 * n * width,
    )
    return out


def solution(mesh):
    rows, cols = mesh.devices.shape
    fine = Mesh(mesh.devices.reshape(2, rows // 2, 2, 2, 2, cols // NZ), ALL)
    return jax.shard_map(
        on_device,
        mesh=fine,
        in_specs=(P(ALL, None), P(ALL, None)),
        out_specs=P(ALL, None),
        check_vma=False,
    )
```

time: 119 us -> 130 us (1.092)
  blocking collectives: 23.7 us -> 46.5 us
  starting transfers between devices: 55.1 us -> 39.7 us
  waiting for transfers between devices: 32 us -> 37.2 us
  Pallas kernels: 6.83 us -> 3.81 us
    all_to_all x0 -> x1, blocking collectives: none -> 25.6 us  [on_device(): got = lax.all_to_all(give, quad, 0, 0)]
    ppermute x5 -> x3, starting transfers between devices: 37.7 us -> 21.9 us  [swap(): return lax.ppermute(x, axis, [(0, 1), (1, 0)])]
    all_to_all x3 -> x0, waiting for transfers between devices: 15.1 us -> none  [the longest x2 11.2 us: gather_y(): return lax.all_to_all(copies, 'y', 0, 0).reshape(NY * n, width)]
    ppermute x0 -> x4, starting transfers between devices: none -> 14.4 us  [shift_y(): return lax.ppermute(x, 'y', [(i, (i + d) % NY) for i in range(NY)])]
    all_to_all x3 -> x0, starting transfers between devices: 14 us -> none  [the longest x2 8.09 us: gather_y(): return lax.all_to_all(copies, 'y', 0, 0).reshape(NY * n, width)]
    ppermute x0 -> x4, waiting for transfers between devices: none -> 13.3 us  [shift_y(): return lax.ppermute(x, 'y', [(i, (i + d) % NY) for i in range(NY)])]
    ppermute x5 -> x3, waiting for transfers between devices: 16.8 us -> 23.9 us  [swap(): return lax.ppermute(x, axis, [(0, 1), (1, 0)])]
    pallas_call x12 -> x8, Pallas kernels: 6.83 us -> 3.81 us  [call(): pl.pallas_call(run, out_shape=out_shape, in_specs=[whole] * count + [pl.B...]
  transfers between devices with their start and end apart: 9 -> 8, of which waited for: 6 -> 5; matrix products, arithmetic and copies ran while one was open for 0% -> 0% of each run, Pallas kernels for 1% -> 0%
where the time goes in v3:
time: 130 us; the launch traced here: 129 us
  blocking collectives  46.5 us (36%)
  starting transfers between devices  39.7 us (31%)
  waiting for transfers between devices  37.2 us (29%)
  Pallas kernels  3.81 us (3%)
  local copies, waits for them, and re-layouts  1.89 us (1%)
    all_to_all x1, blocking collectives, on_device(): got = lax.all_to_all(give, quad, 0, 0)  25.6 us
    ppermute x3, waiting for transfers between devices, swap(): return lax.ppermute(x, axis, [(0, 1), (1, 0)])  23.9 us
    ppermute x3, starting transfers between devices, swap(): return lax.ppermute(x, axis, [(0, 1), (1, 0)])  21.9 us
    ppermute x4, starting transfers between devices, shift_y(): return lax.ppermute(x, 'y', [(i, (i + d) % NY) for i in range(NY)])  14.4 us
    ppermute x4, waiting for transfers between devices, shift_y(): return lax.ppermute(x, 'y', [(i, (i + d) % NY) for i in range(NY)])  13.3 us
    all_to_all x1, blocking collectives, on_device(): e = lax.all_to_all(e, some, 0, 0)  12.1 us
    all_to_all x1, blocking collectives, on_device(): blocks = lax.all_to_all(blocks, 'y', 0, 0)  8.79 us
    pallas_call x8, Pallas kernels, call(): pl.pallas_call(run, out_shape=out_shape, in_specs=[whole] * count + [pl.B...  3.81 us
  transfers between devices with their start and end apart: 8, of which 5 were waited for; matrix products, arithmetic and copies ran while one was open for 0% of the time, Pallas kernels for 0%

profile of v3, /device:TPU:2, one launch (start us, length us, event | category | flops | bytes accessed | tf_op | source)
XLA Modules:
  0.0 129.2 jit_solution(6781344699757730184)
XLA Ops:
  0.0 0.0 copy-start
  0.0 0.9 copy-done
  0.9 0.0 copy-start.2
  0.9 0.9 copy-done.2
  1.9 0.2 shard_map.28.refs_0_
  2.0 4.9 %collective-permute-start.1 = (bf16[128,1536]{1,0:T(8,128)(2,1)S(1)}, bf16[128,1536]{1,0:T(8,128)(2,1)S(1)}, u32[]{:S(2)}, u32[]{:S(2)}) collective-permute-start(bf16[128,1536]{1,0:T(8,128)(2,1)S(1)} %shard_map.28.refs_0_), channel_id=1, source_target_pairs={{0,3},{1,0},{2,1},{3,2},{4,7},{5,4},{6,5},{7,6},{8,11},{9,8},{10,9... | collective-permute-start | bytes 1179656 | tf_op jit(solution)/shard_map/ppermute | solution.py:156
  7.0 1.9 %collective-permute-start = (bf16[128,1536]{1,0:T(8,128)(2,1)S(1)}, bf16[128,1536]{1,0:T(8,128)(2,1)S(1)}, u32[]{:S(2)}, u32[]{:S(2)}) collective-permute-start(bf16[128,1536]{1,0:T(8,128)(2,1)S(1)} %shard_map.28.refs_0_), channel_id=1, source_target_pairs={{0,1},{1,2},{2,3},{3,0},{4,5},{5,6},{6,7},{7,4},{8,9},{9,10},{10,1... | collective-permute-start | bytes 1179656 | tf_op jit(solution)/shard_map/ppermute | solution.py:156
  8.9 6.4 %collective-permute-done.1.refs_2_ = bf16[128,1536]{1,0:T(8,128)(2,1)S(1)} collective-permute-done((bf16[128,1536]{1,0:T(8,128)(2,1)S(1)}, bf16[128,1536]{1,0:T(8,128)(2,1)S(1)}, u32[]{:S(2)}, u32[]{:S(2)}) %collective-permute-start.1) | collective-permute-done | bytes 393248 | tf_op jit(solution)/shard_map/ppermute | solution.py:156
  15.3 5.6 %collective-permute-start.3 = (bf16[64,1536]{1,0:T(8,128)(2,1)S(1)}, bf16[64,1536]{1,0:T(8,128)(2,1)S(1)}, u32[]{:S(2)}, u32[]{:S(2)}) collective-permute-start(bf16[64,1536]{1,0:T(8,128)(2,1)S(1)} %slice.9), channel_id=1, source_target_pairs={{0,3},{1,0},{2,1},{3,2},{4,7},{5,4},{6,5},{7,6},{8,11},{9,8},{10,9... | collective-permute-start | bytes 589832 | tf_op jit(solution)/shard_map/ppermute | solution.py:156
  20.9 0.0 collective-permute-done.refs_1_
  21.0 1.9 %collective-permute-start.2 = (bf16[64,1536]{1,0:T(8,128)(2,1)S(1)}, bf16[64,1536]{1,0:T(8,128)(2,1)S(1)}, u32[]{:S(2)}, u32[]{:S(2)}) collective-permute-start(bf16[64,1536]{1,0:T(8,128)(2,1)S(1)} %slice.8), channel_id=1, source_target_pairs={{0,1},{1,2},{2,3},{3,0},{4,5},{5,6},{6,7},{7,4},{8,9},{9,10},{10,1... | collective-permute-start | bytes 589832 | tf_op jit(solution)/shard_map/ppermute | solution.py:156
  22.9 1.3 %collective-permute-done.3.refs_4_ = bf16[64,1536]{1,0:T(8,128)(2,1)S(1)} collective-permute-done((bf16[64,1536]{1,0:T(8,128)(2,1)S(1)}, bf16[64,1536]{1,0:T(8,128)(2,1)S(1)}, u32[]{:S(2)}, u32[]{:S(2)}) %collective-permute-start.3) | collective-permute-done | bytes 196640 | tf_op jit(solution)/shard_map/ppermute | solution.py:156
  24.2 5.5 %collective-permute-done.2.refs_3_ = bf16[64,1536]{1,0:T(8,128)(2,1)S(1)} collective-permute-done((bf16[64,1536]{1,0:T(8,128)(2,1)S(1)}, bf16[64,1536]{1,0:T(8,128)(2,1)S(1)}, u32[]{:S(2)}, u32[]{:S(2)}) %collective-permute-start.2) | collective-permute-done | bytes 196640 | tf_op jit(solution)/shard_map/ppermute | solution.py:156
  29.8 0.8 shard_map.29
  30.6 25.6 %all_to_all.20.refs_0_ = bf16[4,48,2304]{2,1,0:T(8,128)(2,1)S(1)} all-to-all(bf16[4,48,2304]{2,1,0:T(8,128)(2,1)S(1)} %get-tuple-element.11), channel_id=1, replica_groups=mesh['zh'=2,'xc'=8,'zf'=2,'z2'=2,'z1'=2,'y'=4] {'z2','z1'}, dimensions={0} | all-to-all | bytes 1769472 | tf_op jit(solution)/shard_map/all_to_all | solution.py:185
  56.2 0.1 shard_map.30
  56.3 9.1 %collective-permute-start.4 = (bf16[48,1536]{1,0:T(8,128)(2,1)S(1)}, bf16[48,1536]{1,0:T(8,128)(2,1)S(1)}, u32[]{:S(2)}, u32[]{:S(2)}) collective-permute-start(bf16[48,1536]{1,0:T(8,128)(2,1)S(1)} %get-tuple-element.13), channel_id=1, source_target_pairs={{0,16},{16,0},{1,17},{17,1},{2,18},{18,2},{3,19},{19,3},{4,20},{20... | collective-permute-start | bytes 442376 | tf_op jit(solution)/shard_map/ppermute | solution.py:152
  65.4 1.9 %collective-permute-start.5 = (bf16[48,768]{1,0:T(8,128)(2,1)S(1)}, bf16[48,768]{1,0:T(8,128)(2,1)S(1)}, u32[]{:S(2)}, u32[]{:S(2)}) collective-permute-start(bf16[48,768]{1,0:T(8,128)(2,1)S(1)} %get-tuple-element.15), channel_id=1, source_target_pairs={{0,16},{16,0},{1,17},{17,1},{2,18},{18,2},{3,19},{19,3},{4,20},{20... | collective-permute-start | bytes 221192 | tf_op jit(solution)/shard_map/ppermute | solution.py:152
  67.4 15.4 %collective-permute-done.5.refs_1_ = bf16[48,768]{1,0:T(8,128)(2,1)S(1)} collective-permute-done((bf16[48,768]{1,0:T(8,128)(2,1)S(1)}, bf16[48,768]{1,0:T(8,128)(2,1)S(1)}, u32[]{:S(2)}, u32[]{:S(2)}) %collective-permute-start.5) | collective-permute-done | bytes 73760 | tf_op jit(solution)/shard_map/ppermute | solution.py:152
  82.8 12.1 %all_to_all.21.refs_2_.refs_0_ = f32[32,1,128]{2,1,0:T(1,128)S(1)} all-to-all(f32[32,1,128]{2,1,0:T(1,128)S(1)} %shard_map.31), channel_id=1, replica_groups=mesh['zh'=2,'xc'=8,'zf'=2,'z2'=2,'z1'=2,'y'=4] {'xc','z2','z1'}, dimensions={0} | all-to-all | bytes 32768 | tf_op jit(solution)/shard_map/all_to_all | solution.py:198
  94.9 0.0 collective-permute-done.4.refs_1_
  94.9 0.9 shard_map.32.refs_1_
  95.8 3.5 %all-to-all-start.2 = ((bf16[4,48,1536]{2,1,0:T(8,128)(2,1)}), bf16[4,48,1536]{2,1,0:T(8,128)(2,1)S(1)}, u32[]{:S(2)}, u32[]{:S(2)}) async-start(bf16[4,48,1536]{2,1,0:T(8,128)(2,1)} %shard_map.32.refs_1_), calls=%async_computation.2 | async-start | bytes 1179648 | tf_op jit(solution)/shard_map/all_to_all | solution.py:206
  99.3 0.0 copy-start.1
  99.3 10.9 %collective-permute-start.6 = (f32[8,128]{1,0:T(8,128)S(1)}, f32[8,128]{1,0:T(8,128)S(1)}, u32[]{:S(2)}, u32[]{:S(2)}) collective-permute-start(f32[8,128]{1,0:T(8,128)S(1)} %shard_map.33.refs_2_), channel_id=1, source_target_pairs={{0,256},{256,0},{1,257},{257,1},{2,258},{258,2},{3,259},{259,3},{4... | collective-permute-start | bytes 12296 | tf_op jit(solution)/shard_map/ppermute | solution.py:152
  110.2 8.5 %collective-permute-done.6.refs_3_ = f32[8,128]{1,0:T(8,128)S(1)} collective-permute-done((f32[8,128]{1,0:T(8,128)S(1)}, f32[8,128]{1,0:T(8,128)S(1)}, u32[]{:S(2)}, u32[]{:S(2)}) %collective-permute-start.6) | collective-permute-done | bytes 4128 | tf_op jit(solution)/shard_map/ppermute | solution.py:152
  118.7 0.0 all-to-all-done.2
  118.7 0.7 shard_map.34
  119.3 8.8 %all_to_all.22.refs_0_ = bf16[4,208,128]{2,1,0:T(8,128)(2,1)S(1)} all-to-all(bf16[4,208,128]{2,1,0:T(8,128)(2,1)S(1)} %shard_map.34), channel_id=1, replica_groups=mesh['zh'=2,'xc'=8,'zf'=2,'z2'=2,'z1'=2,'y'=4] {'y'}, dimensions={0} | all-to-all | bytes 425984 | tf_op jit(solution)/shard_map/all_to_all | solution.py:215
  128.1 0.0 copy-done.1
  128.1 1.1 shard_map.35
  (4 shorter events, 0.1 us)
Async XLA Ops:
  0.0 0.9 copy-start
  0.9 0.9 copy-start.2
  2.0 13.3 %collective-permute-start.1 = (bf16[128,1536]{1,0:T(8,128)(2,1)S(1)}, bf16[128,1536]{1,0:T(8,128)(2,1)S(1)}, u32[]{:S(2)}, u32[]{:S(2)}) collective-permute-start(bf16[128,1536]{1,0:T(8,128)(2,1)S(1)} %shard_map.28.refs_0_), channel_id=1, source_target_pairs={{0,3},{1,0},{2,1},{3,2},{4,7},{5,4},{6,5},{7,6},{8,11},{9,8},{10,9... | collective-permute-start | bytes 1179656 | tf_op jit(solution)/shard_map/ppermute | solution.py:156
  7.0 14.0 %collective-permute-start = (bf16[128,1536]{1,0:T(8,128)(2,1)S(1)}, bf16[128,1536]{1,0:T(8,128)(2,1)S(1)}, u32[]{:S(2)}, u32[]{:S(2)}) collective-permute-start(bf16[128,1536]{1,0:T(8,128)(2,1)S(1)} %shard_map.28.refs_0_), channel_id=1, source_target_pairs={{0,1},{1,2},{2,3},{3,0},{4,5},{5,6},{6,7},{7,4},{8,9},{9,10},{10,1... | collective-permute-start | bytes 1179656 | tf_op jit(solution)/shard_map/ppermute | solution.py:156
  15.3 8.9 %collective-permute-start.3 = (bf16[64,1536]{1,0:T(8,128)(2,1)S(1)}, bf16[64,1536]{1,0:T(8,128)(2,1)S(1)}, u32[]{:S(2)}, u32[]{:S(2)}) collective-permute-start(bf16[64,1536]{1,0:T(8,128)(2,1)S(1)} %slice.9), channel_id=1, source_target_pairs={{0,3},{1,0},{2,1},{3,2},{4,7},{5,4},{6,5},{7,6},{8,11},{9,8},{10,9... | collective-permute-start | bytes 589832 | tf_op jit(solution)/shard_map/ppermute | solution.py:156
  21.0 8.8 %collective-permute-start.2 = (bf16[64,1536]{1,0:T(8,128)(2,1)S(1)}, bf16[64,1536]{1,0:T(8,128)(2,1)S(1)}, u32[]{:S(2)}, u32[]{:S(2)}) collective-permute-start(bf16[64,1536]{1,0:T(8,128)(2,1)S(1)} %slice.8), channel_id=1, source_target_pairs={{0,1},{1,2},{2,3},{3,0},{4,5},{5,6},{6,7},{7,4},{8,9},{9,10},{10,1... | collective-permute-start | bytes 589832 | tf_op jit(solution)/shard_map/ppermute | solution.py:156
  56.3 38.6 %collective-permute-start.4 = (bf16[48,1536]{1,0:T(8,128)(2,1)S(1)}, bf16[48,1536]{1,0:T(8,128)(2,1)S(1)}, u32[]{:S(2)}, u32[]{:S(2)}) collective-permute-start(bf16[48,1536]{1,0:T(8,128)(2,1)S(1)} %get-tuple-element.13), channel_id=1, source_target_pairs={{0,16},{16,0},{1,17},{17,1},{2,18},{18,2},{3,19},{19,3},{4,20},{20... | collective-permute-start | bytes 442376 | tf_op jit(solution)/shard_map/ppermute | solution.py:152
  65.4 17.4 %collective-permute-start.5 = (bf16[48,768]{1,0:T(8,128)(2,1)S(1)}, bf16[48,768]{1,0:T(8,128)(2,1)S(1)}, u32[]{:S(2)}, u32[]{:S(2)}) collective-permute-start(bf16[48,768]{1,0:T(8,128)(2,1)S(1)} %get-tuple-element.15), channel_id=1, source_target_pairs={{0,16},{16,0},{1,17},{17,1},{2,18},{18,2},{3,19},{19,3},{4,20},{20... | collective-permute-start | bytes 221192 | tf_op jit(solution)/shard_map/ppermute | solution.py:152
  95.8 22.9 %all-to-all-start.2 = ((bf16[4,48,1536]{2,1,0:T(8,128)(2,1)}), bf16[4,48,1536]{2,1,0:T(8,128)(2,1)S(1)}, u32[]{:S(2)}, u32[]{:S(2)}) async-start(bf16[4,48,1536]{2,1,0:T(8,128)(2,1)} %shard_map.32.refs_1_), calls=%async_computation.2 | async-start | bytes 1179648 | tf_op jit(solution)/shard_map/all_to_all | solution.py:206
  99.3 28.9 %copy-start.1 = (bf16[128,768]{1,0:T(8,128)(2,1)S(1)}, bf16[128,768]{1,0:T(8,128)(2,1)}, u32[]{:S(2)}) copy-start(bf16[128,768]{1,0:T(8,128)(2,1)} %refs_1_.3) | copy-start | bytes 589828
  99.3 19.3 %collective-permute-start.6 = (f32[8,128]{1,0:T(8,128)S(1)}, f32[8,128]{1,0:T(8,128)S(1)}, u32[]{:S(2)}, u32[]{:S(2)}) collective-permute-start(f32[8,128]{1,0:T(8,128)S(1)} %shard_map.33.refs_2_), channel_id=1, source_target_pairs={{0,256},{256,0},{1,257},{257,1},{2,258},{258,2},{3,259},{259,3},{4... | collective-permute-start | bytes 12296 | tf_op jit(solution)/shard_map/ppermute | solution.py:152

commit v4 on v2

--- a/solution.py
+++ b/solution.py
@@ -61,10 +61,8 @@
     return jnp.sum(parts.astype(F32), axis=0, keepdims=True)
 
 
-def units_kernel(x_ref, copies_ref):
-    unit = unit_rows(x_ref[...])[0].astype(BF16)
-    for i in range(copies_ref.shape[0]):
-        copies_ref[i] = unit
+def units_kernel(x_ref, unit_ref):
+    unit_ref[...] = jnp.broadcast_to(unit_rows(x_ref[...])[0].astype(BF16), unit_ref.shape)
 
 
 def nt(left, right):
@@ -86,9 +84,24 @@
     give_ref[...] = sums[pl.ds(pl.multiple_of((1 - here) * rows, TILE), rows)].astype(BF16)
 
 
-def teacher_kernel(ring_ref, keep_ref, give_ref, flip, sums):
-    sums[...] = jnp.dot(turned(ring_ref, flip), ring_ref[...], preferred_element_type=F32)
-    split_rows(sums, "z1", keep_ref, give_ref)
+def teacher_kernel(ring_ref, keep_ref, give_ref, flip, upper):
+    y = lax.axis_index("y")
+    count = ring_ref.shape[1] // LANES
+    for i, block in ((0, y), (1, jnp.minimum(count - y, count - 1))):
+        begin = pl.multiple_of(block * LANES, LANES)
+        flip[i * LANES : (i + 1) * LANES] = ring_ref[:, pl.ds(begin, LANES)].T
+    for k in range(count):
+        first = k < count - y
+        row_block = jnp.where(first, y, count - y)
+        col_block = jnp.where(first, y + k, k)
+        used = jnp.logical_or(first, 2 * y < count)
+        col_block = jnp.where(used, col_block, 0)
+        weight = jnp.where(used, jnp.where(row_block == col_block, 1.0, 2.0**0.5), 0.0)
+        left = flip[pl.ds(pl.multiple_of(jnp.where(first, 0, LANES), LANES), LANES)]
+        right = ring_ref[:, pl.ds(pl.multiple_of(col_block * LANES, LANES), LANES)]
+        block = jnp.dot(left, right, preferred_element_type=F32)
+        upper[k * LANES : (k + 1) * LANES] = weight * block
+    split_rows(upper, "z1", keep_ref, give_ref)
 
 
 def student_kernel(ring_s, ring_t, give_ref, flip):
@@ -96,14 +109,14 @@
     quad, rows = give_ref.shape[:2]
     part = quad * rows
     left = turned(ring_s, flip)
+    ss = jnp.dot(left, ring_s[...], preferred_element_type=F32)
     row = lax.broadcasted_iota(jnp.int32, (part, width), 0) + lax.axis_index("y") * part
     on = row == lax.broadcasted_iota(jnp.int32, (part, width), 1)
-    ss = jnp.dot(left, ring_s[...], preferred_element_type=F32)
-    ss = (ss - jnp.where(on, ring_s.shape[0] / width, 0.0)).astype(BF16)
-    st = -jnp.dot(left, ring_t[...], preferred_element_type=F32).astype(BF16)
-    for i in range(quad):
-        give_ref[i, :, :width] = ss[i * rows : (i + 1) * rows]
-        give_ref[i, :, width:] = st[i * rows : (i + 1) * rows]
+    ss = ss - jnp.where(on, ring_s.shape[0] / width, 0.0)
+    st = -jnp.dot(left, ring_t[...], preferred_element_type=F32)
+    for at, sums in ((0, ss), (width, st)):
+        for i in range(quad):
+            give_ref[i, :, at : at + width] = sums[i * rows : (i + 1) * rows].astype(BF16)
 
 
 def quad_kernel(got_ref, total_ref, send_ref):
@@ -119,9 +132,7 @@
 
 def energy_kernel(mine_ref, got_ref, e_ref):
     tt = mine_ref[...] + got_ref[...].astype(F32)
-    e = jnp.sum(tt * tt, axis=0, keepdims=True)
-    e = sum(e[:, i : i + LANES] for i in range(0, e.shape[1], LANES))
-    e_ref[...] = jnp.broadcast_to(e, e_ref.shape)
+    e_ref[...] = jnp.broadcast_to(jnp.sum(tt * tt, axis=0, keepdims=True), e_ref.shape)
 
 
 def energies_kernel(e_ref, out_ref):
@@ -192,13 +203,23 @@
     ring_s = gather_y(student)
 
     quad = ("z2", "z1")
-    tt, tt_give = call(teacher_kernel, pair(half, width), [ring_t], 2 * mac, scratch(width))
+    tt, tt_give = call(
+        teacher_kernel,
+        pair(width // 2, LANES),
+        [ring_t],
+        mac,
+        [pltpu.VMEM((2 * LANES, texts), BF16), pltpu.VMEM((width, LANES), F32)],
+    )
     tt_got = swap(tt_give, "z1")
     tt, tt_give = call(
-        halve_kernel, pair(rows, width), [tt, tt_got], part * width, [pltpu.VMEM((half, width), F32)]
+        halve_kernel,
+        pair(width // 4, LANES),
+        [tt, tt_got],
+        part * width,
+        [pltpu.VMEM((width // 2, LANES), F32)],
     )
     tt_got = swap(tt_give, "z2")
-    tt, tt_give = call(add_kernel, pair(rows, width), [tt, tt_got], rows * width)
+    tt, tt_give = call(add_kernel, pair(width // 4, LANES), [tt, tt_got], rows * width)
     tt_got = swap(tt_give, "zf")
     (give,) = call(
         student_kernel,

time: 119 us -> 116 us (0.975)
  waiting for transfers between devices: 32 us -> 30.5 us
    ppermute x5, waiting for transfers between devices: 16.8 us -> 15.6 us  [swap(): return lax.ppermute(x, axis, [(0, 1), (1, 0)])]
where the time goes in v4:
time: 116 us
  starting transfers between devices  54.4 us (47%)
  waiting for transfers between devices  30.5 us (26%)
  blocking collectives  23.1 us (20%)
  Pallas kernels  6.84 us (6%)
    ppermute x5, starting transfers between devices, swap(): return lax.ppermute(x, axis, [(0, 1), (1, 0)])  37.3 us
    ppermute x5, waiting for transfers between devices, swap(): return lax.ppermute(x, axis, [(0, 1), (1, 0)])  15.6 us
    all_to_all x1, blocking collectives, on_device(): e = lax.all_to_all(e, some, 0, 0)  12.7 us
    all_to_all x2, waiting for transfers between devices, gather_y(): return lax.all_to_all(copies, 'y', 0, 0).reshape(NY * n, width)  11.2 us
    all_to_all x1, blocking collectives, on_device(): blocks = lax.all_to_all(blocks, 'y', 0, 0)  10.4 us
    all_to_all x2, starting transfers between devices, gather_y(): return lax.all_to_all(copies, 'y', 0, 0).reshape(NY * n, width)  8.09 us
    pallas_call x12, Pallas kernels, call(): pl.pallas_call(run, out_shape=out_shape, in_specs=[whole] * count + [pl.B...  6.84 us
    all_to_all x1, starting transfers between devices, on_device(): got = lax.all_to_all(give, quad, 0, 0)  5.61 us
  transfers between devices with their start and end apart: 9, of which 6 were waited for; matrix products, arithmetic and copies ran while one was open for 0% of the time, Pallas kernels for 1%

profile of v4, /device:TPU:2, one launch (start us, length us, event | category | flops | bytes accessed | tf_op | source)
XLA Modules:
  0.0 115.9 jit_solution(18243580569606961711)
XLA Ops:
  0.0 0.0 copy-start.1
  0.0 0.9 copy-done.1
  0.9 1.1 shard_map.29
  2.0 0.0 copy-start
  2.0 4.6 %all-to-all-start.1 = ((bf16[4,128,768]{2,1,0:T(8,128)(2,1)}), bf16[4,128,768]{2,1,0:T(8,128)(2,1)S(1)}, u32[]{:S(2)}, u32[]{:S(2)}) async-start(bf16[4,128,768]{2,1,0:T(8,128)(2,1)} %shard_map.29), calls=%async_computation.1 | async-start | bytes 1572864 | tf_op jit(solution)/shard_map/all_to_all | solution.py:184
  6.6 0.0 copy-done
  6.6 1.0 shard_map.28
  7.6 11.2 %all-to-all-done.1 = bf16[4,128,768]{2,1,0:T(8,128)(2,1)S(1)} async-done(((bf16[4,128,768]{2,1,0:T(8,128)(2,1)}), bf16[4,128,768]{2,1,0:T(8,128)(2,1)S(1)}, u32[]{:S(2)}, u32[]{:S(2)}) %all-to-all-start.1) | async-done | bytes 786464 | tf_op jit(solution)/shard_map/all_to_all | solution.py:184
  18.9 3.5 %all-to-all-start = ((bf16[4,128,768]{2,1,0:T(8,128)(2,1)}), bf16[4,128,768]{2,1,0:T(8,128)(2,1)S(1)}, u32[]{:S(2)}, u32[]{:S(2)}) async-start(bf16[4,128,768]{2,1,0:T(8,128)(2,1)} %shard_map.28), calls=%async_computation | async-start | bytes 1572864 | tf_op jit(solution)/shard_map/all_to_all | solution.py:184
  22.4 0.5 shard_map.30
  22.9 3.8 %collective-permute-start = (bf16[384,128]{1,0:T(8,128)(2,1)S(1)}, bf16[384,128]{1,0:T(8,128)(2,1)S(1)}, u32[]{:S(2)}, u32[]{:S(2)}) collective-permute-start(bf16[384,128]{1,0:T(8,128)(2,1)S(1)} %get-tuple-element.14), channel_id=1, source_target_pairs={{0,4},{4,0},{1,5},{5,1},{2,6},{6,2},{3,7},{7,3},{8,12},{12,8},{9,1... | collective-permute-start | bytes 294920 | tf_op jit(solution)/shard_map/ppermute | solution.py:178
  26.7 2.7 %collective-permute-done.refs_1_ = bf16[384,128]{1,0:T(8,128)(2,1)S(1)} collective-permute-done((bf16[384,128]{1,0:T(8,128)(2,1)S(1)}, bf16[384,128]{1,0:T(8,128)(2,1)S(1)}, u32[]{:S(2)}, u32[]{:S(2)}) %collective-permute-start) | collective-permute-done | bytes 98336 | tf_op jit(solution)/shard_map/ppermute | solution.py:178
  29.4 5.2 %collective-permute-start.1 = (bf16[192,128]{1,0:T(8,128)(2,1)S(1)}, bf16[192,128]{1,0:T(8,128)(2,1)S(1)}, u32[]{:S(2)}, u32[]{:S(2)}) collective-permute-start(bf16[192,128]{1,0:T(8,128)(2,1)S(1)} %get-tuple-element.16), channel_id=1, source_target_pairs={{0,8},{8,0},{1,9},{9,1},{2,10},{10,2},{3,11},{11,3},{4,12},{12,4},... | collective-permute-start | bytes 147464 | tf_op jit(solution)/shard_map/ppermute | solution.py:178
  34.6 2.1 %collective-permute-done.1.refs_1_ = bf16[192,128]{1,0:T(8,128)(2,1)S(1)} collective-permute-done((bf16[192,128]{1,0:T(8,128)(2,1)S(1)}, bf16[192,128]{1,0:T(8,128)(2,1)S(1)}, u32[]{:S(2)}, u32[]{:S(2)}) %collective-permute-start.1) | collective-permute-done | bytes 49184 | tf_op jit(solution)/shard_map/ppermute | solution.py:178
  36.7 0.0 all-to-all-done
  36.7 1.4 %shard_map.33 = bf16[4,48,1536]{2,1,0:T(8,128)(2,1)} custom-call(bf16[512,768]{1,0:T(8,128)(2,1)S(1)} %bitcast.6, bf16[512,768]{1,0:T(8,128)(2,1)S(1)} %bitcast.4, bf16[192,128]{1,0:T(8,128)(2,1)S(1)} %get-tuple-element.17.refs_2_), custom_call_target="tpu_custom_call" | custom-call | flops 301989888 | bytes 2162688 | tf_op jit(solution)/shard_map/pallas_call | solution.py:30
  38.1 5.6 %all-to-all-start.2 = ((bf16[4,48,1536]{2,1,0:T(8,128)(2,1)}), bf16[4,48,1536]{2,1,0:T(8,128)(2,1)S(1)}, u32[]{:S(2)}, u32[]{:S(2)}) async-start(bf16[4,48,1536]{2,1,0:T(8,128)(2,1)} %shard_map.33), calls=%async_computation.2 | async-start | bytes 1179648 | tf_op jit(solution)/shard_map/all_to_all | solution.py:232
  43.7 9.1 %collective-permute-start.2 = (bf16[192,128]{1,0:T(8,128)(2,1)S(1)}, bf16[192,128]{1,0:T(8,128)(2,1)S(1)}, u32[]{:S(2)}, u32[]{:S(2)}) collective-permute-start(bf16[192,128]{1,0:T(8,128)(2,1)S(1)} %get-tuple-element.17.refs_2_), channel_id=1, source_target_pairs={{0,16},{16,0},{1,17},{17,1},{2,18},{18,2},{3,19},{19,3},{4,20},{20... | collective-permute-start | bytes 147464 | tf_op jit(solution)/shard_map/ppermute | solution.py:178
  52.8 2.2 %collective-permute-done.2.refs_1_ = bf16[192,128]{1,0:T(8,128)(2,1)S(1)} collective-permute-done((bf16[192,128]{1,0:T(8,128)(2,1)S(1)}, bf16[192,128]{1,0:T(8,128)(2,1)S(1)}, u32[]{:S(2)}, u32[]{:S(2)}) %collective-permute-start.2) | collective-permute-done | bytes 49184 | tf_op jit(solution)/shard_map/ppermute | solution.py:178
  55.0 3.6 %all-to-all-done.2.refs_0_ = bf16[4,48,1536]{2,1,0:T(8,128)(2,1)S(1)} async-done(((bf16[4,48,1536]{2,1,0:T(8,128)(2,1)}), bf16[4,48,1536]{2,1,0:T(8,128)(2,1)S(1)}, u32[]{:S(2)}, u32[]{:S(2)}) %all-to-all-start.2) | async-done | bytes 589856 | tf_op jit(solution)/shard_map/all_to_all | solution.py:232
  58.6 0.1 shard_map.34
  58.7 9.0 %collective-permute-start.3 = (bf16[48,1536]{1,0:T(8,128)(2,1)S(1)}, bf16[48,1536]{1,0:T(8,128)(2,1)S(1)}, u32[]{:S(2)}, u32[]{:S(2)}) collective-permute-start(bf16[48,1536]{1,0:T(8,128)(2,1)S(1)} %get-tuple-element.19.refs_2_), channel_id=1, source_target_pairs={{0,16},{16,0},{1,17},{17,1},{2,18},{18,2},{3,19},{19,3},{4,20},{20... | collective-permute-start | bytes 442376 | tf_op jit(solution)/shard_map/ppermute | solution.py:178
  67.8 12.7 %all_to_all.30.refs_2_.refs_0_ = f32[32,1,128]{2,1,0:T(1,128)S(1)} all-to-all(f32[32,1,128]{2,1,0:T(1,128)S(1)} %shard_map.35), channel_id=1, replica_groups=mesh['zh'=2,'xc'=8,'zf'=2,'z2'=2,'z1'=2,'y'=4] {'xc','z2','z1'}, dimensions={0} | all-to-all | bytes 32768 | tf_op jit(solution)/shard_map/all_to_all | solution.py:245
  80.5 0.0 collective-permute-done.3.refs_1_
  80.5 0.9 shard_map.36.refs_1_
  81.4 3.5 %all-to-all-start.4 = ((bf16[4,48,1536]{2,1,0:T(8,128)(2,1)}), bf16[4,48,1536]{2,1,0:T(8,128)(2,1)S(1)}, u32[]{:S(2)}, u32[]{:S(2)}) async-start(bf16[4,48,1536]{2,1,0:T(8,128)(2,1)} %shard_map.36.refs_1_), calls=%async_computation.4 | async-start | bytes 1179648 | tf_op jit(solution)/shard_map/all_to_all | solution.py:253
  84.9 10.1 %collective-permute-start.4 = (f32[8,128]{1,0:T(8,128)S(1)}, f32[8,128]{1,0:T(8,128)S(1)}, u32[]{:S(2)}, u32[]{:S(2)}) collective-permute-start(f32[8,128]{1,0:T(8,128)S(1)} %shard_map.37.refs_3_), channel_id=1, source_target_pairs={{0,256},{256,0},{1,257},{257,1},{2,258},{258,2},{3,259},{259,3},{4... | collective-permute-start | bytes 12296 | tf_op jit(solution)/shard_map/ppermute | solution.py:178
  95.0 8.7 %collective-permute-done.4.refs_4_ = f32[8,128]{1,0:T(8,128)S(1)} collective-permute-done((f32[8,128]{1,0:T(8,128)S(1)}, f32[8,128]{1,0:T(8,128)S(1)}, u32[]{:S(2)}, u32[]{:S(2)}) %collective-permute-start.4) | collective-permute-done | bytes 4128 | tf_op jit(solution)/shard_map/ppermute | solution.py:178
  103.7 0.0 all-to-all-done.4
  103.7 0.7 shard_map.38
  104.4 10.4 %all_to_all.31.refs_0_ = bf16[4,208,128]{2,1,0:T(8,128)(2,1)S(1)} all-to-all(bf16[4,208,128]{2,1,0:T(8,128)(2,1)S(1)} %shard_map.38), channel_id=1, replica_groups=mesh['zh'=2,'xc'=8,'zf'=2,'z2'=2,'z1'=2,'y'=4] {'y'}, dimensions={0} | all-to-all | bytes 425984 | tf_op jit(solution)/shard_map/all_to_all | solution.py:262
  114.8 1.1 shard_map.39
  (4 shorter events, 0.1 us)
Async XLA Ops:
  0.0 0.9 copy-start.1
  2.0 4.6 %copy-start = (bf16[128,768]{1,0:T(8,128)(2,1)S(1)}, bf16[128,768]{1,0:T(8,128)(2,1)}, u32[]{:S(2)}) copy-start(bf16[128,768]{1,0:T(8,128)(2,1)} %refs_1_.1) | copy-start | bytes 589828
  2.0 16.9 %all-to-all-start.1 = ((bf16[4,128,768]{2,1,0:T(8,128)(2,1)}), bf16[4,128,768]{2,1,0:T(8,128)(2,1)S(1)}, u32[]{:S(2)}, u32[]{:S(2)}) async-start(bf16[4,128,768]{2,1,0:T(8,128)(2,1)} %shard_map.29), calls=%async_computation.1 | async-start | bytes 1572864 | tf_op jit(solution)/shard_map/all_to_all | solution.py:184
  18.9 17.8 %all-to-all-start = ((bf16[4,128,768]{2,1,0:T(8,128)(2,1)}), bf16[4,128,768]{2,1,0:T(8,128)(2,1)S(1)}, u32[]{:S(2)}, u32[]{:S(2)}) async-start(bf16[4,128,768]{2,1,0:T(8,128)(2,1)} %shard_map.28), calls=%async_computation | async-start | bytes 1572864 | tf_op jit(solution)/shard_map/all_to_all | solution.py:184
  22.9 6.5 %collective-permute-start = (bf16[384,128]{1,0:T(8,128)(2,1)S(1)}, bf16[384,128]{1,0:T(8,128)(2,1)S(1)}, u32[]{:S(2)}, u32[]{:S(2)}) collective-permute-start(bf16[384,128]{1,0:T(8,128)(2,1)S(1)} %get-tuple-element.14), channel_id=1, source_target_pairs={{0,4},{4,0},{1,5},{5,1},{2,6},{6,2},{3,7},{7,3},{8,12},{12,8},{9,1... | collective-permute-start | bytes 294920 | tf_op jit(solution)/shard_map/ppermute | solution.py:178
  29.4 7.2 %collective-permute-start.1 = (bf16[192,128]{1,0:T(8,128)(2,1)S(1)}, bf16[192,128]{1,0:T(8,128)(2,1)S(1)}, u32[]{:S(2)}, u32[]{:S(2)}) collective-permute-start(bf16[192,128]{1,0:T(8,128)(2,1)S(1)} %get-tuple-element.16), channel_id=1, source_target_pairs={{0,8},{8,0},{1,9},{9,1},{2,10},{10,2},{3,11},{11,3},{4,12},{12,4},... | collective-permute-start | bytes 147464 | tf_op jit(solution)/shard_map/ppermute | solution.py:178
  38.1 20.5 %all-to-all-start.2 = ((bf16[4,48,1536]{2,1,0:T(8,128)(2,1)}), bf16[4,48,1536]{2,1,0:T(8,128)(2,1)S(1)}, u32[]{:S(2)}, u32[]{:S(2)}) async-start(bf16[4,48,1536]{2,1,0:T(8,128)(2,1)} %shard_map.33), calls=%async_computation.2 | async-start | bytes 1179648 | tf_op jit(solution)/shard_map/all_to_all | solution.py:232
  43.7 11.3 %collective-permute-start.2 = (bf16[192,128]{1,0:T(8,128)(2,1)S(1)}, bf16[192,128]{1,0:T(8,128)(2,1)S(1)}, u32[]{:S(2)}, u32[]{:S(2)}) collective-permute-start(bf16[192,128]{1,0:T(8,128)(2,1)S(1)} %get-tuple-element.17.refs_2_), channel_id=1, source_target_pairs={{0,16},{16,0},{1,17},{17,1},{2,18},{18,2},{3,19},{19,3},{4,20},{20... | collective-permute-start | bytes 147464 | tf_op jit(solution)/shard_map/ppermute | solution.py:178
  58.7 21.8 %collective-permute-start.3 = (bf16[48,1536]{1,0:T(8,128)(2,1)S(1)}, bf16[48,1536]{1,0:T(8,128)(2,1)S(1)}, u32[]{:S(2)}, u32[]{:S(2)}) collective-permute-start(bf16[48,1536]{1,0:T(8,128)(2,1)S(1)} %get-tuple-element.19.refs_2_), channel_id=1, source_target_pairs={{0,16},{16,0},{1,17},{17,1},{2,18},{18,2},{3,19},{19,3},{4,20},{20... | collective-permute-start | bytes 442376 | tf_op jit(solution)/shard_map/ppermute | solution.py:178
  81.4 22.4 %all-to-all-start.4 = ((bf16[4,48,1536]{2,1,0:T(8,128)(2,1)}), bf16[4,48,1536]{2,1,0:T(8,128)(2,1)S(1)}, u32[]{:S(2)}, u32[]{:S(2)}) async-start(bf16[4,48,1536]{2,1,0:T(8,128)(2,1)} %shard_map.36.refs_1_), calls=%async_computation.4 | async-start | bytes 1179648 | tf_op jit(solution)/shard_map/all_to_all | solution.py:253
  84.9 18.9 %collective-permute-start.4 = (f32[8,128]{1,0:T(8,128)S(1)}, f32[8,128]{1,0:T(8,128)S(1)}, u32[]{:S(2)}, u32[]{:S(2)}) collective-permute-start(f32[8,128]{1,0:T(8,128)S(1)} %shard_map.37.refs_3_), channel_id=1, source_target_pairs={{0,256},{256,0},{1,257},{257,1},{2,258},{258,2},{3,259},{259,3},{4... | collective-permute-start | bytes 12296 | tf_op jit(solution)/shard_map/ppermute | solution.py:178

commit v5 on v4

--- a/solution.py
+++ b/solution.py
@@ -189,15 +189,12 @@
     batch_texts = n * lax.axis_size(COL)
     total_texts = n * lax.axis_size(ALL)
     part = width // NY
-    half, rows = part // 2, part // 4
+    rows = part // 4
     texts = n * NY
     mac = texts * part * width
 
     def pair(rows, wide):
         return [struct((rows, wide), F32), struct((rows, wide), BF16)]
-
-    def scratch(wide):
-        return [pltpu.VMEM((2 * LANES, texts), BF16), pltpu.VMEM((part, wide), F32)]
 
     ring_t = gather_y(teacher)
     ring_s = gather_y(student)
@@ -220,15 +217,15 @@
     )
     tt_got = swap(tt_give, "z2")
     tt, tt_give = call(add_kernel, pair(width // 4, LANES), [tt, tt_got], rows * width)
-    tt_got = swap(tt_give, "zf")
     (give,) = call(
         student_kernel,
         [struct((4, rows, 2 * width), BF16)],
         [ring_s, ring_t],
         4 * mac,
         [pltpu.VMEM((2 * LANES, texts), BF16)],
-        after=[tt_give],
-    )
+    )
+    give = lax.optimization_barrier((give, tt_give))[0]
+    tt_got = swap(tt_give, "zf")
     got = lax.all_to_all(give, quad, 0, 0)
     keep, give = call(
         quad_kernel, pair(rows, 2 * width), [got], 4 * rows * width, after=[tt_got]

time: 116 us -> 115 us (level)
  waiting for transfers between devices: 30.5 us -> 29 us
    ppermute x5, waiting for transfers between devices: 15.6 us -> 14.2 us  [swap(): return lax.ppermute(x, axis, [(0, 1), (1, 0)])]
  transfers between devices with their start and end apart: 9 -> 9, of which waited for: 6 -> 6; matrix products, arithmetic and copies ran while one was open for 0% -> 0% of each run, Pallas kernels for 1% -> 3%
where the time goes in v5:
time: 115 us; the launch traced here: 114 us
  starting transfers between devices  54.5 us (47%)
  waiting for transfers between devices  29 us (25%)
  blocking collectives  23.1 us (20%)
  Pallas kernels  6.84 us (6%)
    ppermute x5, starting transfers between devices, swap(): return lax.ppermute(x, axis, [(0, 1), (1, 0)])  37.3 us
    ppermute x5, waiting for transfers between devices, swap(): return lax.ppermute(x, axis, [(0, 1), (1, 0)])  14.2 us
    all_to_all x1, blocking collectives, on_device(): e = lax.all_to_all(e, some, 0, 0)  12.7 us
    all_to_all x2, waiting for transfers between devices, gather_y(): return lax.all_to_all(copies, 'y', 0, 0).reshape(NY * n, width)  11.2 us
    all_to_all x1, blocking collectives, on_device(): blocks = lax.all_to_all(blocks, 'y', 0, 0)  10.4 us
    all_to_all x2, starting transfers between devices, gather_y(): return lax.all_to_all(copies, 'y', 0, 0).reshape(NY * n, width)  8.09 us
    pallas_call x12, Pallas kernels, call(): pl.pallas_call(run, out_shape=out_shape, in_specs=[whole] * count + [pl.B...  6.84 us
    all_to_all x1, starting transfers between devices, on_device(): got = lax.all_to_all(give, quad, 0, 0)  5.62 us
  transfers between devices with their start and end apart: 9, of which 6 were waited for; matrix products, arithmetic and copies ran while one was open for 0% of the time, Pallas kernels for 3%

profile of v5, /device:TPU:2, one launch (start us, length us, event | category | flops | bytes accessed | tf_op | source)
XLA Modules:
  0.0 114.5 jit_solution(5134104771976239463)
XLA Ops:
  0.0 0.0 copy-start.1
  0.0 0.9 copy-done.1
  0.9 1.1 shard_map.29
  2.0 0.0 copy-start
  2.0 4.6 %all-to-all-start.1 = ((bf16[4,128,768]{2,1,0:T(8,128)(2,1)}), bf16[4,128,768]{2,1,0:T(8,128)(2,1)S(1)}, u32[]{:S(2)}, u32[]{:S(2)}) async-start(bf16[4,128,768]{2,1,0:T(8,128)(2,1)} %shard_map.29), calls=%async_computation.1 | async-start | bytes 1572864 | tf_op jit(solution)/shard_map/all_to_all | solution.py:184
  6.6 0.0 copy-done
  6.6 1.0 shard_map.28
  7.6 11.2 %all-to-all-done.1 = bf16[4,128,768]{2,1,0:T(8,128)(2,1)S(1)} async-done(((bf16[4,128,768]{2,1,0:T(8,128)(2,1)}), bf16[4,128,768]{2,1,0:T(8,128)(2,1)S(1)}, u32[]{:S(2)}, u32[]{:S(2)}) %all-to-all-start.1) | async-done | bytes 786464 | tf_op jit(solution)/shard_map/all_to_all | solution.py:184
  18.9 3.5 %all-to-all-start = ((bf16[4,128,768]{2,1,0:T(8,128)(2,1)}), bf16[4,128,768]{2,1,0:T(8,128)(2,1)S(1)}, u32[]{:S(2)}, u32[]{:S(2)}) async-start(bf16[4,128,768]{2,1,0:T(8,128)(2,1)} %shard_map.28), calls=%async_computation | async-start | bytes 1572864 | tf_op jit(solution)/shard_map/all_to_all | solution.py:184
  22.4 0.5 shard_map.31
  22.9 3.8 %collective-permute-start = (bf16[384,128]{1,0:T(8,128)(2,1)S(1)}, bf16[384,128]{1,0:T(8,128)(2,1)S(1)}, u32[]{:S(2)}, u32[]{:S(2)}) collective-permute-start(bf16[384,128]{1,0:T(8,128)(2,1)S(1)} %get-tuple-element.15), channel_id=1, source_target_pairs={{0,4},{4,0},{1,5},{5,1},{2,6},{6,2},{3,7},{7,3},{8,12},{12,8},{9,1... | collective-permute-start | bytes 294920 | tf_op jit(solution)/shard_map/ppermute | solution.py:178
  26.7 2.7 %collective-permute-done.refs_1_ = bf16[384,128]{1,0:T(8,128)(2,1)S(1)} collective-permute-done((bf16[384,128]{1,0:T(8,128)(2,1)S(1)}, bf16[384,128]{1,0:T(8,128)(2,1)S(1)}, u32[]{:S(2)}, u32[]{:S(2)}) %collective-permute-start) | collective-permute-done | bytes 98336 | tf_op jit(solution)/shard_map/ppermute | solution.py:178
  29.4 5.2 %collective-permute-start.1 = (bf16[192,128]{1,0:T(8,128)(2,1)S(1)}, bf16[192,128]{1,0:T(8,128)(2,1)S(1)}, u32[]{:S(2)}, u32[]{:S(2)}) collective-permute-start(bf16[192,128]{1,0:T(8,128)(2,1)S(1)} %get-tuple-element.17), channel_id=1, source_target_pairs={{0,8},{8,0},{1,9},{9,1},{2,10},{10,2},{3,11},{11,3},{4,12},{12,4},... | collective-permute-start | bytes 147464 | tf_op jit(solution)/shard_map/ppermute | solution.py:178
  34.6 0.0 all-to-all-done
  34.6 1.4 %shard_map.30 = bf16[4,48,1536]{2,1,0:T(8,128)(2,1)} custom-call(bf16[512,768]{1,0:T(8,128)(2,1)S(1)} %bitcast.6, bf16[512,768]{1,0:T(8,128)(2,1)S(1)} %bitcast.4), custom_call_target="tpu_custom_call" | custom-call | flops 301989888 | bytes 2162688 | tf_op jit(solution)/shard_map/pallas_call | solution.py:30
  36.0 0.6 collective-permute-done.1.refs_1_
  36.7 5.6 %all-to-all-start.2 = ((bf16[4,48,1536]{2,1,0:T(8,128)(2,1)}), bf16[4,48,1536]{2,1,0:T(8,128)(2,1)S(1)}, u32[]{:S(2)}, u32[]{:S(2)}) async-start(bf16[4,48,1536]{2,1,0:T(8,128)(2,1)} %shard_map.30), calls=%async_computation.2 | async-start | bytes 1179648 | tf_op jit(solution)/shard_map/all_to_all | solution.py:229
  42.3 9.1 %collective-permute-start.2 = (bf16[192,128]{1,0:T(8,128)(2,1)S(1)}, bf16[192,128]{1,0:T(8,128)(2,1)S(1)}, u32[]{:S(2)}, u32[]{:S(2)}) collective-permute-start(bf16[192,128]{1,0:T(8,128)(2,1)S(1)} %get-tuple-element.18), channel_id=1, source_target_pairs={{0,16},{16,0},{1,17},{17,1},{2,18},{18,2},{3,19},{19,3},{4,20},{20... | collective-permute-start | bytes 147464 | tf_op jit(solution)/shard_map/ppermute | solution.py:178
  51.4 2.2 %collective-permute-done.2.refs_1_ = bf16[192,128]{1,0:T(8,128)(2,1)S(1)} collective-permute-done((bf16[192,128]{1,0:T(8,128)(2,1)S(1)}, bf16[192,128]{1,0:T(8,128)(2,1)S(1)}, u32[]{:S(2)}, u32[]{:S(2)}) %collective-permute-start.2) | collective-permute-done | bytes 49184 | tf_op jit(solution)/shard_map/ppermute | solution.py:178
  53.6 3.6 %all-to-all-done.2.refs_0_ = bf16[4,48,1536]{2,1,0:T(8,128)(2,1)S(1)} async-done(((bf16[4,48,1536]{2,1,0:T(8,128)(2,1)}), bf16[4,48,1536]{2,1,0:T(8,128)(2,1)S(1)}, u32[]{:S(2)}, u32[]{:S(2)}) %all-to-all-start.2) | async-done | bytes 589856 | tf_op jit(solution)/shard_map/all_to_all | solution.py:229
  57.2 0.1 shard_map.34
  57.3 9.0 %collective-permute-start.3 = (bf16[48,1536]{1,0:T(8,128)(2,1)S(1)}, bf16[48,1536]{1,0:T(8,128)(2,1)S(1)}, u32[]{:S(2)}, u32[]{:S(2)}) collective-permute-start(bf16[48,1536]{1,0:T(8,128)(2,1)S(1)} %get-tuple-element.21.refs_2_), channel_id=1, source_target_pairs={{0,16},{16,0},{1,17},{17,1},{2,18},{18,2},{3,19},{19,3},{4,20},{20... | collective-permute-start | bytes 442376 | tf_op jit(solution)/shard_map/ppermute | solution.py:178
  66.4 12.7 %all_to_all.30.refs_2_.refs_0_ = f32[32,1,128]{2,1,0:T(1,128)S(1)} all-to-all(f32[32,1,128]{2,1,0:T(1,128)S(1)} %shard_map.35), channel_id=1, replica_groups=mesh['zh'=2,'xc'=8,'zf'=2,'z2'=2,'z1'=2,'y'=4] {'xc','z2','z1'}, dimensions={0} | all-to-all | bytes 32768 | tf_op jit(solution)/shard_map/all_to_all | solution.py:242
  79.1 0.0 collective-permute-done.3.refs_1_
  79.1 0.9 shard_map.36.refs_1_
  79.9 3.5 %all-to-all-start.4 = ((bf16[4,48,1536]{2,1,0:T(8,128)(2,1)}), bf16[4,48,1536]{2,1,0:T(8,128)(2,1)S(1)}, u32[]{:S(2)}, u32[]{:S(2)}) async-start(bf16[4,48,1536]{2,1,0:T(8,128)(2,1)} %shard_map.36.refs_1_), calls=%async_computation.4 | async-start | bytes 1179648 | tf_op jit(solution)/shard_map/all_to_all | solution.py:250
  83.5 10.2 %collective-permute-start.4 = (f32[8,128]{1,0:T(8,128)S(1)}, f32[8,128]{1,0:T(8,128)S(1)}, u32[]{:S(2)}, u32[]{:S(2)}) collective-permute-start(f32[8,128]{1,0:T(8,128)S(1)} %shard_map.37.refs_3_), channel_id=1, source_target_pairs={{0,256},{256,0},{1,257},{257,1},{2,258},{258,2},{3,259},{259,3},{4... | collective-permute-start | bytes 12296 | tf_op jit(solution)/shard_map/ppermute | solution.py:178
  93.6 8.7 %collective-permute-done.4.refs_4_ = f32[8,128]{1,0:T(8,128)S(1)} collective-permute-done((f32[8,128]{1,0:T(8,128)S(1)}, f32[8,128]{1,0:T(8,128)S(1)}, u32[]{:S(2)}, u32[]{:S(2)}) %collective-permute-start.4) | collective-permute-done | bytes 4128 | tf_op jit(solution)/shard_map/ppermute | solution.py:178
  102.3 0.0 all-to-all-done.4
  102.3 0.7 shard_map.38
  103.0 10.4 %all_to_all.31.refs_0_ = bf16[4,208,128]{2,1,0:T(8,128)(2,1)S(1)} all-to-all(bf16[4,208,128]{2,1,0:T(8,128)(2,1)S(1)} %shard_map.38), channel_id=1, replica_groups=mesh['zh'=2,'xc'=8,'zf'=2,'z2'=2,'z1'=2,'y'=4] {'y'}, dimensions={0} | all-to-all | bytes 425984 | tf_op jit(solution)/shard_map/all_to_all | solution.py:259
  113.4 1.1 shard_map.39
  (4 shorter events, 0.1 us)
Async XLA Ops:
  0.0 0.9 copy-start.1
  2.0 4.6 %copy-start = (bf16[128,768]{1,0:T(8,128)(2,1)S(1)}, bf16[128,768]{1,0:T(8,128)(2,1)}, u32[]{:S(2)}) copy-start(bf16[128,768]{1,0:T(8,128)(2,1)} %refs_1_.1) | copy-start | bytes 589828
  2.0 16.9 %all-to-all-start.1 = ((bf16[4,128,768]{2,1,0:T(8,128)(2,1)}), bf16[4,128,768]{2,1,0:T(8,128)(2,1)S(1)}, u32[]{:S(2)}, u32[]{:S(2)}) async-start(bf16[4,128,768]{2,1,0:T(8,128)(2,1)} %shard_map.29), calls=%async_computation.1 | async-start | bytes 1572864 | tf_op jit(solution)/shard_map/all_to_all | solution.py:184
  18.9 15.7 %all-to-all-start = ((bf16[4,128,768]{2,1,0:T(8,128)(2,1)}), bf16[4,128,768]{2,1,0:T(8,128)(2,1)S(1)}, u32[]{:S(2)}, u32[]{:S(2)}) async-start(bf16[4,128,768]{2,1,0:T(8,128)(2,1)} %shard_map.28), calls=%async_computation | async-start | bytes 1572864 | tf_op jit(solution)/shard_map/all_to_all | solution.py:184
  22.9 6.5 %collective-permute-start = (bf16[384,128]{1,0:T(8,128)(2,1)S(1)}, bf16[384,128]{1,0:T(8,128)(2,1)S(1)}, u32[]{:S(2)}, u32[]{:S(2)}) collective-permute-start(bf16[384,128]{1,0:T(8,128)(2,1)S(1)} %get-tuple-element.15), channel_id=1, source_target_pairs={{0,4},{4,0},{1,5},{5,1},{2,6},{6,2},{3,7},{7,3},{8,12},{12,8},{9,1... | collective-permute-start | bytes 294920 | tf_op jit(solution)/shard_map/ppermute | solution.py:178
  29.4 7.2 %collective-permute-start.1 = (bf16[192,128]{1,0:T(8,128)(2,1)S(1)}, bf16[192,128]{1,0:T(8,128)(2,1)S(1)}, u32[]{:S(2)}, u32[]{:S(2)}) collective-permute-start(bf16[192,128]{1,0:T(8,128)(2,1)S(1)} %get-tuple-element.17), channel_id=1, source_target_pairs={{0,8},{8,0},{1,9},{9,1},{2,10},{10,2},{3,11},{11,3},{4,12},{12,4},... | collective-permute-start | bytes 147464 | tf_op jit(solution)/shard_map/ppermute | solution.py:178
  36.7 20.5 %all-to-all-start.2 = ((bf16[4,48,1536]{2,1,0:T(8,128)(2,1)}), bf16[4,48,1536]{2,1,0:T(8,128)(2,1)S(1)}, u32[]{:S(2)}, u32[]{:S(2)}) async-start(bf16[4,48,1536]{2,1,0:T(8,128)(2,1)} %shard_map.30), calls=%async_computation.2 | async-start | bytes 1179648 | tf_op jit(solution)/shard_map/all_to_all | solution.py:229
  42.3 11.3 %collective-permute-start.2 = (bf16[192,128]{1,0:T(8,128)(2,1)S(1)}, bf16[192,128]{1,0:T(8,128)(2,1)S(1)}, u32[]{:S(2)}, u32[]{:S(2)}) collective-permute-start(bf16[192,128]{1,0:T(8,128)(2,1)S(1)} %get-tuple-element.18), channel_id=1, source_target_pairs={{0,16},{16,0},{1,17},{17,1},{2,18},{18,2},{3,19},{19,3},{4,20},{20... | collective-permute-start | bytes 147464 | tf_op jit(solution)/shard_map/ppermute | solution.py:178
  57.3 21.8 %collective-permute-start.3 = (bf16[48,1536]{1,0:T(8,128)(2,1)S(1)}, bf16[48,1536]{1,0:T(8,128)(2,1)S(1)}, u32[]{:S(2)}, u32[]{:S(2)}) collective-permute-start(bf16[48,1536]{1,0:T(8,128)(2,1)S(1)} %get-tuple-element.21.refs_2_), channel_id=1, source_target_pairs={{0,16},{16,0},{1,17},{17,1},{2,18},{18,2},{3,19},{19,3},{4,20},{20... | collective-permute-start | bytes 442376 | tf_op jit(solution)/shard_map/ppermute | solution.py:178
  79.9 22.4 %all-to-all-start.4 = ((bf16[4,48,1536]{2,1,0:T(8,128)(2,1)}), bf16[4,48,1536]{2,1,0:T(8,128)(2,1)S(1)}, u32[]{:S(2)}, u32[]{:S(2)}) async-start(bf16[4,48,1536]{2,1,0:T(8,128)(2,1)} %shard_map.36.refs_1_), calls=%async_computation.4 | async-start | bytes 1179648 | tf_op jit(solution)/shard_map/all_to_all | solution.py:250
  83.5 18.9 %collective-permute-start.4 = (f32[8,128]{1,0:T(8,128)S(1)}, f32[8,128]{1,0:T(8,128)S(1)}, u32[]{:S(2)}, u32[]{:S(2)}) collective-permute-start(f32[8,128]{1,0:T(8,128)S(1)} %shard_map.37.refs_3_), channel_id=1, source_target_pairs={{0,256},{256,0},{1,257},{257,1},{2,258},{258,2},{3,259},{259,3},{4... | collective-permute-start | bytes 12296 | tf_op jit(solution)/shard_map/ppermute | solution.py:178

commit v6 on v5

--- a/solution.py
+++ b/solution.py
@@ -77,14 +77,7 @@
     return flip[pl.ds(rest, part)]
 
 
-def split_rows(sums, axis, keep_ref, give_ref):
-    rows = keep_ref.shape[0]
-    here = lax.axis_index(axis)
-    keep_ref[...] = sums[pl.ds(pl.multiple_of(here * rows, TILE), rows)]
-    give_ref[...] = sums[pl.ds(pl.multiple_of((1 - here) * rows, TILE), rows)].astype(BF16)
-
-
-def teacher_kernel(ring_ref, keep_ref, give_ref, flip, upper):
+def teacher_kernel(ring_ref, keep_ref, give1_ref, give2_ref, give3_ref, flip, upper):
     y = lax.axis_index("y")
     count = ring_ref.shape[1] // LANES
     for i, block in ((0, y), (1, jnp.minimum(count - y, count - 1))):
@@ -101,7 +94,11 @@
         right = ring_ref[:, pl.ds(pl.multiple_of(col_block * LANES, LANES), LANES)]
         block = jnp.dot(left, right, preferred_element_type=F32)
         upper[k * LANES : (k + 1) * LANES] = weight * block
-    split_rows(upper, "z1", keep_ref, give_ref)
+    z1, z2 = lax.axis_index("z1"), lax.axis_index("z2")
+    rows = keep_ref.shape[0]
+    for m, ref in enumerate((keep_ref, give1_ref, give2_ref, give3_ref)):
+        piece = 2 * (1 - z2 if m & 2 else z2) + (1 - z1 if m & 1 else z1)
+        ref[...] = upper[pl.ds(pl.multiple_of(piece * rows, TILE), rows)].astype(ref.dtype)
 
 
 def student_kernel(ring_s, ring_t, give_ref, flip):
@@ -125,11 +122,6 @@
     send_ref[...] = total.astype(BF16)
 
 
-def halve_kernel(mine_ref, got_ref, keep_ref, give_ref, sums):
-    sums[...] = mine_ref[...] + got_ref[...].astype(F32)
-    split_rows(sums, "z2", keep_ref, give_ref)
-
-
 def energy_kernel(mine_ref, got_ref, e_ref):
     tt = mine_ref[...] + got_ref[...].astype(F32)
     e_ref[...] = jnp.broadcast_to(jnp.sum(tt * tt, axis=0, keepdims=True), e_ref.shape)
@@ -139,8 +131,10 @@
     out_ref[...] = jnp.broadcast_to(jnp.sum(e_ref[...], axis=0), out_ref.shape)
 
 
-def add_kernel(mine_ref, got_ref, total_ref, send_ref):
-    total = mine_ref[...] + got_ref[...].astype(F32)
+def add_kernel(mine_ref, got1_ref, got2_ref, got3_ref, total_ref, send_ref):
+    total = mine_ref[...]
+    for ref in (got1_ref, got2_ref, got3_ref):
+        total = total + ref[...].astype(F32)
     total_ref[...] = total
     send_ref[...] = total.astype(BF16)
 
@@ -180,7 +174,18 @@
 
 def gather_y(x):
     n, width = x.shape
-    (copies,) = call(units_kernel, [struct((NY, n, width), BF16)], [x], 5 * n * width)
+    block = n // 2
+    copies = pl.pallas_call(
+        units_kernel,
+        out_shape=struct((NY, n, width), BF16),
+        grid=(n // block,),
+        in_specs=[pl.BlockSpec((block, width), lambda i: (i, 0))],
+        out_specs=pl.BlockSpec((NY, block, width), lambda i: (0, i, 0)),
+        compiler_params=pltpu.CompilerParams(vmem_limit_bytes=VMEM_LIMIT),
+        cost_estimate=pl.CostEstimate(
+            flops=5 * n * width, bytes_accessed=10 * n * width, transcendentals=0
+        ),
+    )(x)
     return lax.all_to_all(copies, "y", 0, 0).reshape(NY * n, width)
 
 
@@ -200,23 +205,18 @@
     ring_s = gather_y(student)
 
     quad = ("z2", "z1")
-    tt, tt_give = call(
+    piece = width // 4
+    tt, *tt_give = call(
         teacher_kernel,
-        pair(width // 2, LANES),
+        [struct((piece, LANES), F32)] + [struct((piece, LANES), BF16)] * 3,
         [ring_t],
         mac,
         [pltpu.VMEM((2 * LANES, texts), BF16), pltpu.VMEM((width, LANES), F32)],
     )
-    tt_got = swap(tt_give, "z1")
-    tt, tt_give = call(
-        halve_kernel,
-        pair(width // 4, LANES),
-        [tt, tt_got],
-        part * width,
-        [pltpu.VMEM((width // 2, LANES), F32)],
-    )
-    tt_got = swap(tt_give, "z2")
-    tt, tt_give = call(add_kernel, pair(width // 4, LANES), [tt, tt_got], rows * width)
+    tt_got = [
+        lax.ppermute(x, quad, [(i, i ^ m) for i in range(4)]) for m, x in zip((1, 2, 3), tt_give)
+    ]
+    tt, tt_give = call(add_kernel, pair(piece, LANES), [tt, *tt_got], 3 * piece * LANES)
     (give,) = call(
         student_kernel,
         [struct((4, rows, 2 * width), BF16)],

time: 115 us -> 116 us (level)
  waiting for transfers between devices: 29 us -> 30.3 us
    ppermute x0 -> x3, starting transfers between devices: none -> 10.9 us  [on_device(): lax.ppermute(x, quad, [(i, i ^ m) for i in range(4)])]
    ppermute x5 -> x3, starting transfers between devices: 37.3 us -> 27.9 us  [swap(): return lax.ppermute(x, axis, [(0, 1), (1, 0)])]
    ppermute x0 -> x3, waiting for transfers between devices: none -> 4.43 us  [on_device(): lax.ppermute(x, quad, [(i, i ^ m) for i in range(4)])]
    ppermute x5 -> x3, waiting for transfers between devices: 14.2 us -> 10.8 us  [swap(): return lax.ppermute(x, axis, [(0, 1), (1, 0)])]
    pallas_call x12 -> x9, Pallas kernels: 6.84 us -> 4.68 us  [call(): pl.pallas_call(run, out_shape=out_shape, in_specs=[whole] * count + [pl.B...]
    all_to_all x1, starting transfers between devices: 5.62 us -> 3.49 us  [on_device(): got = lax.all_to_all(give, quad, 0, 0)]
    pallas_call x0 -> x2, Pallas kernels: none -> 2.05 us  [gather_y(): pl.pallas_call(units_kernel, out_shape=struct((NY, n, width), BF16), grid...]
  transfers between devices with their start and end apart: 9 -> 10, of which waited for: 6 -> 5; matrix products, arithmetic and copies ran while one was open for 0% -> 0% of each run, Pallas kernels for 3% -> 3%
where the time goes in v6:
time: 116 us; the launch traced here: 115 us
  starting transfers between devices  53.9 us (46%)
  waiting for transfers between devices  30.3 us (26%)
  blocking collectives  23.4 us (20%)
  Pallas kernels  6.73 us (6%)
    ppermute x3, starting transfers between devices, swap(): return lax.ppermute(x, axis, [(0, 1), (1, 0)])  27.9 us
    all_to_all x1, blocking collectives, on_device(): e = lax.all_to_all(e, some, 0, 0)  12.7 us
    all_to_all x2, waiting for transfers between devices, gather_y(): return lax.all_to_all(copies, 'y', 0, 0).reshape(NY * n, width)  11.3 us
    ppermute x3, starting transfers between devices, on_device(): lax.ppermute(x, quad, [(i, i ^ m) for i in range(4)])  10.9 us
    ppermute x3, waiting for transfers between devices, swap(): return lax.ppermute(x, axis, [(0, 1), (1, 0)])  10.8 us
    all_to_all x1, blocking collectives, on_device(): blocks = lax.all_to_all(blocks, 'y', 0, 0)  10.7 us
    all_to_all x2, starting transfers between devices, gather_y(): return lax.all_to_all(copies, 'y', 0, 0).reshape(NY * n, width)  8.09 us
    pallas_call x9, Pallas kernels, call(): pl.pallas_call(run, out_shape=out_shape, in_specs=[whole] * count + [pl.B...  4.68 us
  transfers between devices with their start and end apart: 10, of which 5 were waited for; matrix products, arithmetic and copies ran while one was open for 0% of the time, Pallas kernels for 3%

profile of v6, /device:TPU:2, one launch (start us, length us, event | category | flops | bytes accessed | tf_op | source)
XLA Modules:
  0.0 115.4 jit_solution(8558913364623342773)
XLA Ops:
  0.0 0.0 copy-start.1
  0.0 0.9 copy-done.1
  0.9 1.0 shard_map.29
  2.0 0.0 copy-start
  2.0 4.6 %all-to-all-start.1 = ((bf16[4,128,768]{2,1,0:T(8,128)(2,1)}), bf16[4,128,768]{2,1,0:T(8,128)(2,1)S(1)}, u32[]{:S(2)}, u32[]{:S(2)}) async-start(bf16[4,128,768]{2,1,0:T(8,128)(2,1)} %shard_map.29), calls=%async_computation.1 | async-start | bytes 1572864 | tf_op jit(solution)/shard_map/all_to_all | solution.py:189
  6.6 0.0 copy-done
  6.6 1.0 shard_map.28
  7.6 11.3 %all-to-all-done.1 = bf16[4,128,768]{2,1,0:T(8,128)(2,1)S(1)} async-done(((bf16[4,128,768]{2,1,0:T(8,128)(2,1)}), bf16[4,128,768]{2,1,0:T(8,128)(2,1)S(1)}, u32[]{:S(2)}, u32[]{:S(2)}) %all-to-all-start.1) | async-done | bytes 786464 | tf_op jit(solution)/shard_map/all_to_all | solution.py:189
  18.8 3.5 %all-to-all-start = ((bf16[4,128,768]{2,1,0:T(8,128)(2,1)}), bf16[4,128,768]{2,1,0:T(8,128)(2,1)S(1)}, u32[]{:S(2)}, u32[]{:S(2)}) async-start(bf16[4,128,768]{2,1,0:T(8,128)(2,1)} %shard_map.28), calls=%async_computation | async-start | bytes 1572864 | tf_op jit(solution)/shard_map/all_to_all | solution.py:189
  22.3 0.5 shard_map.31
  22.8 3.8 %collective-permute-start = (bf16[192,128]{1,0:T(8,128)(2,1)S(1)}, bf16[192,128]{1,0:T(8,128)(2,1)S(1)}, u32[]{:S(2)}, u32[]{:S(2)}) collective-permute-start(bf16[192,128]{1,0:T(8,128)(2,1)S(1)} %get-tuple-element.15), channel_id=1, source_target_pairs={{0,4},{4,0},{8,12},{12,8},{1,5},{5,1},{9,13},{13,9},{2,6},{6,2},{1... | collective-permute-start | bytes 147464 | tf_op jit(solution)/shard_map/ppermute | solution.py:217
  26.7 5.2 %collective-permute-start.1 = (bf16[192,128]{1,0:T(8,128)(2,1)S(1)}, bf16[192,128]{1,0:T(8,128)(2,1)S(1)}, u32[]{:S(2)}, u32[]{:S(2)}) collective-permute-start(bf16[192,128]{1,0:T(8,128)(2,1)S(1)} %get-tuple-element.16), channel_id=1, source_target_pairs={{0,8},{4,12},{8,0},{12,4},{1,9},{5,13},{9,1},{13,5},{2,10},{6,14},... | collective-permute-start | bytes 147464 | tf_op jit(solution)/shard_map/ppermute | solution.py:217
  31.9 1.9 %collective-permute-start.2 = (bf16[192,128]{1,0:T(8,128)(2,1)S(1)}, bf16[192,128]{1,0:T(8,128)(2,1)S(1)}, u32[]{:S(2)}, u32[]{:S(2)}) collective-permute-start(bf16[192,128]{1,0:T(8,128)(2,1)S(1)} %get-tuple-element.17), channel_id=1, source_target_pairs={{0,12},{4,8},{8,4},{12,0},{1,13},{5,9},{9,5},{13,1},{2,14},{6,10},... | collective-permute-start | bytes 147464 | tf_op jit(solution)/shard_map/ppermute | solution.py:217
  33.8 0.0 all-to-all-done
  33.8 1.4 %shard_map.30 = bf16[4,48,1536]{2,1,0:T(8,128)(2,1)} custom-call(bf16[512,768]{1,0:T(8,128)(2,1)S(1)} %bitcast.6, bf16[512,768]{1,0:T(8,128)(2,1)S(1)} %bitcast.4), custom_call_target="tpu_custom_call" | custom-call | flops 301989888 | bytes 2162688 | tf_op jit(solution)/shard_map/pallas_call | solution.py:30
  35.2 0.0 collective-permute-done.refs_1_
  35.2 0.0 collective-permute-done.1.refs_2_
  35.2 4.4 %collective-permute-done.2.refs_3_ = bf16[192,128]{1,0:T(8,128)(2,1)S(1)} collective-permute-done((bf16[192,128]{1,0:T(8,128)(2,1)S(1)}, bf16[192,128]{1,0:T(8,128)(2,1)S(1)}, u32[]{:S(2)}, u32[]{:S(2)}) %collective-permute-start.2) | collective-permute-done | bytes 49184 | tf_op jit(solution)/shard_map/ppermute | solution.py:217
  39.7 3.5 %all-to-all-start.2 = ((bf16[4,48,1536]{2,1,0:T(8,128)(2,1)}), bf16[4,48,1536]{2,1,0:T(8,128)(2,1)S(1)}, u32[]{:S(2)}, u32[]{:S(2)}) async-start(bf16[4,48,1536]{2,1,0:T(8,128)(2,1)} %shard_map.30), calls=%async_computation.2 | async-start | bytes 1179648 | tf_op jit(solution)/shard_map/all_to_all | solution.py:229
  43.2 9.1 %collective-permute-start.3 = (bf16[192,128]{1,0:T(8,128)(2,1)S(1)}, bf16[192,128]{1,0:T(8,128)(2,1)S(1)}, u32[]{:S(2)}, u32[]{:S(2)}) collective-permute-start(bf16[192,128]{1,0:T(8,128)(2,1)S(1)} %get-tuple-element.18), channel_id=1, source_target_pairs={{0,16},{16,0},{1,17},{17,1},{2,18},{18,2},{3,19},{19,3},{4,20},{20... | collective-permute-start | bytes 147464 | tf_op jit(solution)/shard_map/ppermute | solution.py:172
  52.3 2.1 %collective-permute-done.3.refs_1_ = bf16[192,128]{1,0:T(8,128)(2,1)S(1)} collective-permute-done((bf16[192,128]{1,0:T(8,128)(2,1)S(1)}, bf16[192,128]{1,0:T(8,128)(2,1)S(1)}, u32[]{:S(2)}, u32[]{:S(2)}) %collective-permute-start.3) | collective-permute-done | bytes 49184 | tf_op jit(solution)/shard_map/ppermute | solution.py:172
  54.4 3.8 %all-to-all-done.2.refs_0_ = bf16[4,48,1536]{2,1,0:T(8,128)(2,1)S(1)} async-done(((bf16[4,48,1536]{2,1,0:T(8,128)(2,1)}), bf16[4,48,1536]{2,1,0:T(8,128)(2,1)S(1)}, u32[]{:S(2)}, u32[]{:S(2)}) %all-to-all-start.2) | async-done | bytes 589856 | tf_op jit(solution)/shard_map/all_to_all | solution.py:229
  58.2 0.1 shard_map.33
  58.3 9.0 %collective-permute-start.4 = (bf16[48,1536]{1,0:T(8,128)(2,1)S(1)}, bf16[48,1536]{1,0:T(8,128)(2,1)S(1)}, u32[]{:S(2)}, u32[]{:S(2)}) collective-permute-start(bf16[48,1536]{1,0:T(8,128)(2,1)S(1)} %get-tuple-element.21.refs_2_), channel_id=1, source_target_pairs={{0,16},{16,0},{1,17},{17,1},{2,18},{18,2},{3,19},{19,3},{4,20},{20... | collective-permute-start | bytes 442376 | tf_op jit(solution)/shard_map/ppermute | solution.py:172
  67.3 12.7 %all_to_all.30.refs_2_.refs_0_ = f32[32,1,128]{2,1,0:T(1,128)S(1)} all-to-all(f32[32,1,128]{2,1,0:T(1,128)S(1)} %shard_map.34), channel_id=1, replica_groups=mesh['zh'=2,'xc'=8,'zf'=2,'z2'=2,'z1'=2,'y'=4] {'xc','z2','z1'}, dimensions={0} | all-to-all | bytes 32768 | tf_op jit(solution)/shard_map/all_to_all | solution.py:242
  80.0 0.0 collective-permute-done.4.refs_1_
  80.0 0.9 shard_map.35.refs_1_
  80.9 3.5 %all-to-all-start.4 = ((bf16[4,48,1536]{2,1,0:T(8,128)(2,1)}), bf16[4,48,1536]{2,1,0:T(8,128)(2,1)S(1)}, u32[]{:S(2)}, u32[]{:S(2)}) async-start(bf16[4,48,1536]{2,1,0:T(8,128)(2,1)} %shard_map.35.refs_1_), calls=%async_computation.4 | async-start | bytes 1179648 | tf_op jit(solution)/shard_map/all_to_all | solution.py:250
  84.4 9.9 %collective-permute-start.5 = (f32[8,128]{1,0:T(8,128)S(1)}, f32[8,128]{1,0:T(8,128)S(1)}, u32[]{:S(2)}, u32[]{:S(2)}) collective-permute-start(f32[8,128]{1,0:T(8,128)S(1)} %shard_map.36.refs_3_), channel_id=1, source_target_pairs={{0,256},{256,0},{1,257},{257,1},{2,258},{258,2},{3,259},{259,3},{4... | collective-permute-start | bytes 12296 | tf_op jit(solution)/shard_map/ppermute | solution.py:172
  94.3 8.7 %collective-permute-done.5.refs_4_ = f32[8,128]{1,0:T(8,128)S(1)} collective-permute-done((f32[8,128]{1,0:T(8,128)S(1)}, f32[8,128]{1,0:T(8,128)S(1)}, u32[]{:S(2)}, u32[]{:S(2)}) %collective-permute-start.5) | collective-permute-done | bytes 4128 | tf_op jit(solution)/shard_map/ppermute | solution.py:172
  102.9 0.0 all-to-all-done.4
  102.9 0.7 shard_map.37
  103.6 10.7 %all_to_all.31.refs_0_ = bf16[4,208,128]{2,1,0:T(8,128)(2,1)S(1)} all-to-all(bf16[4,208,128]{2,1,0:T(8,128)(2,1)S(1)} %shard_map.37), channel_id=1, replica_groups=mesh['zh'=2,'xc'=8,'zf'=2,'z2'=2,'z1'=2,'y'=4] {'y'}, dimensions={0} | all-to-all | bytes 425984 | tf_op jit(solution)/shard_map/all_to_all | solution.py:259
  114.3 1.1 shard_map.38
  (3 shorter events, 0.1 us)
Async XLA Ops:
  0.0 0.9 copy-start.1
  2.0 4.6 %copy-start = (bf16[128,768]{1,0:T(8,128)(2,1)S(1)}, bf16[128,768]{1,0:T(8,128)(2,1)}, u32[]{:S(2)}) copy-start(bf16[128,768]{1,0:T(8,128)(2,1)} %refs_1_.1) | copy-start | bytes 589828
  2.0 16.9 %all-to-all-start.1 = ((bf16[4,128,768]{2,1,0:T(8,128)(2,1)}), bf16[4,128,768]{2,1,0:T(8,128)(2,1)S(1)}, u32[]{:S(2)}, u32[]{:S(2)}) async-start(bf16[4,128,768]{2,1,0:T(8,128)(2,1)} %shard_map.29), calls=%async_computation.1 | async-start | bytes 1572864 | tf_op jit(solution)/shard_map/all_to_all | solution.py:189
  18.8 14.9 %all-to-all-start = ((bf16[4,128,768]{2,1,0:T(8,128)(2,1)}), bf16[4,128,768]{2,1,0:T(8,128)(2,1)S(1)}, u32[]{:S(2)}, u32[]{:S(2)}) async-start(bf16[4,128,768]{2,1,0:T(8,128)(2,1)} %shard_map.28), calls=%async_computation | async-start | bytes 1572864 | tf_op jit(solution)/shard_map/all_to_all | solution.py:189
  22.8 12.4 %collective-permute-start = (bf16[192,128]{1,0:T(8,128)(2,1)S(1)}, bf16[192,128]{1,0:T(8,128)(2,1)S(1)}, u32[]{:S(2)}, u32[]{:S(2)}) collective-permute-start(bf16[192,128]{1,0:T(8,128)(2,1)S(1)} %get-tuple-element.15), channel_id=1, source_target_pairs={{0,4},{4,0},{8,12},{12,8},{1,5},{5,1},{9,13},{13,9},{2,6},{6,2},{1... | collective-permute-start | bytes 147464 | tf_op jit(solution)/shard_map/ppermute | solution.py:217
  26.7 8.5 %collective-permute-start.1 = (bf16[192,128]{1,0:T(8,128)(2,1)S(1)}, bf16[192,128]{1,0:T(8,128)(2,1)S(1)}, u32[]{:S(2)}, u32[]{:S(2)}) collective-permute-start(bf16[192,128]{1,0:T(8,128)(2,1)S(1)} %get-tuple-element.16), channel_id=1, source_target_pairs={{0,8},{4,12},{8,0},{12,4},{1,9},{5,13},{9,1},{13,5},{2,10},{6,14},... | collective-permute-start | bytes 147464 | tf_op jit(solution)/shard_map/ppermute | solution.py:217
  31.9 7.8 %collective-permute-start.2 = (bf16[192,128]{1,0:T(8,128)(2,1)S(1)}, bf16[192,128]{1,0:T(8,128)(2,1)S(1)}, u32[]{:S(2)}, u32[]{:S(2)}) collective-permute-start(bf16[192,128]{1,0:T(8,128)(2,1)S(1)} %get-tuple-element.17), channel_id=1, source_target_pairs={{0,12},{4,8},{8,4},{12,0},{1,13},{5,9},{9,5},{13,1},{2,14},{6,10},... | collective-permute-start | bytes 147464 | tf_op jit(solution)/shard_map/ppermute | solution.py:217
  39.7 18.5 %all-to-all-start.2 = ((bf16[4,48,1536]{2,1,0:T(8,128)(2,1)}), bf16[4,48,1536]{2,1,0:T(8,128)(2,1)S(1)}, u32[]{:S(2)}, u32[]{:S(2)}) async-start(bf16[4,48,1536]{2,1,0:T(8,128)(2,1)} %shard_map.30), calls=%async_computation.2 | async-start | bytes 1179648 | tf_op jit(solution)/shard_map/all_to_all | solution.py:229
  43.2 11.2 %collective-permute-start.3 = (bf16[192,128]{1,0:T(8,128)(2,1)S(1)}, bf16[192,128]{1,0:T(8,128)(2,1)S(1)}, u32[]{:S(2)}, u32[]{:S(2)}) collective-permute-start(bf16[192,128]{1,0:T(8,128)(2,1)S(1)} %get-tuple-element.18), channel_id=1, source_target_pairs={{0,16},{16,0},{1,17},{17,1},{2,18},{18,2},{3,19},{19,3},{4,20},{20... | collective-permute-start | bytes 147464 | tf_op jit(solution)/shard_map/ppermute | solution.py:172
  58.3 21.7 %collective-permute-start.4 = (bf16[48,1536]{1,0:T(8,128)(2,1)S(1)}, bf16[48,1536]{1,0:T(8,128)(2,1)S(1)}, u32[]{:S(2)}, u32[]{:S(2)}) collective-permute-start(bf16[48,1536]{1,0:T(8,128)(2,1)S(1)} %get-tuple-element.21.refs_2_), channel_id=1, source_target_pairs={{0,16},{16,0},{1,17},{17,1},{2,18},{18,2},{3,19},{19,3},{4,20},{20... | collective-permute-start | bytes 442376 | tf_op jit(solution)/shard_map/ppermute | solution.py:172
  80.9 22.1 %all-to-all-start.4 = ((bf16[4,48,1536]{2,1,0:T(8,128)(2,1)}), bf16[4,48,1536]{2,1,0:T(8,128)(2,1)S(1)}, u32[]{:S(2)}, u32[]{:S(2)}) async-start(bf16[4,48,1536]{2,1,0:T(8,128)(2,1)} %shard_map.35.refs_1_), calls=%async_computation.4 | async-start | bytes 1179648 | tf_op jit(solution)/shard_map/all_to_all | solution.py:250
  84.4 18.6 %collective-permute-start.5 = (f32[8,128]{1,0:T(8,128)S(1)}, f32[8,128]{1,0:T(8,128)S(1)}, u32[]{:S(2)}, u32[]{:S(2)}) collective-permute-start(f32[8,128]{1,0:T(8,128)S(1)} %shard_map.36.refs_3_), channel_id=1, source_target_pairs={{0,256},{256,0},{1,257},{257,1},{2,258},{258,2},{3,259},{259,3},{4... | collective-permute-start | bytes 12296 | tf_op jit(solution)/shard_map/ppermute | solution.py:172

commit v7 on v5

--- a/solution.py
+++ b/solution.py
@@ -61,8 +61,20 @@
     return jnp.sum(parts.astype(F32), axis=0, keepdims=True)
 
 
-def units_kernel(x_ref, unit_ref):
-    unit_ref[...] = jnp.broadcast_to(unit_rows(x_ref[...])[0].astype(BF16), unit_ref.shape)
+def send_copies(src, out_ref, sems):
+    copies = [pltpu.make_async_copy(src, out_ref.at[i], sems.at[i]) for i in range(out_ref.shape[0])]
+    for copy in copies:
+        copy.start()
+    for copy in copies:
+        copy.wait()
+
+
+def units_kernel(x_ref, out_ref, x_here, unit, in_sem, out_sems):
+    load = pltpu.make_async_copy(x_ref, x_here, in_sem)
+    load.start()
+    load.wait()
+    unit[...] = unit_rows(x_here[...])[0].astype(BF16)
+    send_copies(unit, out_ref, out_sems)
 
 
 def nt(left, right):
@@ -145,10 +157,9 @@
     send_ref[...] = total.astype(BF16)
 
 
-def exchange_kernel(mine_ref, got_ref, out_ref):
-    out_ref[...] = jnp.broadcast_to(
-        (mine_ref[...] + got_ref[...].astype(F32)).astype(BF16), out_ref.shape
-    )
+def exchange_kernel(mine_ref, got_ref, e_ref, out_ref, total, sems):
+    total[...] = (mine_ref[...] + got_ref[...].astype(F32)).astype(BF16)
+    send_copies(total, out_ref, sems)
 
 
 def pull_kernel(whole, ring_s, ring_t, e_ref, f_ref, out_ref):
@@ -180,7 +191,22 @@
 
 def gather_y(x):
     n, width = x.shape
-    (copies,) = call(units_kernel, [struct((NY, n, width), BF16)], [x], 5 * n * width)
+    copies = pl.pallas_call(
+        units_kernel,
+        out_shape=struct((NY, n, width), BF16),
+        in_specs=[pl.BlockSpec(memory_space=pl.ANY)],
+        out_specs=pl.BlockSpec(memory_space=pl.ANY),
+        scratch_shapes=[
+            pltpu.VMEM((n, width), BF16),
+            pltpu.VMEM((n, width), BF16),
+            pltpu.SemaphoreType.DMA,
+            pltpu.SemaphoreType.DMA((NY,)),
+        ],
+        compiler_params=pltpu.CompilerParams(vmem_limit_bytes=VMEM_LIMIT),
+        cost_estimate=pl.CostEstimate(
+            flops=5 * n * width, bytes_accessed=10 * n * width, transcendentals=0
+        ),
+    )(x)
     return lax.all_to_all(copies, "y", 0, 0).reshape(NY * n, width)
 
 
@@ -240,13 +266,18 @@
         after=[give],
     )
     e = lax.all_to_all(e, some, 0, 0)
-    (mine,) = call(
+    vmem, anywhere = pl.BlockSpec(memory_space=pltpu.VMEM), pl.BlockSpec(memory_space=pl.ANY)
+    mine = pl.pallas_call(
         exchange_kernel,
-        [struct((4, rows, 2 * width), BF16)],
-        [keep, got],
-        2 * rows * width,
-        after=[e],
-    )
+        out_shape=struct((4, rows, 2 * width), BF16),
+        in_specs=[vmem, vmem, anywhere],
+        out_specs=anywhere,
+        scratch_shapes=[pltpu.VMEM((rows, 2 * width), BF16), pltpu.SemaphoreType.DMA((4,))],
+        compiler_params=pltpu.CompilerParams(vmem_limit_bytes=VMEM_LIMIT),
+        cost_estimate=pl.CostEstimate(
+            flops=2 * rows * width, bytes_accessed=28 * rows * width, transcendentals=0
+        ),
+    )(keep, got, e)
     whole = lax.all_to_all(mine, quad, 0, 0).reshape(part, 2 * width)
     (e,) = call(energies_kernel, [struct((8, LANES), F32)], [e], e.size, after=[mine])
     e_far = swap(e, "zh")

time: 115 us -> 115 us (level)
    pallas_call x0 -> x3, Pallas kernels: none -> 3.51 us  [the longest x2 2.62 us: gather_y(): pl.pallas_call(units_kernel, out_shape=struct((NY, n, width), BF16), in_s...]
    pallas_call x12 -> x9, Pallas kernels: 6.84 us -> 3.87 us  [call(): pl.pallas_call(run, out_shape=out_shape, in_specs=[whole] * count + [pl.B...]
where the time goes in v7:
time: 115 us
  starting transfers between devices  54.5 us (47%)
  waiting for transfers between devices  28.7 us (25%)
  blocking collectives  23.1 us (20%)
  Pallas kernels  7.38 us (6%)
    ppermute x5, starting transfers between devices, swap(): return lax.ppermute(x, axis, [(0, 1), (1, 0)])  37.3 us
    ppermute x5, waiting for transfers between devices, swap(): return lax.ppermute(x, axis, [(0, 1), (1, 0)])  14.2 us
    all_to_all x1, blocking collectives, on_device(): e = lax.all_to_all(e, some, 0, 0)  12.7 us
    all_to_all x2, waiting for transfers between devices, gather_y(): return lax.all_to_all(copies, 'y', 0, 0).reshape(NY * n, width)  11 us
    all_to_all x1, blocking collectives, on_device(): blocks = lax.all_to_all(blocks, 'y', 0, 0)  10.4 us
    all_to_all x2, starting transfers between devices, gather_y(): return lax.all_to_all(copies, 'y', 0, 0).reshape(NY * n, width)  8.1 us
    all_to_all x1, starting transfers between devices, on_device(): got = lax.all_to_all(give, quad, 0, 0)  5.62 us
    pallas_call x9, Pallas kernels, call(): pl.pallas_call(run, out_shape=out_shape, in_specs=[whole] * count + [pl.B...  3.87 us
  transfers between devices with their start and end apart: 9, of which 6 were waited for; matrix products, arithmetic and copies ran while one was open for 0% of the time, Pallas kernels for 3%

profile of v7, /device:TPU:2, one launch (start us, length us, event | category | flops | bytes accessed | tf_op | source)
XLA Modules:
  0.0 114.8 jit_solution(14724794056098890283)
XLA Ops:
  0.0 0.0 copy-start.1
  0.0 0.9 copy-done.1
  0.9 1.3 %shard_map.29 = bf16[4,128,768]{2,1,0:T(8,128)(2,1)} custom-call(bf16[128,768]{1,0:T(8,128)(2,1)S(1)} %copy-done.1), custom_call_target="tpu_custom_call" | custom-call | flops 491520 | bytes 983040 | tf_op jit(solution)/shard_map/pallas_call | solution.py:194
  2.2 0.0 copy-start
  2.3 4.6 %all-to-all-start.1 = ((bf16[4,128,768]{2,1,0:T(8,128)(2,1)}), bf16[4,128,768]{2,1,0:T(8,128)(2,1)S(1)}, u32[]{:S(2)}, u32[]{:S(2)}) async-start(bf16[4,128,768]{2,1,0:T(8,128)(2,1)} %shard_map.29), calls=%async_computation.1 | async-start | bytes 1572864 | tf_op jit(solution)/shard_map/all_to_all | solution.py:210
  6.9 0.0 copy-done
  6.9 1.3 %shard_map.28 = bf16[4,128,768]{2,1,0:T(8,128)(2,1)} custom-call(bf16[128,768]{1,0:T(8,128)(2,1)S(1)} %copy-done), custom_call_target="tpu_custom_call" | custom-call | flops 491520 | bytes 983040 | tf_op jit(solution)/shard_map/pallas_call | solution.py:194
  8.2 11.0 %all-to-all-done.1 = bf16[4,128,768]{2,1,0:T(8,128)(2,1)S(1)} async-done(((bf16[4,128,768]{2,1,0:T(8,128)(2,1)}), bf16[4,128,768]{2,1,0:T(8,128)(2,1)S(1)}, u32[]{:S(2)}, u32[]{:S(2)}) %all-to-all-start.1) | async-done | bytes 786464 | tf_op jit(solution)/shard_map/all_to_all | solution.py:210
  19.2 3.5 %all-to-all-start = ((bf16[4,128,768]{2,1,0:T(8,128)(2,1)}), bf16[4,128,768]{2,1,0:T(8,128)(2,1)S(1)}, u32[]{:S(2)}, u32[]{:S(2)}) async-start(bf16[4,128,768]{2,1,0:T(8,128)(2,1)} %shard_map.28), calls=%async_computation | async-start | bytes 1572864 | tf_op jit(solution)/shard_map/all_to_all | solution.py:210
  22.7 0.5 shard_map.31
  23.2 3.8 %collective-permute-start = (bf16[384,128]{1,0:T(8,128)(2,1)S(1)}, bf16[384,128]{1,0:T(8,128)(2,1)S(1)}, u32[]{:S(2)}, u32[]{:S(2)}) collective-permute-start(bf16[384,128]{1,0:T(8,128)(2,1)S(1)} %get-tuple-element.15), channel_id=1, source_target_pairs={{0,4},{4,0},{1,5},{5,1},{2,6},{6,2},{3,7},{7,3},{8,12},{12,8},{9,1... | collective-permute-start | bytes 294920 | tf_op jit(solution)/shard_map/ppermute | solution.py:189
  27.0 2.7 %collective-permute-done.refs_1_ = bf16[384,128]{1,0:T(8,128)(2,1)S(1)} collective-permute-done((bf16[384,128]{1,0:T(8,128)(2,1)S(1)}, bf16[384,128]{1,0:T(8,128)(2,1)S(1)}, u32[]{:S(2)}, u32[]{:S(2)}) %collective-permute-start) | collective-permute-done | bytes 98336 | tf_op jit(solution)/shard_map/ppermute | solution.py:189
  29.7 5.2 %collective-permute-start.1 = (bf16[192,128]{1,0:T(8,128)(2,1)S(1)}, bf16[192,128]{1,0:T(8,128)(2,1)S(1)}, u32[]{:S(2)}, u32[]{:S(2)}) collective-permute-start(bf16[192,128]{1,0:T(8,128)(2,1)S(1)} %get-tuple-element.17), channel_id=1, source_target_pairs={{0,8},{8,0},{1,9},{9,1},{2,10},{10,2},{3,11},{11,3},{4,12},{12,4},... | collective-permute-start | bytes 147464 | tf_op jit(solution)/shard_map/ppermute | solution.py:189
  34.9 0.0 all-to-all-done
  34.9 1.4 %shard_map.30 = bf16[4,48,1536]{2,1,0:T(8,128)(2,1)} custom-call(bf16[512,768]{1,0:T(8,128)(2,1)S(1)} %bitcast.6, bf16[512,768]{1,0:T(8,128)(2,1)S(1)} %bitcast.4), custom_call_target="tpu_custom_call" | custom-call | flops 301989888 | bytes 2162688 | tf_op jit(solution)/shard_map/pallas_call | solution.py:30
  36.3 0.6 collective-permute-done.1.refs_1_
  37.0 5.6 %all-to-all-start.2 = ((bf16[4,48,1536]{2,1,0:T(8,128)(2,1)}), bf16[4,48,1536]{2,1,0:T(8,128)(2,1)S(1)}, u32[]{:S(2)}, u32[]{:S(2)}) async-start(bf16[4,48,1536]{2,1,0:T(8,128)(2,1)} %shard_map.30), calls=%async_computation.2 | async-start | bytes 1179648 | tf_op jit(solution)/shard_map/all_to_all | solution.py:255
  42.6 9.1 %collective-permute-start.2 = (bf16[192,128]{1,0:T(8,128)(2,1)S(1)}, bf16[192,128]{1,0:T(8,128)(2,1)S(1)}, u32[]{:S(2)}, u32[]{:S(2)}) collective-permute-start(bf16[192,128]{1,0:T(8,128)(2,1)S(1)} %get-tuple-element.18), channel_id=1, source_target_pairs={{0,16},{16,0},{1,17},{17,1},{2,18},{18,2},{3,19},{19,3},{4,20},{20... | collective-permute-start | bytes 147464 | tf_op jit(solution)/shard_map/ppermute | solution.py:189
  51.7 2.2 %collective-permute-done.2.refs_1_ = bf16[192,128]{1,0:T(8,128)(2,1)S(1)} collective-permute-done((bf16[192,128]{1,0:T(8,128)(2,1)S(1)}, bf16[192,128]{1,0:T(8,128)(2,1)S(1)}, u32[]{:S(2)}, u32[]{:S(2)}) %collective-permute-start.2) | collective-permute-done | bytes 49184 | tf_op jit(solution)/shard_map/ppermute | solution.py:189
  53.9 3.6 %all-to-all-done.2.refs_0_ = bf16[4,48,1536]{2,1,0:T(8,128)(2,1)S(1)} async-done(((bf16[4,48,1536]{2,1,0:T(8,128)(2,1)}), bf16[4,48,1536]{2,1,0:T(8,128)(2,1)S(1)}, u32[]{:S(2)}, u32[]{:S(2)}) %all-to-all-start.2) | async-done | bytes 589856 | tf_op jit(solution)/shard_map/all_to_all | solution.py:255
  57.5 0.1 shard_map.34
  57.5 9.0 %collective-permute-start.3 = (bf16[48,1536]{1,0:T(8,128)(2,1)S(1)}, bf16[48,1536]{1,0:T(8,128)(2,1)S(1)}, u32[]{:S(2)}, u32[]{:S(2)}) collective-permute-start(bf16[48,1536]{1,0:T(8,128)(2,1)S(1)} %get-tuple-element.21.refs_2_), channel_id=1, source_target_pairs={{0,16},{16,0},{1,17},{17,1},{2,18},{18,2},{3,19},{19,3},{4,20},{20... | collective-permute-start | bytes 442376 | tf_op jit(solution)/shard_map/ppermute | solution.py:189
  66.6 12.7 %all_to_all.30.e_ref.refs_0_ = f32[32,1,128]{2,1,0:T(1,128)S(1)} all-to-all(f32[32,1,128]{2,1,0:T(1,128)S(1)} %shard_map.35), channel_id=1, replica_groups=mesh['zh'=2,'xc'=8,'zf'=2,'z2'=2,'z1'=2,'y'=4] {'xc','z2','z1'}, dimensions={0} | all-to-all | bytes 32768 | tf_op jit(solution)/shard_map/all_to_all | solution.py:268
  79.3 0.0 collective-permute-done.3.got_ref
  79.3 0.9 shard_map.36.refs_1_
  80.2 3.5 %all-to-all-start.4 = ((bf16[4,48,1536]{2,1,0:T(8,128)(2,1)}), bf16[4,48,1536]{2,1,0:T(8,128)(2,1)S(1)}, u32[]{:S(2)}, u32[]{:S(2)}) async-start(bf16[4,48,1536]{2,1,0:T(8,128)(2,1)} %shard_map.36.refs_1_), calls=%async_computation.4 | async-start | bytes 1179648 | tf_op jit(solution)/shard_map/all_to_all | solution.py:281
  83.8 10.1 %collective-permute-start.4 = (f32[8,128]{1,0:T(8,128)S(1)}, f32[8,128]{1,0:T(8,128)S(1)}, u32[]{:S(2)}, u32[]{:S(2)}) collective-permute-start(f32[8,128]{1,0:T(8,128)S(1)} %shard_map.37.refs_3_), channel_id=1, source_target_pairs={{0,256},{256,0},{1,257},{257,1},{2,258},{258,2},{3,259},{259,3},{4... | collective-permute-start | bytes 12296 | tf_op jit(solution)/shard_map/ppermute | solution.py:189
  93.9 8.7 %collective-permute-done.4.refs_4_ = f32[8,128]{1,0:T(8,128)S(1)} collective-permute-done((f32[8,128]{1,0:T(8,128)S(1)}, f32[8,128]{1,0:T(8,128)S(1)}, u32[]{:S(2)}, u32[]{:S(2)}) %collective-permute-start.4) | collective-permute-done | bytes 4128 | tf_op jit(solution)/shard_map/ppermute | solution.py:189
  102.6 0.0 all-to-all-done.4
  102.6 0.7 shard_map.38
  103.3 10.4 %all_to_all.31.refs_0_ = bf16[4,208,128]{2,1,0:T(8,128)(2,1)S(1)} all-to-all(bf16[4,208,128]{2,1,0:T(8,128)(2,1)S(1)} %shard_map.38), channel_id=1, replica_groups=mesh['zh'=2,'xc'=8,'zf'=2,'z2'=2,'z1'=2,'y'=4] {'y'}, dimensions={0} | all-to-all | bytes 425984 | tf_op jit(solution)/shard_map/all_to_all | solution.py:290
  113.7 1.1 shard_map.39
  (4 shorter events, 0.1 us)
Async XLA Ops:
  0.0 0.9 copy-start.1
  2.2 4.6 %copy-start = (bf16[128,768]{1,0:T(8,128)(2,1)S(1)}, bf16[128,768]{1,0:T(8,128)(2,1)}, u32[]{:S(2)}) copy-start(bf16[128,768]{1,0:T(8,128)(2,1)} %refs_1_.1) | copy-start | bytes 589828
  2.3 16.9 %all-to-all-start.1 = ((bf16[4,128,768]{2,1,0:T(8,128)(2,1)}), bf16[4,128,768]{2,1,0:T(8,128)(2,1)S(1)}, u32[]{:S(2)}, u32[]{:S(2)}) async-start(bf16[4,128,768]{2,1,0:T(8,128)(2,1)} %shard_map.29), calls=%async_computation.1 | async-start | bytes 1572864 | tf_op jit(solution)/shard_map/all_to_all | solution.py:210
  19.2 15.7 %all-to-all-start = ((bf16[4,128,768]{2,1,0:T(8,128)(2,1)}), bf16[4,128,768]{2,1,0:T(8,128)(2,1)S(1)}, u32[]{:S(2)}, u32[]{:S(2)}) async-start(bf16[4,128,768]{2,1,0:T(8,128)(2,1)} %shard_map.28), calls=%async_computation | async-start | bytes 1572864 | tf_op jit(solution)/shard_map/all_to_all | solution.py:210
  23.2 6.5 %collective-permute-start = (bf16[384,128]{1,0:T(8,128)(2,1)S(1)}, bf16[384,128]{1,0:T(8,128)(2,1)S(1)}, u32[]{:S(2)}, u32[]{:S(2)}) collective-permute-start(bf16[384,128]{1,0:T(8,128)(2,1)S(1)} %get-tuple-element.15), channel_id=1, source_target_pairs={{0,4},{4,0},{1,5},{5,1},{2,6},{6,2},{3,7},{7,3},{8,12},{12,8},{9,1... | collective-permute-start | bytes 294920 | tf_op jit(solution)/shard_map/ppermute | solution.py:189
  29.7 7.2 %collective-permute-start.1 = (bf16[192,128]{1,0:T(8,128)(2,1)S(1)}, bf16[192,128]{1,0:T(8,128)(2,1)S(1)}, u32[]{:S(2)}, u32[]{:S(2)}) collective-permute-start(bf16[192,128]{1,0:T(8,128)(2,1)S(1)} %get-tuple-element.17), channel_id=1, source_target_pairs={{0,8},{8,0},{1,9},{9,1},{2,10},{10,2},{3,11},{11,3},{4,12},{12,4},... | collective-permute-start | bytes 147464 | tf_op jit(solution)/shard_map/ppermute | solution.py:189
  37.0 20.5 %all-to-all-start.2 = ((bf16[4,48,1536]{2,1,0:T(8,128)(2,1)}), bf16[4,48,1536]{2,1,0:T(8,128)(2,1)S(1)}, u32[]{:S(2)}, u32[]{:S(2)}) async-start(bf16[4,48,1536]{2,1,0:T(8,128)(2,1)} %shard_map.30), calls=%async_computation.2 | async-start | bytes 1179648 | tf_op jit(solution)/shard_map/all_to_all | solution.py:255
  42.6 11.3 %collective-permute-start.2 = (bf16[192,128]{1,0:T(8,128)(2,1)S(1)}, bf16[192,128]{1,0:T(8,128)(2,1)S(1)}, u32[]{:S(2)}, u32[]{:S(2)}) collective-permute-start(bf16[192,128]{1,0:T(8,128)(2,1)S(1)} %get-tuple-element.18), channel_id=1, source_target_pairs={{0,16},{16,0},{1,17},{17,1},{2,18},{18,2},{3,19},{19,3},{4,20},{20... | collective-permute-start | bytes 147464 | tf_op jit(solution)/shard_map/ppermute | solution.py:189
  57.5 21.8 %collective-permute-start.3 = (bf16[48,1536]{1,0:T(8,128)(2,1)S(1)}, bf16[48,1536]{1,0:T(8,128)(2,1)S(1)}, u32[]{:S(2)}, u32[]{:S(2)}) collective-permute-start(bf16[48,1536]{1,0:T(8,128)(2,1)S(1)} %get-tuple-element.21.refs_2_), channel_id=1, source_target_pairs={{0,16},{16,0},{1,17},{17,1},{2,18},{18,2},{3,19},{19,3},{4,20},{20... | collective-permute-start | bytes 442376 | tf_op jit(solution)/shard_map/ppermute | solution.py:189
  80.2 22.4 %all-to-all-start.4 = ((bf16[4,48,1536]{2,1,0:T(8,128)(2,1)}), bf16[4,48,1536]{2,1,0:T(8,128)(2,1)S(1)}, u32[]{:S(2)}, u32[]{:S(2)}) async-start(bf16[4,48,1536]{2,1,0:T(8,128)(2,1)} %shard_map.36.refs_1_), calls=%async_computation.4 | async-start | bytes 1179648 | tf_op jit(solution)/shard_map/all_to_all | solution.py:281
  83.8 18.9 %collective-permute-start.4 = (f32[8,128]{1,0:T(8,128)S(1)}, f32[8,128]{1,0:T(8,128)S(1)}, u32[]{:S(2)}, u32[]{:S(2)}) collective-permute-start(f32[8,128]{1,0:T(8,128)S(1)} %shard_map.37.refs_3_), channel_id=1, source_target_pairs={{0,256},{256,0},{1,257},{257,1},{2,258},{258,2},{3,259},{259,3},{4... | collective-permute-start | bytes 12296 | tf_op jit(solution)/shard_map/ppermute | solution.py:189

commit v8 on v7

--- a/solution.py
+++ b/solution.py
@@ -157,9 +157,10 @@
     send_ref[...] = total.astype(BF16)
 
 
-def exchange_kernel(mine_ref, got_ref, e_ref, out_ref, total, sems):
-    total[...] = (mine_ref[...] + got_ref[...].astype(F32)).astype(BF16)
-    send_copies(total, out_ref, sems)
+def exchange_kernel(mine_ref, got_ref, out_ref):
+    out_ref[...] = jnp.broadcast_to(
+        (mine_ref[...] + got_ref[...].astype(F32)).astype(BF16), out_ref.shape
+    )
 
 
 def pull_kernel(whole, ring_s, ring_t, e_ref, f_ref, out_ref):
@@ -202,7 +203,7 @@
             pltpu.SemaphoreType.DMA,
             pltpu.SemaphoreType.DMA((NY,)),
         ],
-        compiler_params=pltpu.CompilerParams(vmem_limit_bytes=VMEM_LIMIT),
+        compiler_params=pltpu.CompilerParams(vmem_limit_bytes=60 * 1024 * 1024),
         cost_estimate=pl.CostEstimate(
             flops=5 * n * width, bytes_accessed=10 * n * width, transcendentals=0
         ),
@@ -266,18 +267,13 @@
         after=[give],
     )
     e = lax.all_to_all(e, some, 0, 0)
-    vmem, anywhere = pl.BlockSpec(memory_space=pltpu.VMEM), pl.BlockSpec(memory_space=pl.ANY)
-    mine = pl.pallas_call(
+    (mine,) = call(
         exchange_kernel,
-        out_shape=struct((4, rows, 2 * width), BF16),
-        in_specs=[vmem, vmem, anywhere],
-        out_specs=anywhere,
-        scratch_shapes=[pltpu.VMEM((rows, 2 * width), BF16), pltpu.SemaphoreType.DMA((4,))],
-        compiler_params=pltpu.CompilerParams(vmem_limit_bytes=VMEM_LIMIT),
-        cost_estimate=pl.CostEstimate(
-            flops=2 * rows * width, bytes_accessed=28 * rows * width, transcendentals=0
-        ),
-    )(keep, got, e)
+        [struct((4, rows, 2 * width), BF16)],
+        [keep, got],
+        2 * rows * width,
+        after=[e],
+    )
     whole = lax.all_to_all(mine, quad, 0, 0).reshape(part, 2 * width)
     (e,) = call(energies_kernel, [struct((8, LANES), F32)], [e], e.size, after=[mine])
     e_far = swap(e, "zh")

time: 115 us -> 115 us (level)
  Pallas kernels: 7.38 us -> 8.75 us
    pallas_call x2, Pallas kernels: 2.62 us -> 4.02 us  [gather_y(): pl.pallas_call(units_kernel, out_shape=struct((NY, n, width), BF16), in_s...]
    pallas_call x9 -> x10, Pallas kernels: 3.87 us -> 4.73 us  [call(): pl.pallas_call(run, out_shape=out_shape, in_specs=[whole] * count + [pl.B...]
  transfers between devices with their start and end apart: 9 -> 9, of which waited for: 6 -> 6; matrix products, arithmetic and copies ran while one was open for 0% -> 0% of each run, Pallas kernels for 3% -> 4%
where the time goes in v8:
time: 115 us
  starting transfers between devices  54.3 us (47%)
  waiting for transfers between devices  28.1 us (24%)
  blocking collectives  23.2 us (20%)
  Pallas kernels  8.75 us (8%)
    ppermute x5, starting transfers between devices, swap(): return lax.ppermute(x, axis, [(0, 1), (1, 0)])  37.3 us
    ppermute x5, waiting for transfers between devices, swap(): return lax.ppermute(x, axis, [(0, 1), (1, 0)])  14.2 us
    all_to_all x1, blocking collectives, on_device(): e = lax.all_to_all(e, some, 0, 0)  12.7 us
    all_to_all x1, blocking collectives, on_device(): blocks = lax.all_to_all(blocks, 'y', 0, 0)  10.5 us
    all_to_all x2, waiting for transfers between devices, gather_y(): return lax.all_to_all(copies, 'y', 0, 0).reshape(NY * n, width)  10.3 us
    all_to_all x2, starting transfers between devices, gather_y(): return lax.all_to_all(copies, 'y', 0, 0).reshape(NY * n, width)  7.97 us
    all_to_all x1, starting transfers between devices, on_device(): got = lax.all_to_all(give, quad, 0, 0)  5.62 us
    pallas_call x10, Pallas kernels, call(): pl.pallas_call(run, out_shape=out_shape, in_specs=[whole] * count + [pl.B...  4.73 us
  transfers between devices with their start and end apart: 9, of which 6 were waited for; matrix products, arithmetic and copies ran while one was open for 0% of the time, Pallas kernels for 4%

profile of v8, /device:TPU:2, one launch (start us, length us, event | category | flops | bytes accessed | tf_op | source)
XLA Modules:
  0.0 114.5 jit_solution(815348244223770524)
XLA Ops:
  0.0 2.0 %shard_map.29 = bf16[4,128,768]{2,1,0:T(8,128)(2,1)} custom-call(bf16[128,768]{1,0:T(8,128)(2,1)} %x_ref.3), custom_call_target="tpu_custom_call" | custom-call | flops 491520 | bytes 983040 | tf_op jit(solution)/shard_map/pallas_call | solution.py:195
  2.0 4.5 %all-to-all-start.1 = ((bf16[4,128,768]{2,1,0:T(8,128)(2,1)}), bf16[4,128,768]{2,1,0:T(8,128)(2,1)S(1)}, u32[]{:S(2)}, u32[]{:S(2)}) async-start(bf16[4,128,768]{2,1,0:T(8,128)(2,1)} %shard_map.29), calls=%async_computation.1 | async-start | bytes 1572864 | tf_op jit(solution)/shard_map/all_to_all | solution.py:211
  6.5 2.0 %shard_map.28 = bf16[4,128,768]{2,1,0:T(8,128)(2,1)} custom-call(bf16[128,768]{1,0:T(8,128)(2,1)} %refs_1_.1), custom_call_target="tpu_custom_call" | custom-call | flops 491520 | bytes 983040 | tf_op jit(solution)/shard_map/pallas_call | solution.py:195
  8.5 10.3 %all-to-all-done.1 = bf16[4,128,768]{2,1,0:T(8,128)(2,1)S(1)} async-done(((bf16[4,128,768]{2,1,0:T(8,128)(2,1)}), bf16[4,128,768]{2,1,0:T(8,128)(2,1)S(1)}, u32[]{:S(2)}, u32[]{:S(2)}) %all-to-all-start.1) | async-done | bytes 786464 | tf_op jit(solution)/shard_map/all_to_all | solution.py:211
  18.8 3.5 %all-to-all-start = ((bf16[4,128,768]{2,1,0:T(8,128)(2,1)}), bf16[4,128,768]{2,1,0:T(8,128)(2,1)S(1)}, u32[]{:S(2)}, u32[]{:S(2)}) async-start(bf16[4,128,768]{2,1,0:T(8,128)(2,1)} %shard_map.28), calls=%async_computation | async-start | bytes 1572864 | tf_op jit(solution)/shard_map/all_to_all | solution.py:211
  22.3 0.5 shard_map.31
  22.8 3.8 %collective-permute-start = (bf16[384,128]{1,0:T(8,128)(2,1)S(1)}, bf16[384,128]{1,0:T(8,128)(2,1)S(1)}, u32[]{:S(2)}, u32[]{:S(2)}) collective-permute-start(bf16[384,128]{1,0:T(8,128)(2,1)S(1)} %get-tuple-element.15), channel_id=1, source_target_pairs={{0,4},{4,0},{1,5},{5,1},{2,6},{6,2},{3,7},{7,3},{8,12},{12,8},{9,1... | collective-permute-start | bytes 294920 | tf_op jit(solution)/shard_map/ppermute | solution.py:190
  26.6 2.7 %collective-permute-done.refs_1_ = bf16[384,128]{1,0:T(8,128)(2,1)S(1)} collective-permute-done((bf16[384,128]{1,0:T(8,128)(2,1)S(1)}, bf16[384,128]{1,0:T(8,128)(2,1)S(1)}, u32[]{:S(2)}, u32[]{:S(2)}) %collective-permute-start) | collective-permute-done | bytes 98336 | tf_op jit(solution)/shard_map/ppermute | solution.py:190
  29.3 5.2 %collective-permute-start.1 = (bf16[192,128]{1,0:T(8,128)(2,1)S(1)}, bf16[192,128]{1,0:T(8,128)(2,1)S(1)}, u32[]{:S(2)}, u32[]{:S(2)}) collective-permute-start(bf16[192,128]{1,0:T(8,128)(2,1)S(1)} %get-tuple-element.17), channel_id=1, source_target_pairs={{0,8},{8,0},{1,9},{9,1},{2,10},{10,2},{3,11},{11,3},{4,12},{12,4},... | collective-permute-start | bytes 147464 | tf_op jit(solution)/shard_map/ppermute | solution.py:190
  34.5 0.0 all-to-all-done
  34.5 1.4 %shard_map.30 = bf16[4,48,1536]{2,1,0:T(8,128)(2,1)} custom-call(bf16[512,768]{1,0:T(8,128)(2,1)S(1)} %bitcast.6, bf16[512,768]{1,0:T(8,128)(2,1)S(1)} %bitcast.4), custom_call_target="tpu_custom_call" | custom-call | flops 301989888 | bytes 2162688 | tf_op jit(solution)/shard_map/pallas_call | solution.py:30
  36.0 0.6 collective-permute-done.1.refs_1_
  36.6 5.6 %all-to-all-start.2 = ((bf16[4,48,1536]{2,1,0:T(8,128)(2,1)}), bf16[4,48,1536]{2,1,0:T(8,128)(2,1)S(1)}, u32[]{:S(2)}, u32[]{:S(2)}) async-start(bf16[4,48,1536]{2,1,0:T(8,128)(2,1)} %shard_map.30), calls=%async_computation.2 | async-start | bytes 1179648 | tf_op jit(solution)/shard_map/all_to_all | solution.py:256
  42.2 9.1 %collective-permute-start.2 = (bf16[192,128]{1,0:T(8,128)(2,1)S(1)}, bf16[192,128]{1,0:T(8,128)(2,1)S(1)}, u32[]{:S(2)}, u32[]{:S(2)}) collective-permute-start(bf16[192,128]{1,0:T(8,128)(2,1)S(1)} %get-tuple-element.18), channel_id=1, source_target_pairs={{0,16},{16,0},{1,17},{17,1},{2,18},{18,2},{3,19},{19,3},{4,20},{20... | collective-permute-start | bytes 147464 | tf_op jit(solution)/shard_map/ppermute | solution.py:190
  51.3 2.2 %collective-permute-done.2.refs_1_ = bf16[192,128]{1,0:T(8,128)(2,1)S(1)} collective-permute-done((bf16[192,128]{1,0:T(8,128)(2,1)S(1)}, bf16[192,128]{1,0:T(8,128)(2,1)S(1)}, u32[]{:S(2)}, u32[]{:S(2)}) %collective-permute-start.2) | collective-permute-done | bytes 49184 | tf_op jit(solution)/shard_map/ppermute | solution.py:190
  53.5 3.6 %all-to-all-done.2.refs_0_ = bf16[4,48,1536]{2,1,0:T(8,128)(2,1)S(1)} async-done(((bf16[4,48,1536]{2,1,0:T(8,128)(2,1)}), bf16[4,48,1536]{2,1,0:T(8,128)(2,1)S(1)}, u32[]{:S(2)}, u32[]{:S(2)}) %all-to-all-start.2) | async-done | bytes 589856 | tf_op jit(solution)/shard_map/all_to_all | solution.py:256
  57.1 0.1 shard_map.34
  57.2 9.0 %collective-permute-start.3 = (bf16[48,1536]{1,0:T(8,128)(2,1)S(1)}, bf16[48,1536]{1,0:T(8,128)(2,1)S(1)}, u32[]{:S(2)}, u32[]{:S(2)}) collective-permute-start(bf16[48,1536]{1,0:T(8,128)(2,1)S(1)} %get-tuple-element.21.refs_2_), channel_id=1, source_target_pairs={{0,16},{16,0},{1,17},{17,1},{2,18},{18,2},{3,19},{19,3},{4,20},{20... | collective-permute-start | bytes 442376 | tf_op jit(solution)/shard_map/ppermute | solution.py:190
  66.3 12.7 %all_to_all.30.refs_2_.refs_0_ = f32[32,1,128]{2,1,0:T(1,128)S(1)} all-to-all(f32[32,1,128]{2,1,0:T(1,128)S(1)} %shard_map.35), channel_id=1, replica_groups=mesh['zh'=2,'xc'=8,'zf'=2,'z2'=2,'z1'=2,'y'=4] {'xc','z2','z1'}, dimensions={0} | all-to-all | bytes 32768 | tf_op jit(solution)/shard_map/all_to_all | solution.py:269
  79.0 0.0 collective-permute-done.3.refs_1_
  79.0 0.9 shard_map.36.refs_1_
  79.9 3.5 %all-to-all-start.4 = ((bf16[4,48,1536]{2,1,0:T(8,128)(2,1)}), bf16[4,48,1536]{2,1,0:T(8,128)(2,1)S(1)}, u32[]{:S(2)}, u32[]{:S(2)}) async-start(bf16[4,48,1536]{2,1,0:T(8,128)(2,1)} %shard_map.36.refs_1_), calls=%async_computation.4 | async-start | bytes 1179648 | tf_op jit(solution)/shard_map/all_to_all | solution.py:277
  83.4 10.1 %collective-permute-start.4 = (f32[8,128]{1,0:T(8,128)S(1)}, f32[8,128]{1,0:T(8,128)S(1)}, u32[]{:S(2)}, u32[]{:S(2)}) collective-permute-start(f32[8,128]{1,0:T(8,128)S(1)} %shard_map.37.refs_3_), channel_id=1, source_target_pairs={{0,256},{256,0},{1,257},{257,1},{2,258},{258,2},{3,259},{259,3},{4... | collective-permute-start | bytes 12296 | tf_op jit(solution)/shard_map/ppermute | solution.py:190
  93.5 8.7 %collective-permute-done.4.refs_4_ = f32[8,128]{1,0:T(8,128)S(1)} collective-permute-done((f32[8,128]{1,0:T(8,128)S(1)}, f32[8,128]{1,0:T(8,128)S(1)}, u32[]{:S(2)}, u32[]{:S(2)}) %collective-permute-start.4) | collective-permute-done | bytes 4128 | tf_op jit(solution)/shard_map/ppermute | solution.py:190
  102.2 0.0 all-to-all-done.4
  102.2 0.7 shard_map.38
  102.9 0.0 copy-start
  102.9 10.5 %all_to_all.31.refs_0_ = bf16[4,208,128]{2,1,0:T(8,128)(2,1)S(1)} all-to-all(bf16[4,208,128]{2,1,0:T(8,128)(2,1)S(1)} %shard_map.38), channel_id=1, replica_groups=mesh['zh'=2,'xc'=8,'zf'=2,'z2'=2,'z1'=2,'y'=4] {'y'}, dimensions={0} | all-to-all | bytes 425984 | tf_op jit(solution)/shard_map/all_to_all | solution.py:286
  113.4 0.0 copy-done
  113.4 1.1 shard_map.39
  (4 shorter events, 0.1 us)
Async XLA Ops:
  2.0 16.8 %all-to-all-start.1 = ((bf16[4,128,768]{2,1,0:T(8,128)(2,1)}), bf16[4,128,768]{2,1,0:T(8,128)(2,1)S(1)}, u32[]{:S(2)}, u32[]{:S(2)}) async-start(bf16[4,128,768]{2,1,0:T(8,128)(2,1)} %shard_map.29), calls=%async_computation.1 | async-start | bytes 1572864 | tf_op jit(solution)/shard_map/all_to_all | solution.py:211
  18.8 15.7 %all-to-all-start = ((bf16[4,128,768]{2,1,0:T(8,128)(2,1)}), bf16[4,128,768]{2,1,0:T(8,128)(2,1)S(1)}, u32[]{:S(2)}, u32[]{:S(2)}) async-start(bf16[4,128,768]{2,1,0:T(8,128)(2,1)} %shard_map.28), calls=%async_computation | async-start | bytes 1572864 | tf_op jit(solution)/shard_map/all_to_all | solution.py:211
  22.8 6.5 %collective-permute-start = (bf16[384,128]{1,0:T(8,128)(2,1)S(1)}, bf16[384,128]{1,0:T(8,128)(2,1)S(1)}, u32[]{:S(2)}, u32[]{:S(2)}) collective-permute-start(bf16[384,128]{1,0:T(8,128)(2,1)S(1)} %get-tuple-element.15), channel_id=1, source_target_pairs={{0,4},{4,0},{1,5},{5,1},{2,6},{6,2},{3,7},{7,3},{8,12},{12,8},{9,1... | collective-permute-start | bytes 294920 | tf_op jit(solution)/shard_map/ppermute | solution.py:190
  29.3 7.2 %collective-permute-start.1 = (bf16[192,128]{1,0:T(8,128)(2,1)S(1)}, bf16[192,128]{1,0:T(8,128)(2,1)S(1)}, u32[]{:S(2)}, u32[]{:S(2)}) collective-permute-start(bf16[192,128]{1,0:T(8,128)(2,1)S(1)} %get-tuple-element.17), channel_id=1, source_target_pairs={{0,8},{8,0},{1,9},{9,1},{2,10},{10,2},{3,11},{11,3},{4,12},{12,4},... | collective-permute-start | bytes 147464 | tf_op jit(solution)/shard_map/ppermute | solution.py:190
  36.6 20.5 %all-to-all-start.2 = ((bf16[4,48,1536]{2,1,0:T(8,128)(2,1)}), bf16[4,48,1536]{2,1,0:T(8,128)(2,1)S(1)}, u32[]{:S(2)}, u32[]{:S(2)}) async-start(bf16[4,48,1536]{2,1,0:T(8,128)(2,1)} %shard_map.30), calls=%async_computation.2 | async-start | bytes 1179648 | tf_op jit(solution)/shard_map/all_to_all | solution.py:256
  42.2 11.3 %collective-permute-start.2 = (bf16[192,128]{1,0:T(8,128)(2,1)S(1)}, bf16[192,128]{1,0:T(8,128)(2,1)S(1)}, u32[]{:S(2)}, u32[]{:S(2)}) collective-permute-start(bf16[192,128]{1,0:T(8,128)(2,1)S(1)} %get-tuple-element.18), channel_id=1, source_target_pairs={{0,16},{16,0},{1,17},{17,1},{2,18},{18,2},{3,19},{19,3},{4,20},{20... | collective-permute-start | bytes 147464 | tf_op jit(solution)/shard_map/ppermute | solution.py:190
  57.2 21.8 %collective-permute-start.3 = (bf16[48,1536]{1,0:T(8,128)(2,1)S(1)}, bf16[48,1536]{1,0:T(8,128)(2,1)S(1)}, u32[]{:S(2)}, u32[]{:S(2)}) collective-permute-start(bf16[48,1536]{1,0:T(8,128)(2,1)S(1)} %get-tuple-element.21.refs_2_), channel_id=1, source_target_pairs={{0,16},{16,0},{1,17},{17,1},{2,18},{18,2},{3,19},{19,3},{4,20},{20... | collective-permute-start | bytes 442376 | tf_op jit(solution)/shard_map/ppermute | solution.py:190
  79.9 22.4 %all-to-all-start.4 = ((bf16[4,48,1536]{2,1,0:T(8,128)(2,1)}), bf16[4,48,1536]{2,1,0:T(8,128)(2,1)S(1)}, u32[]{:S(2)}, u32[]{:S(2)}) async-start(bf16[4,48,1536]{2,1,0:T(8,128)(2,1)} %shard_map.36.refs_1_), calls=%async_computation.4 | async-start | bytes 1179648 | tf_op jit(solution)/shard_map/all_to_all | solution.py:277
  83.4 18.9 %collective-permute-start.4 = (f32[8,128]{1,0:T(8,128)S(1)}, f32[8,128]{1,0:T(8,128)S(1)}, u32[]{:S(2)}, u32[]{:S(2)}) collective-permute-start(f32[8,128]{1,0:T(8,128)S(1)} %shard_map.37.refs_3_), channel_id=1, source_target_pairs={{0,256},{256,0},{1,257},{257,1},{2,258},{258,2},{3,259},{259,3},{4... | collective-permute-start | bytes 12296 | tf_op jit(solution)/shard_map/ppermute | solution.py:190
  102.9 10.5 %copy-start = (bf16[128,768]{1,0:T(8,128)(2,1)S(1)}, bf16[128,768]{1,0:T(8,128)(2,1)}, u32[]{:S(2)}) copy-start(bf16[128,768]{1,0:T(8,128)(2,1)} %refs_1_.1) | copy-start | bytes 589828

commit v9 on v5

--- a/solution.py
+++ b/solution.py
@@ -216,6 +216,7 @@
         [pltpu.VMEM((width // 2, LANES), F32)],
     )
     tt_got = swap(tt_give, "z2")
+    z2_give = tt_give
     tt, tt_give = call(add_kernel, pair(width // 4, LANES), [tt, tt_got], rows * width)
     (give,) = call(
         student_kernel,
@@ -224,7 +225,7 @@
         4 * mac,
         [pltpu.VMEM((2 * LANES, texts), BF16)],
     )
-    give = lax.optimization_barrier((give, tt_give))[0]
+    give = lax.optimization_barrier((give, z2_give))[0]
     tt_got = swap(tt_give, "zf")
     got = lax.all_to_all(give, quad, 0, 0)
     keep, give = call(

time: 115 us -> 123 us (1.070)
  waiting for transfers between devices: 29 us -> 39.9 us
  blocking collectives: 23.1 us -> 21 us
    ppermute x5, waiting for transfers between devices: 14.2 us -> 21.7 us  [swap(): return lax.ppermute(x, axis, [(0, 1), (1, 0)])]
    all_to_all x2, waiting for transfers between devices: 11.2 us -> 18.2 us  [gather_y(): return lax.all_to_all(copies, 'y', 0, 0).reshape(NY * n, width)]
    all_to_all x1, waiting for transfers between devices: 3.57 us -> 0.01 us  [on_device(): got = lax.all_to_all(give, quad, 0, 0)]
    all_to_all x1, blocking collectives: 10.4 us -> 8.79 us  [on_device(): blocks = lax.all_to_all(blocks, 'y', 0, 0)]
    ppermute x5, starting transfers between devices: 37.3 us -> 35.9 us  [swap(): return lax.ppermute(x, axis, [(0, 1), (1, 0)])]
  transfers between devices with their start and end apart: 9 -> 9, of which waited for: 6 -> 5; matrix products, arithmetic and copies ran while one was open for 0% -> 0% of each run, Pallas kernels for 3% -> 3%
where the time goes in v9:
time: 123 us; the launch traced here: 122 us
  starting transfers between devices  53.4 us (43%)
  waiting for transfers between devices  39.9 us (32%)
  blocking collectives  21 us (17%)
  Pallas kernels  6.84 us (6%)
    ppermute x5, starting transfers between devices, swap(): return lax.ppermute(x, axis, [(0, 1), (1, 0)])  35.9 us
    ppermute x5, waiting for transfers between devices, swap(): return lax.ppermute(x, axis, [(0, 1), (1, 0)])  21.7 us
    all_to_all x2, waiting for transfers between devices, gather_y(): return lax.all_to_all(copies, 'y', 0, 0).reshape(NY * n, width)  18.2 us
    all_to_all x1, blocking collectives, on_device(): e = lax.all_to_all(e, some, 0, 0)  12.3 us
    all_to_all x1, blocking collectives, on_device(): blocks = lax.all_to_all(blocks, 'y', 0, 0)  8.79 us
    all_to_all x2, starting transfers between devices, gather_y(): return lax.all_to_all(copies, 'y', 0, 0).reshape(NY * n, width)  8.09 us
    pallas_call x12, Pallas kernels, call(): pl.pallas_call(run, out_shape=out_shape, in_specs=[whole] * count + [pl.B...  6.84 us
    all_to_all x1, starting transfers between devices, on_device(): got = lax.all_to_all(give, quad, 0, 0)  5.9 us
  transfers between devices with their start and end apart: 9, of which 5 were waited for; matrix products, arithmetic and copies ran while one was open for 0% of the time, Pallas kernels for 3%

profile of v9, /device:TPU:2, one launch (start us, length us, event | category | flops | bytes accessed | tf_op | source)
XLA Modules:
  0.0 122.2 jit_solution(2940428587188186268)
XLA Ops:
  0.0 0.0 copy-start.1
  0.0 0.9 copy-done.1
  0.9 1.1 shard_map.29
  2.0 0.0 copy-start
  2.0 4.6 %all-to-all-start.1 = ((bf16[4,128,768]{2,1,0:T(8,128)(2,1)}), bf16[4,128,768]{2,1,0:T(8,128)(2,1)S(1)}, u32[]{:S(2)}, u32[]{:S(2)}) async-start(bf16[4,128,768]{2,1,0:T(8,128)(2,1)} %shard_map.29), calls=%async_computation.1 | async-start | bytes 1572864 | tf_op jit(solution)/shard_map/all_to_all | solution.py:184
  6.6 0.0 copy-done
  6.6 1.0 shard_map.28
  7.6 11.2 %all-to-all-done.1 = bf16[4,128,768]{2,1,0:T(8,128)(2,1)S(1)} async-done(((bf16[4,128,768]{2,1,0:T(8,128)(2,1)}), bf16[4,128,768]{2,1,0:T(8,128)(2,1)S(1)}, u32[]{:S(2)}, u32[]{:S(2)}) %all-to-all-start.1) | async-done | bytes 786464 | tf_op jit(solution)/shard_map/all_to_all | solution.py:184
  18.9 3.5 %all-to-all-start = ((bf16[4,128,768]{2,1,0:T(8,128)(2,1)}), bf16[4,128,768]{2,1,0:T(8,128)(2,1)S(1)}, u32[]{:S(2)}, u32[]{:S(2)}) async-start(bf16[4,128,768]{2,1,0:T(8,128)(2,1)} %shard_map.28), calls=%async_computation | async-start | bytes 1572864 | tf_op jit(solution)/shard_map/all_to_all | solution.py:184
  22.4 0.5 shard_map.31
  22.9 3.8 %collective-permute-start = (bf16[384,128]{1,0:T(8,128)(2,1)S(1)}, bf16[384,128]{1,0:T(8,128)(2,1)S(1)}, u32[]{:S(2)}, u32[]{:S(2)}) collective-permute-start(bf16[384,128]{1,0:T(8,128)(2,1)S(1)} %get-tuple-element.15), channel_id=1, source_target_pairs={{0,4},{4,0},{1,5},{5,1},{2,6},{6,2},{3,7},{7,3},{8,12},{12,8},{9,1... | collective-permute-start | bytes 294920 | tf_op jit(solution)/shard_map/ppermute | solution.py:178
  26.7 7.0 %all-to-all-done = bf16[4,128,768]{2,1,0:T(8,128)(2,1)S(1)} async-done(((bf16[4,128,768]{2,1,0:T(8,128)(2,1)}), bf16[4,128,768]{2,1,0:T(8,128)(2,1)S(1)}, u32[]{:S(2)}, u32[]{:S(2)}) %all-to-all-start) | async-done | bytes 786464 | tf_op jit(solution)/shard_map/all_to_all | solution.py:184
  33.7 1.4 %shard_map.30 = bf16[4,48,1536]{2,1,0:T(8,128)(2,1)} custom-call(bf16[512,768]{1,0:T(8,128)(2,1)S(1)} %bitcast.6, bf16[512,768]{1,0:T(8,128)(2,1)S(1)} %bitcast.4), custom_call_target="tpu_custom_call" | custom-call | flops 301989888 | bytes 2162688 | tf_op jit(solution)/shard_map/pallas_call | solution.py:30
  35.1 0.0 collective-permute-done.refs_1_
  35.2 5.9 %all-to-all-start.2 = ((bf16[4,48,1536]{2,1,0:T(8,128)(2,1)}), bf16[4,48,1536]{2,1,0:T(8,128)(2,1)S(1)}, u32[]{:S(2)}, u32[]{:S(2)}) async-start(bf16[4,48,1536]{2,1,0:T(8,128)(2,1)} %shard_map.30), calls=%async_computation.2 | async-start | bytes 1179648 | tf_op jit(solution)/shard_map/all_to_all | solution.py:230
  41.1 4.8 %collective-permute-start.1 = (bf16[192,128]{1,0:T(8,128)(2,1)S(1)}, bf16[192,128]{1,0:T(8,128)(2,1)S(1)}, u32[]{:S(2)}, u32[]{:S(2)}) collective-permute-start(bf16[192,128]{1,0:T(8,128)(2,1)S(1)} %get-tuple-element.16), channel_id=1, source_target_pairs={{0,8},{8,0},{1,9},{9,1},{2,10},{10,2},{3,11},{11,3},{4,12},{12,4},... | collective-permute-start | bytes 147464 | tf_op jit(solution)/shard_map/ppermute | solution.py:178
  45.9 10.8 %collective-permute-done.1.refs_1_ = bf16[192,128]{1,0:T(8,128)(2,1)S(1)} collective-permute-done((bf16[192,128]{1,0:T(8,128)(2,1)S(1)}, bf16[192,128]{1,0:T(8,128)(2,1)S(1)}, u32[]{:S(2)}, u32[]{:S(2)}) %collective-permute-start.1) | collective-permute-done | bytes 49184 | tf_op jit(solution)/shard_map/ppermute | solution.py:178
  56.7 9.1 %collective-permute-start.2 = (bf16[192,128]{1,0:T(8,128)(2,1)S(1)}, bf16[192,128]{1,0:T(8,128)(2,1)S(1)}, u32[]{:S(2)}, u32[]{:S(2)}) collective-permute-start(bf16[192,128]{1,0:T(8,128)(2,1)S(1)} %get-tuple-element.19), channel_id=1, source_target_pairs={{0,16},{16,0},{1,17},{17,1},{2,18},{18,2},{3,19},{19,3},{4,20},{20... | collective-permute-start | bytes 147464 | tf_op jit(solution)/shard_map/ppermute | solution.py:178
  65.8 2.1 %collective-permute-done.2.refs_1_ = bf16[192,128]{1,0:T(8,128)(2,1)S(1)} collective-permute-done((bf16[192,128]{1,0:T(8,128)(2,1)S(1)}, bf16[192,128]{1,0:T(8,128)(2,1)S(1)}, u32[]{:S(2)}, u32[]{:S(2)}) %collective-permute-start.2) | collective-permute-done | bytes 49184 | tf_op jit(solution)/shard_map/ppermute | solution.py:178
  67.9 0.0 all-to-all-done.2.refs_0_
  67.9 0.1 shard_map.34
  67.9 7.8 %collective-permute-start.3 = (bf16[48,1536]{1,0:T(8,128)(2,1)S(1)}, bf16[48,1536]{1,0:T(8,128)(2,1)S(1)}, u32[]{:S(2)}, u32[]{:S(2)}) collective-permute-start(bf16[48,1536]{1,0:T(8,128)(2,1)S(1)} %get-tuple-element.21.refs_2_), channel_id=1, source_target_pairs={{0,16},{16,0},{1,17},{17,1},{2,18},{18,2},{3,19},{19,3},{4,20},{20... | collective-permute-start | bytes 442376 | tf_op jit(solution)/shard_map/ppermute | solution.py:178
  75.8 12.3 %all_to_all.30.refs_2_.refs_0_ = f32[32,1,128]{2,1,0:T(1,128)S(1)} all-to-all(f32[32,1,128]{2,1,0:T(1,128)S(1)} %shard_map.35), channel_id=1, replica_groups=mesh['zh'=2,'xc'=8,'zf'=2,'z2'=2,'z1'=2,'y'=4] {'xc','z2','z1'}, dimensions={0} | all-to-all | bytes 32768 | tf_op jit(solution)/shard_map/all_to_all | solution.py:243
  88.1 0.0 collective-permute-done.3.refs_1_
  88.1 0.9 shard_map.36.refs_1_
  89.0 3.5 %all-to-all-start.4 = ((bf16[4,48,1536]{2,1,0:T(8,128)(2,1)}), bf16[4,48,1536]{2,1,0:T(8,128)(2,1)S(1)}, u32[]{:S(2)}, u32[]{:S(2)}) async-start(bf16[4,48,1536]{2,1,0:T(8,128)(2,1)} %shard_map.36.refs_1_), calls=%async_computation.4 | async-start | bytes 1179648 | tf_op jit(solution)/shard_map/all_to_all | solution.py:251
  92.5 10.3 %collective-permute-start.4 = (f32[8,128]{1,0:T(8,128)S(1)}, f32[8,128]{1,0:T(8,128)S(1)}, u32[]{:S(2)}, u32[]{:S(2)}) collective-permute-start(f32[8,128]{1,0:T(8,128)S(1)} %shard_map.37.refs_3_), channel_id=1, source_target_pairs={{0,256},{256,0},{1,257},{257,1},{2,258},{258,2},{3,259},{259,3},{4... | collective-permute-start | bytes 12296 | tf_op jit(solution)/shard_map/ppermute | solution.py:178
  102.8 8.8 %collective-permute-done.4.refs_4_ = f32[8,128]{1,0:T(8,128)S(1)} collective-permute-done((f32[8,128]{1,0:T(8,128)S(1)}, f32[8,128]{1,0:T(8,128)S(1)}, u32[]{:S(2)}, u32[]{:S(2)}) %collective-permute-start.4) | collective-permute-done | bytes 4128 | tf_op jit(solution)/shard_map/ppermute | solution.py:178
  111.7 0.0 all-to-all-done.4
  111.7 0.7 shard_map.38
  112.3 8.8 %all_to_all.31.refs_0_ = bf16[4,208,128]{2,1,0:T(8,128)(2,1)S(1)} all-to-all(bf16[4,208,128]{2,1,0:T(8,128)(2,1)S(1)} %shard_map.38), channel_id=1, replica_groups=mesh['zh'=2,'xc'=8,'zf'=2,'z2'=2,'z1'=2,'y'=4] {'y'}, dimensions={0} | all-to-all | bytes 425984 | tf_op jit(solution)/shard_map/all_to_all | solution.py:260
  121.1 1.1 shard_map.39
  (4 shorter events, 0.1 us)
Async XLA Ops:
  0.0 0.9 copy-start.1
  2.0 4.6 %copy-start = (bf16[128,768]{1,0:T(8,128)(2,1)S(1)}, bf16[128,768]{1,0:T(8,128)(2,1)}, u32[]{:S(2)}) copy-start(bf16[128,768]{1,0:T(8,128)(2,1)} %refs_1_.1) | copy-start | bytes 589828
  2.0 16.9 %all-to-all-start.1 = ((bf16[4,128,768]{2,1,0:T(8,128)(2,1)}), bf16[4,128,768]{2,1,0:T(8,128)(2,1)S(1)}, u32[]{:S(2)}, u32[]{:S(2)}) async-start(bf16[4,128,768]{2,1,0:T(8,128)(2,1)} %shard_map.29), calls=%async_computation.1 | async-start | bytes 1572864 | tf_op jit(solution)/shard_map/all_to_all | solution.py:184
  18.9 14.8 %all-to-all-start = ((bf16[4,128,768]{2,1,0:T(8,128)(2,1)}), bf16[4,128,768]{2,1,0:T(8,128)(2,1)S(1)}, u32[]{:S(2)}, u32[]{:S(2)}) async-start(bf16[4,128,768]{2,1,0:T(8,128)(2,1)} %shard_map.28), calls=%async_computation | async-start | bytes 1572864 | tf_op jit(solution)/shard_map/all_to_all | solution.py:184
  22.9 12.2 %collective-permute-start = (bf16[384,128]{1,0:T(8,128)(2,1)S(1)}, bf16[384,128]{1,0:T(8,128)(2,1)S(1)}, u32[]{:S(2)}, u32[]{:S(2)}) collective-permute-start(bf16[384,128]{1,0:T(8,128)(2,1)S(1)} %get-tuple-element.15), channel_id=1, source_target_pairs={{0,4},{4,0},{1,5},{5,1},{2,6},{6,2},{3,7},{7,3},{8,12},{12,8},{9,1... | collective-permute-start | bytes 294920 | tf_op jit(solution)/shard_map/ppermute | solution.py:178
  35.2 32.7 %all-to-all-start.2 = ((bf16[4,48,1536]{2,1,0:T(8,128)(2,1)}), bf16[4,48,1536]{2,1,0:T(8,128)(2,1)S(1)}, u32[]{:S(2)}, u32[]{:S(2)}) async-start(bf16[4,48,1536]{2,1,0:T(8,128)(2,1)} %shard_map.30), calls=%async_computation.2 | async-start | bytes 1179648 | tf_op jit(solution)/shard_map/all_to_all | solution.py:230
  41.1 15.6 %collective-permute-start.1 = (bf16[192,128]{1,0:T(8,128)(2,1)S(1)}, bf16[192,128]{1,0:T(8,128)(2,1)S(1)}, u32[]{:S(2)}, u32[]{:S(2)}) collective-permute-start(bf16[192,128]{1,0:T(8,128)(2,1)S(1)} %get-tuple-element.16), channel_id=1, source_target_pairs={{0,8},{8,0},{1,9},{9,1},{2,10},{10,2},{3,11},{11,3},{4,12},{12,4},... | collective-permute-start | bytes 147464 | tf_op jit(solution)/shard_map/ppermute | solution.py:178
  56.7 11.2 %collective-permute-start.2 = (bf16[192,128]{1,0:T(8,128)(2,1)S(1)}, bf16[192,128]{1,0:T(8,128)(2,1)S(1)}, u32[]{:S(2)}, u32[]{:S(2)}) collective-permute-start(bf16[192,128]{1,0:T(8,128)(2,1)S(1)} %get-tuple-element.19), channel_id=1, source_target_pairs={{0,16},{16,0},{1,17},{17,1},{2,18},{18,2},{3,19},{19,3},{4,20},{20... | collective-permute-start | bytes 147464 | tf_op jit(solution)/shard_map/ppermute | solution.py:178
  67.9 20.1 %collective-permute-start.3 = (bf16[48,1536]{1,0:T(8,128)(2,1)S(1)}, bf16[48,1536]{1,0:T(8,128)(2,1)S(1)}, u32[]{:S(2)}, u32[]{:S(2)}) collective-permute-start(bf16[48,1536]{1,0:T(8,128)(2,1)S(1)} %get-tuple-element.21.refs_2_), channel_id=1, source_target_pairs={{0,16},{16,0},{1,17},{17,1},{2,18},{18,2},{3,19},{19,3},{4,20},{20... | collective-permute-start | bytes 442376 | tf_op jit(solution)/shard_map/ppermute | solution.py:178
  89.0 22.7 %all-to-all-start.4 = ((bf16[4,48,1536]{2,1,0:T(8,128)(2,1)}), bf16[4,48,1536]{2,1,0:T(8,128)(2,1)S(1)}, u32[]{:S(2)}, u32[]{:S(2)}) async-start(bf16[4,48,1536]{2,1,0:T(8,128)(2,1)} %shard_map.36.refs_1_), calls=%async_computation.4 | async-start | bytes 1179648 | tf_op jit(solution)/shard_map/all_to_all | solution.py:251
  92.5 19.2 %collective-permute-start.4 = (f32[8,128]{1,0:T(8,128)S(1)}, f32[8,128]{1,0:T(8,128)S(1)}, u32[]{:S(2)}, u32[]{:S(2)}) collective-permute-start(f32[8,128]{1,0:T(8,128)S(1)} %shard_map.37.refs_3_), channel_id=1, source_target_pairs={{0,256},{256,0},{1,257},{257,1},{2,258},{258,2},{3,259},{259,3},{4... | collective-permute-start | bytes 12296 | tf_op jit(solution)/shard_map/ppermute | solution.py:178
